TPU v7x, 256 devices: a whole 4x4x8 slice. The times are simulated.
256 devices in a mesh: seq: 32 (over x, z), head: 8 (over y, core).
Axes of the slice: x: 4, y: 4, z: 8, core: 2. Of those that a mesh axis runs over, the one named last changes fastest.
Arguments:
- queries: bfloat16 [16384, 4096], P('seq', 'head'), may hold values from -8 to 8
- key_rows: bfloat16 [16384, 512], P('seq'), may hold values from -8 to 8
- value_rows: bfloat16 [16384, 512], P('seq'), may hold values from -6 to 6
- doc_lengths: int32 [128], replicated, may hold values from 1 to 256, 16384 in all
- residual_in: bfloat16 [16384, 2048], P(('seq', 'head')), may hold values from -6 to 6
- out_weight: bfloat16 [4096, 2048], P('head'), may hold values from -0.09375 to 0.09375
- norm_gain: float32 [2048], replicated, may hold values from 0.5 to 1.5
- expert_ids: int32 [16384, 8], P(('seq', 'head')), may hold values from 0 to 127, all different within a row; in each aligned block of 64 rows (0 to 63, 64 to 127, ...) at most 5 rows name the same one
- gate_weights: float32 [16384, 8], P(('seq', 'head')), may hold values from 0.05 to 0.3
- w_gate: bfloat16 [256, 2048, 384], P(('seq', 'head')), may hold values from -0.125 to 0.125
- w_up: bfloat16 [256, 2048, 384], P(('seq', 'head')), may hold values from -0.125 to 0.125
- w_down: bfloat16 [256, 384, 2048], P(('seq', 'head')), may hold values from -0.21875 to 0.21875
Outputs:
- layer_out: bfloat16 [16384, 2048], P(('seq', 'head'))
Inputs may be any that keep to these rules, and one draw needn't show every extreme that they name: `doc_lengths`: the lengths sum to 16384 and the longest is exactly 256. `expert_ids`: a token names 8 different experts; among the 64 tokens of one device, in aligned blocks in order, no expert is named by more than 5 of them, a bound that some block reaches.
All inputs are finite; a program needn't handle non-finite values.
Results may differ from a plain program's by a relative error of at most 0.011.
Values may be sent and summed in bfloat16 or wider, within the bound.
No kernel may reach another device: no remote copies, remote signals or barrier semaphores. Data moves between devices by JAX's collectives and lax.ppermute only.
A program may use at most 128 MiB of HBM per device.

v0:
```python
import math

import jax
import jax.numpy as jnp
from jax import lax
from jax.sharding import PartitionSpec as P

HQ = 32
KVH = 4
HD = 128


masked_low = -1e30


def from_behind(value, axis, by):
    devices = lax.axis_size(axis)
    pairs = [(i, i + by) for i in range(devices) if 0 <= i + by < devices]
    return lax.ppermute(value, axis, pairs)


def doc_of(positions, doc_lengths):
    doc_ends = jnp.cumsum(doc_lengths)
    return jnp.sum((positions[:, None] >= doc_ends[None, :]).astype(jnp.int32), axis=1)


def expert_rows(row_block_slice, w_gate, w_up, w_down):
    gate_act = jnp.dot(row_block_slice, w_gate[0], preferred_element_type=jnp.float32)
    up_act = jnp.dot(row_block_slice, w_up[0], preferred_element_type=jnp.float32)
    hidden = (jax.nn.silu(gate_act) * up_act).astype(jnp.bfloat16)
    return jnp.dot(hidden, w_down[0], preferred_element_type=jnp.float32).astype(jnp.bfloat16)


def local(
    queries,
    key_rows,
    value_rows,
    doc_lengths,
    residual_in,
    out_weight,
    norm_gain,
    expert_ids,
    gate_weights,
    w_gate,
    w_up,
    w_down,
):
    tok_rows = queries.shape[0]
    half_rows = tok_rows // 2
    head_dim = HD
    heads_here = queries.shape[1] // head_dim
    group_size = HQ // KVH
    seq_index = lax.axis_index("seq")
    group_index = lax.axis_index("head") * heads_here // group_size
    query_block_list = queries.reshape(2, half_rows, heads_here, head_dim)
    query_pos = seq_index * tok_rows + jnp.arange(tok_rows, dtype=jnp.int32)
    query_doc = doc_of(query_pos, doc_lengths).reshape(2, half_rows)
    query_pos = query_pos.reshape(2, half_rows)
    key_head = lax.dynamic_slice_in_dim(key_rows, group_index * head_dim, head_dim, 1)
    value_head = lax.dynamic_slice_in_dim(value_rows, group_index * head_dim, head_dim, 1)
    own_pair = jnp.stack([key_head, value_head])
    previous_tail = from_behind(own_pair[:, half_rows:], "seq", 1)
    joined = jnp.concatenate([previous_tail, own_pair], axis=1)
    key_window_slices = jnp.stack([joined[:, :tok_rows], joined[:, half_rows:]], axis=1)
    key_pos = (
        seq_index * tok_rows
        - half_rows
        + jnp.arange(2, dtype=jnp.int32)[:, None] * half_rows
        + jnp.arange(tok_rows, dtype=jnp.int32)[None, :]
    )
    key_doc = doc_of(key_pos.reshape(-1), doc_lengths).reshape(2, tok_rows)
    score_scale = 1.0 / math.sqrt(head_dim)
    scores = (
        jnp.einsum(
            "fiza,fla->fzil",
            query_block_list,
            key_window_slices[0],
            preferred_element_type=jnp.float32,
        )
        * score_scale
    )
    visible = (
        (key_pos[:, None, :] <= query_pos[:, :, None])
        & (key_doc[:, None, :] == query_doc[:, :, None])
        & (key_pos[:, None, :] >= 0)
    )
    visible = visible[:, None]
    row_top = jnp.max(jnp.where(visible, scores, masked_low), axis=3, keepdims=True)
    weights = jnp.exp(jnp.where(visible, scores - row_top, masked_low))
    totals = jnp.sum(weights, axis=3)
    mixture = jnp.einsum(
        "zvoe,zey->zvoy",
        weights.astype(jnp.bfloat16),
        key_window_slices[1],
        preferred_element_type=jnp.float32,
    )
    attention_result = (mixture / totals[:, :, :, None]).astype(jnp.bfloat16)
    attn_rows = attention_result.transpose(0, 2, 1, 3).reshape(tok_rows, heads_here * head_dim)
    projected = lax.psum_scatter(
        jnp.dot(attn_rows, out_weight, preferred_element_type=jnp.float32).astype(jnp.bfloat16),
        "head",
        scatter_dimension=0,
        tiled=True,
    ).astype(jnp.float32)
    mid = residual_in.astype(jnp.float32) + projected
    spread = jnp.mean(mid * mid, axis=1, keepdims=True)
    normed = (mid * lax.rsqrt(spread + 1e-06) * norm_gain[None, :]).astype(jnp.bfloat16)
    seq_devices = lax.axis_size("seq")
    head_devices = lax.axis_size("head")
    expert_count = seq_devices * head_devices // 2
    row_count, top_count = expert_ids.shape
    capacity = max(2, (9 * row_count * top_count + 8 * expert_count - 1) // (8 * expert_count))
    width = normed.shape[1]
    flat_ids = expert_ids.reshape(-1)
    one_hot = (flat_ids[:, None] == jnp.arange(expert_count, dtype=jnp.int32)[None, :]).astype(
        jnp.int32
    )
    earlier = jnp.cumsum(one_hot, axis=0) - one_hot
    slot_index = jnp.sum(earlier * one_hot, axis=1)
    target = flat_ids * capacity + slot_index
    owner = (
        jnp.zeros((expert_count * capacity,), jnp.int32)
        .at[target]
        .set(jnp.arange(row_count * top_count, dtype=jnp.int32))
    )
    filled = jnp.zeros((expert_count * capacity,), jnp.int32).at[target].set(1)
    picked = jnp.where(filled[:, None] > 0, normed[owner // top_count], jnp.zeros((), jnp.bfloat16))
    outgoing = picked.reshape(seq_devices, head_devices // 2, 1, capacity, width)
    outgoing = jnp.broadcast_to(
        outgoing, (seq_devices, head_devices // 2, 2, capacity, width)
    ).reshape(seq_devices, head_devices, capacity, width)
    arrived = lax.all_to_all(
        lax.all_to_all(outgoing, "seq", split_axis=0, concat_axis=0, tiled=True),
        "head",
        split_axis=1,
        concat_axis=1,
        tiled=True,
    )
    part = expert_rows(arrived.reshape(-1, width), w_gate, w_up, w_down).reshape(arrived.shape)
    returned = lax.all_to_all(
        lax.all_to_all(part, "seq", split_axis=0, concat_axis=0, tiled=True),
        "head",
        split_axis=1,
        concat_axis=1,
        tiled=True,
    )
    halves = returned.reshape(expert_count, 2, capacity, width)
    first_half = halves[:, 0].reshape(-1, width)[target].astype(jnp.float32)
    second_half = halves[:, 1].reshape(-1, width)[target].astype(jnp.float32)
    combined = lax.optimization_barrier((first_half + second_half).astype(jnp.bfloat16)).astype(
        jnp.float32
    )
    combined = combined.reshape(row_count, top_count, width)
    expert_sum = jnp.sum(combined * gate_weights[:, :, None], axis=1)
    return (mid + expert_sum).astype(jnp.bfloat16)


def solution(mesh):
    placed = (
        P("seq", "head"),
        P("seq", None),
        P("seq", None),
        P(),
        P(("seq", "head"), None),
        P("head", None),
        P(),
        P(("seq", "head"), None),
        P(("seq", "head"), None),
        P(("seq", "head"), None, None),
        P(("seq", "head"), None, None),
        P(("seq", "head"), None, None),
    )
    return jax.shard_map(
        local, mesh=mesh, in_specs=placed, out_specs=P(("seq", "head"), None), check_vma=False
    )
```

profile of v0, /device:TPU:2, one launch (start us, length us, event | category | flops | bytes accessed | tf_op | source)
XLA Modules:
  0.0 608.1 jit_solution(7116511428840959242)
XLA Ops:
  19.0 4.4 fusion.68
  35.9 29.5 %reduce-scatter.2.cloned.1.call-done = bf16[64,2048]{1,0:T(8,128)(2,1)} async-done(((bf16[512,2048]{1,0:T(8,128)(2,1)}), bf16[64,2048]{1,0:T(8,128)(2,1)}) %reduce-scatter.2.cloned.1.call-update) | async-done | bytes 262160 | tf_op jit(solution)/shard_map/reduce_scatter | solution.py:99
  79.5 5.0 broadcast_in_dim.67
  84.5 8.7 %reshape.199 = bf16[32,8,5,2048]{3,1,2,0:T(8,128)(2,1)} reshape(bf16[32,4,2,5,2048]{4,2,1,3,0:T(2,128)(2,1)} %broadcast_in_dim.67) | data formatting | bytes 10485760 | tf_op jit(solution)/shard_map/reshape | solution.py:131
  93.2 123.5 %all_to_all.20 = bf16[32,8,5,2048]{3,1,2,0:T(8,128)(2,1)S(1)} all-to-all(bf16[32,8,5,2048]{3,1,2,0:T(8,128)(2,1)} %reshape.199), channel_id=1, replica_groups=mesh['seq'=32,'head'=8] {'seq'}, dimensions={0} | all-to-all | bytes 10485760 | tf_op jit(solution)/shard_map/all_to_all | solution.py:133
  219.5 65.9 %all_to_all.21 = bf16[32,8,5,2048]{3,0,2,1:T(8,128)(2,1)S(1)} all-to-all(bf16[32,8,5,2048]{3,0,2,1:T(8,128)(2,1)S(1)} %copy.79), channel_id=1, replica_groups=mesh['seq'=32,'head'=8] {'head'}, dimensions={1} | all-to-all | bytes 10485760 | tf_op jit(solution)/shard_map/all_to_all | solution.py:132
  285.5 6.4 %copy.80 = bf16[32,8,5,2048]{3,2,1,0:T(8,128)(2,1)} copy(bf16[32,8,5,2048]{3,0,2,1:T(8,128)(2,1)S(1)} %all_to_all.21) | data formatting | bytes 10485760 | tf_op jit(solution)/shard_map/all_to_all | solution.py:132
  291.8 10.1 %reshape.200 = bf16[1280,2048]{1,0:T(8,128)(2,1)} reshape(bf16[32,8,5,2048]{3,2,1,0:T(8,128)(2,1)} %copy.80) | data formatting | bytes 10485760 | tf_op jit(solution)/shard_map/reshape | solution.py:139
  302.0 6.6 %fusion.14 = f32[1280,384]{1,0:T(8,128)} fusion(bf16[1280,2048]{1,0:T(8,128)(2,1)} %reshape.200, bf16[1,2048,384]{2,1,0:T(8,128)(2,1)S(1)} %copy-done.7), kind=kOutput, calls=%fused_computation.27 | convolution fusion | flops 2013265920 | bytes 8781824 | tf_op jit(solution)/shard_map/dot_general | solution.py:28
  308.6 10.3 %convolution_convert_fusion = bf16[1280,2048]{1,0:T(8,128)(2,1)} fusion(bf16[1,384,2048]{2,1,0:T(8,128)(2,1)} %param.23, bf16[1280,2048]{1,0:T(8,128)(2,1)} %reshape.200, f32[1280,384]{1,0:T(8,128)} %fusion.14, bf16[1,2048,384]{2,1,0:T(8,128)(2,1)} %param.22), kind=kOutput, calls=%fused_computation.6 | convolution fusion | flops 4032102400 | bytes 15597568 | tf_op jit(solution)/shard_map/dot_general | solution.py:31
  318.9 9.9 %reshape.201 = bf16[32,8,5,2048]{3,2,1,0:T(8,128)(2,1)} reshape(bf16[1280,2048]{1,0:T(8,128)(2,1)} %convolution_convert_fusion) | data formatting | bytes 10485760 | tf_op jit(solution)/shard_map/reshape | solution.py:139
  328.8 8.8 %copy.81 = bf16[32,8,5,2048]{3,1,2,0:T(8,128)(2,1)S(1)} copy(bf16[32,8,5,2048]{3,2,1,0:T(8,128)(2,1)} %reshape.201) | data formatting | bytes 10485760 | tf_op jit(solution)/shard_map/reshape | solution.py:139
  337.6 124.2 %all_to_all.22 = bf16[32,8,5,2048]{3,1,2,0:T(8,128)(2,1)S(1)} all-to-all(bf16[32,8,5,2048]{3,1,2,0:T(8,128)(2,1)S(1)} %copy.81), channel_id=1, replica_groups=mesh['seq'=32,'head'=8] {'seq'}, dimensions={0} | all-to-all | bytes 10485760 | tf_op jit(solution)/shard_map/all_to_all | solution.py:141
  461.9 5.2 copy.82
  467.1 5.0 all-to-all-start.3
  472.2 60.8 %all-to-all-done.3 = bf16[32,8,5,2048]{3,0,2,1:T(8,128)(2,1)} async-done(((bf16[32,8,5,2048]{3,0,2,1:T(8,128)(2,1)}), bf16[32,8,5,2048]{3,0,2,1:T(8,128)(2,1)}, u32[]{:S(2)}, u32[]{:S(2)}) %all-to-all-start.3) | async-done | bytes 5242912 | tf_op jit(solution)/shard_map/all_to_all | solution.py:140
  533.0 7.9 %copy.83 = bf16[32,8,5,2048]{3,1,0,2:T(8,128)(2,1)} copy(bf16[32,8,5,2048]{3,0,2,1:T(8,128)(2,1)} %all-to-all-done.3) | data formatting | bytes 10485760 | tf_op jit(solution)/shard_map/all_to_all | solution.py:140
  540.9 9.3 %reshape.202 = bf16[128,2,5,2048]{3,1,0,2:T(2,128)(2,1)} reshape(bf16[32,8,5,2048]{3,1,0,2:T(8,128)(2,1)} %copy.83) | data formatting | bytes 10485760 | tf_op jit(solution)/shard_map/reshape | solution.py:147
  550.2 11.9 %fusion.67 = (bf16[128,1,5,2048]{3,1,0,2:T(2,128)(2,1)S(1)}, bf16[128,1,5,2048]{3,1,0,2:T(2,128)(2,1)}) fusion(bf16[128,2,5,2048]{3,1,0,2:T(2,128)(2,1)} %reshape.202), kind=kLoop, calls=%fused_computation.100 | loop fusion | bytes 10485760 | tf_op jit(solution)/shard_map/slice | solution.py:148
  562.1 4.9 copy.84
  566.9 4.2 reshape_squeeze.6
  571.1 7.3 %copy.85 = bf16[128,1,5,2048]{3,2,0,1:T(8,128)(2,1)} copy(bf16[128,1,5,2048]{3,1,0,2:T(2,128)(2,1)} %get-tuple-element.6) | data formatting | bytes 5242880 | tf_op jit(solution)/shard_map/slice | solution.py:149
  578.5 5.6 reshape_squeeze.7
  587.6 7.3 %gather_fusion.2 = bf16[512,2048]{1,0:T(8,128)(2,1)} fusion(bf16[640,2048]{1,0:T(8,128)(2,1)} %reshape_squeeze.7, s32[1024]{0:T(1024)S(1)} %pad_clamp_fusion), kind=kCustom, calls=%fused_computation.2 | custom fusion | bytes 4196352 | tf_op jit(solution)/shard_map/gather | solution.py:149
  (79 shorter events, 51.1 us)
Async XLA Ops:
  6.5 19.8 %copy-start = (bf16[512,2048]{1,0:T(8,128)(2,1)S(1)}, bf16[512,2048]{1,0:T(8,128)(2,1)}, u32[]{:S(2)}) copy-start(bf16[512,2048]{1,0:T(8,128)(2,1)} %param.17) | copy-start | bytes 6291460
  6.5 58.9 %reduce-scatter.2.cloned.1.call-start = ((), (), s32[]{:S(2)}) async-start(), calls=%async_computation.5 | async-start | bytes 2359296 | tf_op jit(solution)/shard_map/reduce_scatter | solution.py:99
  7.7 11.2 %collective-permute-start = (bf16[2,256,128]{2,1,0:T(8,128)(2,1)S(1)}, bf16[2,256,128]{2,1,0:T(8,128)(2,1)S(1)}, u32[]{:S(2)}, u32[]{:S(2)}) collective-permute-start(bf16[2,256,128]{2,1,0:T(8,128)(2,1)S(1)} %fusion.49), channel_id=1, source_target_pairs={{0,8},{8,16},{16,24},{24,32},{32,40},{40,48},{48,56},{56,64},{64,7... | collective-permute-start | bytes 393224 | tf_op jit(solution)/shard_map/ppermute | solution.py:19
  26.4 2.7 copy-start.4
  29.0 36.4 %copy-start.2 = (bf16[64,2048]{1,0:T(8,128)(2,1)S(1)}, bf16[64,2048]{1,0:T(8,128)(2,1)}, u32[]{:S(2)}) copy-start(bf16[64,2048]{1,0:T(8,128)(2,1)} %param.16) | copy-start | bytes 786436
  29.0 37.6 %copy-start.5 = (f32[2048]{0:T(1024)S(1)}, f32[2048]{0:T(1024)}, u32[]{:S(2)}) copy-start(f32[2048]{0:T(1024)} %param.18) | copy-start | bytes 24580
  291.8 10.1 %copy-start.7 = (bf16[1,2048,384]{2,1,0:T(8,128)(2,1)S(1)}, bf16[1,2048,384]{2,1,0:T(8,128)(2,1)}, u32[]{:S(2)}) copy-start(bf16[1,2048,384]{2,1,0:T(8,128)(2,1)} %param.21) | copy-start | bytes 4718596
  467.1 5.0 copy-start.6
  467.1 65.9 %all-to-all-start.3 = ((bf16[32,8,5,2048]{3,0,2,1:T(8,128)(2,1)}), bf16[32,8,5,2048]{3,0,2,1:T(8,128)(2,1)}, u32[]{:S(2)}, u32[]{:S(2)}) async-start(bf16[32,8,5,2048]{3,0,2,1:T(8,128)(2,1)} %copy.82), calls=%async_computation.4 | async-start | bytes 10485760 | tf_op jit(solution)/shard_map/all_to_all | solution.py:140
  594.9 5.8 copy-start.1
  598.1 1.8 copy-start.3
Sparse Core Ops, SparseCore 0:
  29.1 36.2 reduce-scatter.1
where the time goes:
time: 619 us; the launch traced here: 608 us
  blocking collectives  314 us (51%)
  local copies, waits for them, and re-layouts  138 us (22%)
  waiting for transfers between devices  93.4 us (15%)
  matrix products  26.5 us (4%)
  between operations  14.2 us (2%)
  other arithmetic  13.5 us (2%)
  starting transfers between devices  8.85 us (1%)
    all_to_all x1, blocking collectives, local(): lax.all_to_all(part, 'seq', split_axis=0, concat_axis=0, tiled=True)  124 us
    all_to_all x1, blocking collectives, local(): lax.all_to_all(outgoing, 'seq', split_axis=0, concat_axis=0, tiled=True)  123 us
    all_to_all x1, blocking collectives, local(): lax.all_to_all(lax.all_to_all(outgoing, 'seq', split_axis=0, concat_axis=...  65.9 us
    all_to_all x1, waiting for transfers between devices, local(): lax.all_to_all(lax.all_to_all(part, 'seq', split_axis=0, concat_axis=0, t...  60.8 us
    reduce_scatter x1, waiting for transfers between devices, local(): lax.psum_scatter(jnp.dot(attn_rows, out_weight, preferred_element_type=jn...  29.5 us
    reshape x2, local copies, waits for them, and re-layouts, local(): expert_rows(arrived.reshape(-1, width), w_gate, w_up, w_down)  18.7 us
    slice x2, local copies, waits for them, and re-layouts, local(): first_half = halves[:, 0].reshape(-1, width)[target].astype(jnp.float32)  16.7 us
  transfers between devices with their start and end apart: 3, of which 3 were waited for; matrix products, arithmetic and copies ran while one was open for 2% of the time, Pallas kernels for 0%

commit v1 on v0

v1 whole, which is shorter than its diff:
```python
import math

import jax
import jax.numpy as jnp
from jax import lax
from jax.sharding import Mesh, PartitionSpec as P

HQ = 32
KVH = 4
HD = 128
NX, NZ, NY, NC = 4, 8, 4, 2
ROWS = 64
CAP = 5
PLANE = NX * NY
SLOTS = NZ * CAP

BF = jnp.bfloat16
F32 = jnp.float32
masked_low = -1e30

RING = (0, -1, 1, -2, 2, -3, 3, 4)


def shift(value, axis, size, by):
    return lax.ppermute(value, axis, [(i, (i + by) % size) for i in range(size)])


def swap_cores(value):
    return lax.ppermute(value, "c", [(0, 1), (1, 0)])


def from_behind(value):
    devices = NX * NZ
    return lax.ppermute(value, ("x", "z"), [(i, i + 1) for i in range(devices - 1)])


def doc_of(positions, doc_lengths):
    doc_ends = jnp.cumsum(doc_lengths)
    return jnp.sum((positions[:, None] >= doc_ends[None, :]).astype(jnp.int32), axis=1)


def attend(queries, key_rows, value_rows, doc_lengths):
    tok_rows = queries.shape[0]
    half_rows = tok_rows // 2
    heads_here = queries.shape[1] // HD
    seq_index = lax.axis_index(("x", "z"))
    group_index = lax.axis_index("y")
    query_block_list = queries.reshape(2, half_rows, heads_here, HD)
    query_pos = seq_index * tok_rows + jnp.arange(tok_rows, dtype=jnp.int32)
    query_doc = doc_of(query_pos, doc_lengths).reshape(2, half_rows)
    query_pos = query_pos.reshape(2, half_rows)
    key_head = lax.dynamic_slice_in_dim(key_rows, group_index * HD, HD, 1)
    value_head = lax.dynamic_slice_in_dim(value_rows, group_index * HD, HD, 1)
    own_pair = jnp.stack([key_head, value_head])
    previous_tail = from_behind(own_pair[:, half_rows:])
    joined = jnp.concatenate([previous_tail, own_pair], axis=1)
    windows = jnp.stack([joined[:, :tok_rows], joined[:, half_rows:]], axis=1)
    key_pos = (
        seq_index * tok_rows
        - half_rows
        + jnp.arange(2, dtype=jnp.int32)[:, None] * half_rows
        + jnp.arange(tok_rows, dtype=jnp.int32)[None, :]
    )
    key_doc = doc_of(key_pos.reshape(-1), doc_lengths).reshape(2, tok_rows)
    scores = jnp.einsum(
        "fiza,fla->fzil", query_block_list, windows[0], preferred_element_type=F32
    ) * (1.0 / math.sqrt(HD))
    visible = (
        (key_pos[:, None, :] <= query_pos[:, :, None])
        & (key_doc[:, None, :] == query_doc[:, :, None])
        & (key_pos[:, None, :] >= 0)
    )
    visible = visible[:, None]
    row_top = jnp.max(jnp.where(visible, scores, masked_low), axis=3, keepdims=True)
    weights = jnp.exp(jnp.where(visible, scores - row_top, masked_low))
    totals = jnp.sum(weights, axis=3)
    mixture = jnp.einsum(
        "zvoe,zey->zvoy", weights.astype(BF), windows[1], preferred_element_type=F32
    )
    result = (mixture / totals[:, :, :, None]).astype(BF)
    return result.transpose(0, 2, 1, 3).reshape(tok_rows, heads_here * HD)


def project(attn_rows, out_weight):
    width = out_weight.shape[1]
    y, c = lax.axis_index("y"), lax.axis_index("c")
    blocks = attn_rows.reshape(NY, NC, ROWS, -1)

    def rows_for(core):
        picked = [
            lax.dynamic_slice(blocks, ((y + k) % NY, core, 0, 0), (1, 1, ROWS, blocks.shape[3]))
            for k in range(NY)
        ]
        return jnp.concatenate(picked, axis=0).reshape(NY * ROWS, -1)

    theirs = jnp.dot(rows_for(1 - c), out_weight, preferred_element_type=F32).astype(BF)
    arrived = swap_cores(theirs)
    mine = jnp.dot(rows_for(c), out_weight, preferred_element_type=F32)
    both = (mine + arrived.astype(F32)).reshape(NY, ROWS, width)
    total = both[0]
    for k in range(1, NY):
        total = total + shift(both[k].astype(BF), "y", NY, k).astype(F32)
    return total


def ring_gather(own):
    width = own.shape[1]
    half = width // 2
    right = left = own
    blocks = [own]
    for _ in range(3):
        right = shift(right, "z", NZ, 1)
        left = shift(left, "z", NZ, -1)
        blocks += [right, left]
    a = shift(right[:, :half], "z", NZ, 1)
    b = shift(left[:, half:], "z", NZ, -1)
    blocks.append(jnp.concatenate([a, b], axis=1))
    return jnp.concatenate(blocks, axis=0)


def ring_sum(blocks):
    half = blocks[0].shape[1] // 2

    def add(a, b):
        return (a.astype(F32) + b.astype(F32)).astype(BF)

    a = shift(blocks[4][:, :half], "z", NZ, 1)
    b = shift(blocks[4][:, half:], "z", NZ, -1)
    right = jnp.concatenate([add(blocks[3][:, :half], a), blocks[3][:, half:]], axis=1)
    left = jnp.concatenate([blocks[-3][:, :half], add(blocks[-3][:, half:], b)], axis=1)
    for step in (2, 1):
        right = add(shift(right, "z", NZ, 1), blocks[step])
        left = add(shift(left, "z", NZ, -1), blocks[-step])
    right = shift(right, "z", NZ, 1)
    left = shift(left, "z", NZ, -1)
    return blocks[0].astype(F32) + right.astype(F32) + left.astype(F32)


def slots_of(expert_ids, gate_weights):
    z = lax.axis_index("z")
    own = jnp.concatenate([expert_ids.astype(F32), gate_weights], axis=1)
    everywhere = lax.all_gather(own, "z", axis=0, tiled=False)
    order = (z + jnp.array(RING, jnp.int32)) % NZ
    everywhere = jnp.take(everywhere, order, axis=0)
    top = expert_ids.shape[1]
    ids = everywhere[:, :, :top].astype(jnp.int32)
    gates = everywhere[:, :, top:]
    place = jnp.arange(PLANE, dtype=jnp.int32)
    experts = (place // NY * NZ + z) * NY + place % NY
    match = ids[None] == experts[:, None, None, None]
    named = jnp.any(match, axis=3)
    gate = jnp.sum(jnp.where(match, gates[None], 0.0), axis=3)
    before = jnp.triu(jnp.ones((ROWS, ROWS), BF), 1)
    rank = jnp.dot(
        named.astype(BF).reshape(PLANE * NZ, ROWS), before, preferred_element_type=F32
    ).reshape(PLANE, NZ, ROWS)
    slot = rank.astype(jnp.int32) + jnp.arange(NZ, dtype=jnp.int32)[None, :, None] * CAP
    slot = jnp.where(named, slot, -1).reshape(PLANE, 1, NZ * ROWS)
    hit = slot == jnp.arange(SLOTS, dtype=jnp.int32)[None, :, None]
    one_hot = hit.astype(BF).reshape(PLANE * SLOTS, NZ * ROWS)
    weighted = jnp.where(hit, gate.reshape(PLANE, 1, NZ * ROWS), 0.0).astype(BF)
    return one_hot, weighted.reshape(PLANE * SLOTS, NZ * ROWS)


def expert_rows(rows, w_gate, w_up, w_down):
    gate_act = jnp.dot(rows, w_gate, preferred_element_type=F32)
    up_act = jnp.dot(rows, w_up, preferred_element_type=F32)
    hidden = (jax.nn.silu(gate_act) * up_act).astype(BF)
    return jnp.dot(hidden, w_down, preferred_element_type=F32).astype(BF)


def exchange(rows):
    width = rows.shape[1]
    out = lax.all_to_all(
        rows.reshape(PLANE, SLOTS, width), ("x", "y"), split_axis=0, concat_axis=0, tiled=True
    )
    return out.reshape(PLANE * SLOTS, width)


def local(
    queries,
    key_rows,
    value_rows,
    doc_lengths,
    residual_in,
    out_weight,
    norm_gain,
    expert_ids,
    gate_weights,
    w_gate,
    w_up,
    w_down,
):
    one_hot, weighted = slots_of(expert_ids, gate_weights)
    attn_rows = attend(queries, key_rows, value_rows, doc_lengths)
    mid = residual_in.astype(F32) + project(attn_rows, out_weight)
    spread = jnp.mean(mid * mid, axis=1, keepdims=True)
    normed = (mid * lax.rsqrt(spread + 1e-06) * norm_gain[None, :]).astype(BF)

    tokens = ring_gather(normed)
    outgoing = jnp.dot(one_hot, tokens, preferred_element_type=F32).astype(BF)
    mine = exchange(outgoing)
    theirs = swap_cores(mine)
    part_mine = expert_rows(mine, w_gate[0], w_up[0], w_down[0])
    part_theirs = expert_rows(theirs, w_gate[0], w_up[0], w_down[0])
    other_half = swap_cores(part_theirs)
    pair_out = (part_mine.astype(F32) + other_half.astype(F32)).astype(BF)
    returned = exchange(pair_out)
    plane_sum = lax.dot_general(
        weighted, returned, (((0,), (0,)), ((), ())), preferred_element_type=F32
    ).astype(BF)
    blocks = plane_sum.reshape(NZ, ROWS, -1)
    expert_sum = ring_sum({offset: blocks[i] for i, offset in enumerate(RING)})
    return (mid + expert_sum).astype(BF)


def solution(mesh):
    mesh = Mesh(mesh.devices.reshape(NX, NZ, NY, NC), ("x", "z", "y", "c"))
    seq, head = ("x", "z"), ("y", "c")
    every = seq + head
    placed = (
        P(seq, head),
        P(seq, None),
        P(seq, None),
        P(),
        P(every, None),
        P(head, None),
        P(),
        P(every, None),
        P(every, None),
        P(every, None, None),
        P(every, None, None),
        P(every, None, None),
    )
    return jax.shard_map(
        local, mesh=mesh, in_specs=placed, out_specs=P(every, None), check_vma=False
    )
```

time: 619 us -> 238 us (0.38); the launches traced: 608 us -> 237 us
  blocking collectives: 314 us -> 52.6 us
  local copies, waits for them, and re-layouts: 138 us -> 12 us
  starting transfers between devices: 8.85 us -> 43.2 us
  between operations: 14.2 us -> 0.48 us
  matrix products: 26.5 us -> 39 us
  waiting for transfers between devices: 93.4 us -> 82.4 us
  other arithmetic: 13.5 us -> 6.9 us
    all_to_all x3 -> x1, blocking collectives: 314 us -> 28.1 us  [exchange(): lax.all_to_all(rows.reshape(PLANE, SLOTS, width), ('x', 'y'), split_axis=...]
    reshape x6 -> x1, local copies, waits for them, and re-layouts: 48 us -> 1.17 us  [attend(): query_block_list = queries.reshape(2, half_rows, heads_here, HD)]
    ppermute x1 -> x23, waiting for transfers between devices: 3.11 us -> 46.7 us  [the longest x19 38.3 us: shift(): lax.ppermute(value, axis, [(i, (i + by) % size) for i in range(size)])]
    ppermute x1 -> x23, starting transfers between devices: 3.83 us -> 36.5 us  [the longest x19 32.6 us: shift(): lax.ppermute(value, axis, [(i, (i + by) % size) for i in range(size)])]
    reduce_scatter x1 -> x0, waiting for transfers between devices: 29.5 us -> none  [local(): lax.psum_scatter(jnp.dot(attn_rows, out_weight, preferred_element_type=jn...]
    all_to_all x1, waiting for transfers between devices: 60.8 us -> 35.7 us  [exchange(): lax.all_to_all(rows.reshape(PLANE, SLOTS, width), ('x', 'y'), split_axis=...]
    all_gather x0 -> x1, blocking collectives: none -> 24.6 us  [slots_of(): everywhere = lax.all_gather(own, 'z', axis=0, tiled=False)]
    slice x3 -> x4, local copies, waits for them, and re-layouts: 24 us -> 0.12 us  [the longest x1 0.06 us: project(): total = total + shift(both[k].astype(BF), 'y', NY, k).astype(F32)]
  transfers between devices with their start and end apart: 3 -> 24, of which waited for: 3 -> 15; matrix products, arithmetic and copies ran while one was open for 2% -> 7% of each run, Pallas kernels for 0% -> 0%
where the time goes in v1:
time: 238 us; the launch traced here: 237 us
  waiting for transfers between devices  82.4 us (35%)
  blocking collectives  52.6 us (22%)
  starting transfers between devices  43.2 us (18%)
  matrix products  39 us (16%)
  local copies, waits for them, and re-layouts  12 us (5%)
  other arithmetic  6.9 us (3%)
    ppermute x19, waiting for transfers between devices, shift(): lax.ppermute(value, axis, [(i, (i + by) % size) for i in range(size)])  38.3 us
    all_to_all x1, waiting for transfers between devices, exchange(): lax.all_to_all(rows.reshape(PLANE, SLOTS, width), ('x', 'y'), split_axis=...  35.7 us
    ppermute x19, starting transfers between devices, shift(): lax.ppermute(value, axis, [(i, (i + by) % size) for i in range(size)])  32.6 us
    all_to_all x1, blocking collectives, exchange(): lax.all_to_all(rows.reshape(PLANE, SLOTS, width), ('x', 'y'), split_axis=...  28.1 us
    all_gather x1, blocking collectives, slots_of(): everywhere = lax.all_gather(own, 'z', axis=0, tiled=False)  24.6 us
    dot_general x2, matrix products, expert_rows(): return jnp.dot(hidden, w_down, preferred_element_type=F32).astype(BF)  15.6 us
    unnamed x27, local copies, waits for them, and re-layouts  7.3 us
    all_to_all x1, starting transfers between devices, exchange(): lax.all_to_all(rows.reshape(PLANE, SLOTS, width), ('x', 'y'), split_axis=...  6.64 us
  transfers between devices with their start and end apart: 24, of which 15 were waited for; matrix products, arithmetic and copies ran while one was open for 7% of the time, Pallas kernels for 0%

profile of v1, /device:TPU:2, one launch (start us, length us, event | category | flops | bytes accessed | tf_op | source)
XLA Modules:
  0.0 236.6 jit_solution(1109411318106042018)
XLA Ops:
  1.2 3.8 %collective-permute-start = (bf16[2,256,128]{2,1,0:T(8,128)(2,1)S(1)}, bf16[2,256,128]{2,1,0:T(8,128)(2,1)S(1)}, u32[]{:S(2)}, u32[]{:S(2)}) collective-permute-start(bf16[2,256,128]{2,1,0:T(8,128)(2,1)S(1)} %fusion.68), channel_id=1, source_target_pairs={{0,8},{8,16},{16,24},{24,32},{32,40},{40,48},{48,56},{56,64},{64,7... | collective-permute-start | bytes 393224 | tf_op jit(solution)/shard_map/ppermute | solution.py:34
  12.4 4.3 %fusion.99 = (f32[2,4,256]{2,1,0:T(4,128)S(1)}, bf16[2,4,256,512]{2,3,1,0:T(8,128)(2,1)}) fusion(pred[2,256,512]{1,2,0:T(8,128)(4,1)} %and_and_fusion, bf16[2,256,4,128]{3,2,1,0:T(4,128)(2,1)S(1)} %reshape.203, bf16[2,1,512,128]{3,2,1,0:T(8,128)(2,1)S(1)} %get-tuple-element.35, bf16[2,1,512,128]{3,2,1,0:T(8,128)(2,1)S(1)} %get-tuple-element.34), kind=kOutput, calls=%fused_computation.152 | convolution fusion | flops 545260032 | bytes 4726784 | tf_op jit(solution)/shard_map/sub | solution.py:75
  21.9 24.6 %all-gather.1 = f32[8,64,16]{1,2,0:T(8,128)S(1)} all-gather(f32[1,64,16]{1,2,0:T(8,128)S(1)} %maximum_bitcast_fusion), channel_id=2, replica_groups=mesh['x'=4,'z'=8,'y'=4,'c'=2] {'z'}, dimensions={0}, use_global_device_ids=true | all-gather | bytes 36864 | tf_op jit(solution)/shard_map/all_gather | solution.py:142
  56.0 3.8 %collective-permute-done.3 = bf16[64,2048]{1,0:T(8,128)(2,1)S(1)} collective-permute-done((bf16[64,2048]{1,0:T(8,128)(2,1)S(1)}, bf16[64,2048]{1,0:T(8,128)(2,1)S(1)}, u32[]{:S(2)}, u32[]{:S(2)}) %collective-permute-start.3) | collective-permute-done | bytes 262176 | tf_op jit(solution)/shard_map/ppermute | solution.py:25
  64.7 5.3 %collective-permute-done.5 = bf16[64,2048]{1,0:T(8,128)(2,1)S(1)} collective-permute-done((bf16[64,2048]{1,0:T(8,128)(2,1)S(1)}, bf16[64,2048]{1,0:T(8,128)(2,1)S(1)}, u32[]{:S(2)}, u32[]{:S(2)}) %collective-permute-start.5) | collective-permute-done | bytes 262176 | tf_op jit(solution)/shard_map/ppermute | solution.py:25
  70.0 3.2 %collective-permute-start.8 = (bf16[64,2048]{1,0:T(8,128)(2,1)S(1)}, bf16[64,2048]{1,0:T(8,128)(2,1)S(1)}, u32[]{:S(2)}, u32[]{:S(2)}) collective-permute-start(bf16[64,2048]{1,0:T(8,128)(2,1)S(1)} %collective-permute-done.6), channel_id=1, source_target_pairs={{0,56},{8,0},{16,8},{24,16},{32,24},{40,32},{48,40},{56,48},{1,57}... | collective-permute-start | bytes 786440 | tf_op jit(solution)/shard_map/ppermute | solution.py:25
  74.7 3.5 %collective-permute-done.7 = bf16[64,2048]{1,0:T(8,128)(2,1)S(1)} collective-permute-done((bf16[64,2048]{1,0:T(8,128)(2,1)S(1)}, bf16[64,2048]{1,0:T(8,128)(2,1)S(1)}, u32[]{:S(2)}, u32[]{:S(2)}) %collective-permute-start.7) | collective-permute-done | bytes 262176 | tf_op jit(solution)/shard_map/ppermute | solution.py:25
  78.2 3.2 %collective-permute-start.10 = (bf16[64,2048]{1,0:T(8,128)(2,1)S(1)}, bf16[64,2048]{1,0:T(8,128)(2,1)S(1)}, u32[]{:S(2)}, u32[]{:S(2)}) collective-permute-start(bf16[64,2048]{1,0:T(8,128)(2,1)S(1)} %collective-permute-done.8), channel_id=1, source_target_pairs={{0,56},{8,0},{16,8},{24,16},{32,24},{40,32},{48,40},{56,48},{1,57}... | collective-permute-start | bytes 786440 | tf_op jit(solution)/shard_map/ppermute | solution.py:25
  85.9 3.3 %collective-permute-start.12 = (bf16[64,1024]{1,0:T(8,128)(2,1)S(1)}, bf16[64,1024]{1,0:T(8,128)(2,1)S(1)}, u32[]{:S(2)}, u32[]{:S(2)}) collective-permute-start(bf16[64,1024]{1,0:T(8,128)(2,1)S(1)} %slice.129), channel_id=1, source_target_pairs={{0,56},{8,0},{16,8},{24,16},{32,24},{40,32},{48,40},{56,48},{1,57}... | collective-permute-start | bytes 393224 | tf_op jit(solution)/shard_map/ppermute | solution.py:25
  95.9 28.1 %all_to_all.10 = bf16[16,40,2048]{2,1,0:T(8,128)(2,1)S(1)} all-to-all(bf16[16,40,2048]{2,1,0:T(8,128)(2,1)S(1)} %bitcast.109), channel_id=1, replica_groups=mesh['x'=4,'z'=8,'y'=4,'c'=2] {'x','y'}, dimensions={0} | all-to-all | bytes 5242880 | tf_op jit(solution)/shard_map/all_to_all | solution.py:174
  125.5 4.9 %collective-permute-done.13 = bf16[640,2048]{1,0:T(8,128)(2,1)S(1)} collective-permute-done((bf16[640,2048]{1,0:T(8,128)(2,1)S(1)}, bf16[640,2048]{1,0:T(8,128)(2,1)S(1)}, u32[]{:S(2)}, u32[]{:S(2)}) %collective-permute-start.13) | collective-permute-done | bytes 2621472 | tf_op jit(solution)/shard_map/ppermute | solution.py:29
  134.4 7.4 %convolution_convert_fusion.1 = bf16[640,2048]{1,0:T(8,128)(2,1)} fusion(bf16[1,384,2048]{2,1,0:T(8,128)(2,1)} %param.24, f32[640,384]{1,0:T(8,128)} %fusion.12, bf16[640,2048]{1,0:T(8,128)(2,1)} %copy-done.8, bf16[1,2048,384]{2,1,0:T(8,128)(2,1)} %param.22), kind=kOutput, calls=%fused_computation.11 | convolution fusion | flops 2016051200 | bytes 9371648 | tf_op jit(solution)/shard_map/dot_general | solution.py:169
  142.0 4.7 %fusion.18 = f32[640,384]{1,0:T(8,128)} fusion(bf16[640,2048]{1,0:T(8,128)(2,1)} %bitcast.106, bf16[1,2048,384]{2,1,0:T(8,128)(2,1)} %param.22), kind=kOutput, calls=%fused_computation.28 | convolution fusion | flops 1006632960 | bytes 5177344 | tf_op jit(solution)/shard_map/dot_general | solution.py:166
  147.1 8.2 %add_convert_fusion = bf16[640,2048]{1,0:T(8,128)(2,1)} fusion(bf16[640,2048]{1,0:T(8,128)(2,1)} %collective-permute-done.14, bf16[1,384,2048]{2,1,0:T(8,128)(2,1)} %param.24, bf16[640,2048]{1,0:T(8,128)(2,1)} %bitcast.107, bf16[1,2048,384]{2,1,0:T(8,128)(2,1)} %param.23, f32[640,384]{1,0:T(8,128)} %fusion.18), kind=kOutput, calls=%fused_computation.2 | convolution fusion | flops 2021294080 | bytes 11993088 | tf_op jit(solution)/shard_map/dot_general | solution.py:169
  155.3 6.6 %all-to-all-start.1 = ((bf16[16,40,2048]{2,1,0:T(8,128)(2,1)}), bf16[16,40,2048]{2,1,0:T(8,128)(2,1)}, u32[]{:S(2)}, u32[]{:S(2)}) async-start(bf16[16,40,2048]{2,1,0:T(8,128)(2,1)} %bitcast.108), calls=%async_computation.1 | async-start | bytes 5242880 | tf_op jit(solution)/shard_map/all_to_all | solution.py:174
  162.3 35.7 %all-to-all-done.1 = bf16[16,40,2048]{2,1,0:T(8,128)(2,1)} async-done(((bf16[16,40,2048]{2,1,0:T(8,128)(2,1)}), bf16[16,40,2048]{2,1,0:T(8,128)(2,1)}, u32[]{:S(2)}, u32[]{:S(2)}) %all-to-all-start.1) | async-done | bytes 2621472 | tf_op jit(solution)/shard_map/all_to_all | solution.py:174
  198.0 3.6 %bitcast_convert_fusion = bf16[512,2048]{1,0:T(8,128)(2,1)S(1)} fusion(bf16[16,40,2048]{2,1,0:T(8,128)(2,1)} %all-to-all-done.1, bf16[16,512]{1,0:T(8,128)(2,1)S(1)} %broadcast_in_dim.92, s32[16,512]{1,0:T(8,128)S(1)} %eq.81), kind=kOutput, calls=%fused_computation.3 | convolution fusion | flops 1343881216 | bytes 4767744 | tf_op jit(solution)/shard_map/dot_general | solution.py:209
  201.7 3.2 %collective-permute-start.19 = (bf16[64,1024]{1,0:T(8,128)(2,1)S(1)}, bf16[64,1024]{1,0:T(8,128)(2,1)S(1)}, u32[]{:S(2)}, u32[]{:S(2)}) collective-permute-start(bf16[64,1024]{1,0:T(8,128)(2,1)S(1)} %get-tuple-element.20), channel_id=1, source_target_pairs={{0,56},{8,0},{16,8},{24,16},{32,24},{40,32},{48,40},{56,48},{1,57}... | collective-permute-start | bytes 393224 | tf_op jit(solution)/shard_map/ppermute | solution.py:25
  207.9 3.3 %collective-permute-start.20 = (bf16[64,2048]{1,0:T(8,128)(2,1)S(1)}, bf16[64,2048]{1,0:T(8,128)(2,1)S(1)}, u32[]{:S(2)}, u32[]{:S(2)}) collective-permute-start(bf16[64,2048]{1,0:T(8,128)(2,1)S(1)} %pad_maximum_fusion.7), channel_id=1, source_target_pairs={{0,56},{8,0},{16,8},{24,16},{32,24},{40,32},{48,40},{56,48},{1,57}... | collective-permute-start | bytes 786440 | tf_op jit(solution)/shard_map/ppermute | solution.py:25
  211.4 3.8 %collective-permute-done.20 = bf16[64,2048]{1,0:T(8,128)(2,1)S(1)} collective-permute-done((bf16[64,2048]{1,0:T(8,128)(2,1)S(1)}, bf16[64,2048]{1,0:T(8,128)(2,1)S(1)}, u32[]{:S(2)}, u32[]{:S(2)}) %collective-permute-start.20) | collective-permute-done | bytes 262176 | tf_op jit(solution)/shard_map/ppermute | solution.py:25
  215.1 3.8 %collective-permute-done.16 = bf16[64,2048]{1,0:T(8,128)(2,1)S(1)} collective-permute-done((bf16[64,2048]{1,0:T(8,128)(2,1)S(1)}, bf16[64,2048]{1,0:T(8,128)(2,1)S(1)}, u32[]{:S(2)}, u32[]{:S(2)}) %collective-permute-start.16) | collective-permute-done | bytes 262176 | tf_op jit(solution)/shard_map/ppermute | solution.py:25
  222.4 5.4 %collective-permute-done.17 = bf16[64,2048]{1,0:T(8,128)(2,1)S(1)} collective-permute-done((bf16[64,2048]{1,0:T(8,128)(2,1)S(1)}, bf16[64,2048]{1,0:T(8,128)(2,1)S(1)}, u32[]{:S(2)}, u32[]{:S(2)}) %collective-permute-start.17) | collective-permute-done | bytes 262176 | tf_op jit(solution)/shard_map/ppermute | solution.py:25
  228.0 3.5 %collective-permute-start.22 = (bf16[64,2048]{1,0:T(8,128)(2,1)S(1)}, bf16[64,2048]{1,0:T(8,128)(2,1)S(1)}, u32[]{:S(2)}, u32[]{:S(2)}) collective-permute-start(bf16[64,2048]{1,0:T(8,128)(2,1)S(1)} %get-tuple-element.14), channel_id=1, source_target_pairs={{0,56},{8,0},{16,8},{24,16},{32,24},{40,32},{48,40},{56,48},{1,57}... | collective-permute-start | bytes 786440 | tf_op jit(solution)/shard_map/ppermute | solution.py:25
  231.5 4.3 %collective-permute-done.18 = bf16[64,2048]{1,0:T(8,128)(2,1)S(1)} collective-permute-done((bf16[64,2048]{1,0:T(8,128)(2,1)S(1)}, bf16[64,2048]{1,0:T(8,128)(2,1)S(1)}, u32[]{:S(2)}, u32[]{:S(2)}) %collective-permute-start.18) | collective-permute-done | bytes 262176 | tf_op jit(solution)/shard_map/ppermute | solution.py:25
  (117 shorter events, 54.6 us)
Async XLA Ops:
  1.2 11.2 %collective-permute-start = (bf16[2,256,128]{2,1,0:T(8,128)(2,1)S(1)}, bf16[2,256,128]{2,1,0:T(8,128)(2,1)S(1)}, u32[]{:S(2)}, u32[]{:S(2)}) collective-permute-start(bf16[2,256,128]{2,1,0:T(8,128)(2,1)S(1)} %fusion.68), channel_id=1, source_target_pairs={{0,8},{8,16},{16,24},{24,32},{32,40},{40,48},{48,56},{56,64},{64,7... | collective-permute-start | bytes 393224 | tf_op jit(solution)/shard_map/ppermute | solution.py:34
  21.9 25.3 %collective-permute-start.1 = (bf16[256,2048]{1,0:T(8,128)(2,1)}, bf16[256,2048]{1,0:T(8,128)(2,1)S(1)}, u32[]{:S(2)}, u32[]{:S(2)}) collective-permute-start(bf16[256,2048]{1,0:T(8,128)(2,1)} %convolution_convert_fusion.3), channel_id=1, source_target_pairs={{0,1},{1,0},{2,3},{3,2},{4,5},{5,4},{6,7},{7,6},{8,9},{9,8},{10,11... | collective-permute-start | bytes 3145736 | tf_op jit(solution)/shard_map/ppermute | solution.py:29
  48.0 7.9 %collective-permute-start.2 = (bf16[64,2048]{1,0:T(8,128)(2,1)S(1)}, bf16[64,2048]{1,0:T(8,128)(2,1)S(1)}, u32[]{:S(2)}, u32[]{:S(2)}) collective-permute-start(bf16[64,2048]{1,0:T(8,128)(2,1)S(1)} %get-tuple-element.23), channel_id=1, source_target_pairs={{0,2},{2,4},{4,6},{6,0},{1,3},{3,5},{5,7},{7,1},{8,10},{10,12},{12... | collective-permute-start | bytes 786440 | tf_op jit(solution)/shard_map/ppermute | solution.py:25
  49.7 10.1 %collective-permute-start.3 = (bf16[64,2048]{1,0:T(8,128)(2,1)S(1)}, bf16[64,2048]{1,0:T(8,128)(2,1)S(1)}, u32[]{:S(2)}, u32[]{:S(2)}) collective-permute-start(bf16[64,2048]{1,0:T(8,128)(2,1)S(1)} %get-tuple-element.25), channel_id=1, source_target_pairs={{0,4},{2,6},{4,0},{6,2},{1,5},{3,7},{5,1},{7,3},{8,12},{10,14},{12... | collective-permute-start | bytes 786440 | tf_op jit(solution)/shard_map/ppermute | solution.py:25
  52.6 7.2 %collective-permute-start.4 = (bf16[64,2048]{1,0:T(8,128)(2,1)S(1)}, bf16[64,2048]{1,0:T(8,128)(2,1)S(1)}, u32[]{:S(2)}, u32[]{:S(2)}) collective-permute-start(bf16[64,2048]{1,0:T(8,128)(2,1)S(1)} %get-tuple-element.24), channel_id=1, source_target_pairs={{0,6},{2,0},{4,2},{6,4},{1,7},{3,1},{5,3},{7,5},{8,14},{10,8},{12,... | collective-permute-start | bytes 786440 | tf_op jit(solution)/shard_map/ppermute | solution.py:25
  60.9 9.1 %collective-permute-start.5 = (bf16[64,2048]{1,0:T(8,128)(2,1)S(1)}, bf16[64,2048]{1,0:T(8,128)(2,1)S(1)}, u32[]{:S(2)}, u32[]{:S(2)}) collective-permute-start(bf16[64,2048]{1,0:T(8,128)(2,1)S(1)} %get-tuple-element.6), channel_id=1, source_target_pairs={{0,8},{8,16},{16,24},{24,32},{32,40},{40,48},{48,56},{56,0},{1,9},... | collective-permute-start | bytes 786440 | tf_op jit(solution)/shard_map/ppermute | solution.py:25
  61.5 8.5 %collective-permute-start.6 = (bf16[64,2048]{1,0:T(8,128)(2,1)S(1)}, bf16[64,2048]{1,0:T(8,128)(2,1)S(1)}, u32[]{:S(2)}, u32[]{:S(2)}) collective-permute-start(bf16[64,2048]{1,0:T(8,128)(2,1)S(1)} %get-tuple-element.6), channel_id=1, source_target_pairs={{0,56},{8,0},{16,8},{24,16},{32,24},{40,32},{48,40},{56,48},{1,57}... | collective-permute-start | bytes 786440 | tf_op jit(solution)/shard_map/ppermute | solution.py:25
  70.0 8.2 %collective-permute-start.7 = (bf16[64,2048]{1,0:T(8,128)(2,1)S(1)}, bf16[64,2048]{1,0:T(8,128)(2,1)S(1)}, u32[]{:S(2)}, u32[]{:S(2)}) collective-permute-start(bf16[64,2048]{1,0:T(8,128)(2,1)S(1)} %collective-permute-done.5), channel_id=1, source_target_pairs={{0,8},{8,16},{16,24},{24,32},{32,40},{40,48},{48,56},{56,0},{1,9},... | collective-permute-start | bytes 786440 | tf_op jit(solution)/shard_map/ppermute | solution.py:25
  70.0 8.2 %collective-permute-start.8 = (bf16[64,2048]{1,0:T(8,128)(2,1)S(1)}, bf16[64,2048]{1,0:T(8,128)(2,1)S(1)}, u32[]{:S(2)}, u32[]{:S(2)}) collective-permute-start(bf16[64,2048]{1,0:T(8,128)(2,1)S(1)} %collective-permute-done.6), channel_id=1, source_target_pairs={{0,56},{8,0},{16,8},{24,16},{32,24},{40,32},{48,40},{56,48},{1,57}... | collective-permute-start | bytes 786440 | tf_op jit(solution)/shard_map/ppermute | solution.py:25
  78.2 7.6 %collective-permute-start.9 = (bf16[64,2048]{1,0:T(8,128)(2,1)S(1)}, bf16[64,2048]{1,0:T(8,128)(2,1)S(1)}, u32[]{:S(2)}, u32[]{:S(2)}) collective-permute-start(bf16[64,2048]{1,0:T(8,128)(2,1)S(1)} %collective-permute-done.7), channel_id=1, source_target_pairs={{0,8},{8,16},{16,24},{24,32},{32,40},{40,48},{48,56},{56,0},{1,9},... | collective-permute-start | bytes 786440 | tf_op jit(solution)/shard_map/ppermute | solution.py:25
  78.2 7.7 %collective-permute-start.10 = (bf16[64,2048]{1,0:T(8,128)(2,1)S(1)}, bf16[64,2048]{1,0:T(8,128)(2,1)S(1)}, u32[]{:S(2)}, u32[]{:S(2)}) collective-permute-start(bf16[64,2048]{1,0:T(8,128)(2,1)S(1)} %collective-permute-done.8), channel_id=1, source_target_pairs={{0,56},{8,0},{16,8},{24,16},{32,24},{40,32},{48,40},{56,48},{1,57}... | collective-permute-start | bytes 786440 | tf_op jit(solution)/shard_map/ppermute | solution.py:25
  85.8 6.3 %collective-permute-start.11 = (bf16[64,1024]{1,0:T(8,128)(2,1)S(1)}, bf16[64,1024]{1,0:T(8,128)(2,1)S(1)}, u32[]{:S(2)}, u32[]{:S(2)}) collective-permute-start(bf16[64,1024]{1,0:T(8,128)(2,1)S(1)} %slice.128), channel_id=1, source_target_pairs={{0,8},{8,16},{16,24},{24,32},{32,40},{40,48},{48,56},{56,0},{1,9},... | collective-permute-start | bytes 393224 | tf_op jit(solution)/shard_map/ppermute | solution.py:25
  85.9 6.1 %collective-permute-start.12 = (bf16[64,1024]{1,0:T(8,128)(2,1)S(1)}, bf16[64,1024]{1,0:T(8,128)(2,1)S(1)}, u32[]{:S(2)}, u32[]{:S(2)}) collective-permute-start(bf16[64,1024]{1,0:T(8,128)(2,1)S(1)} %slice.129), channel_id=1, source_target_pairs={{0,56},{8,0},{16,8},{24,16},{32,24},{40,32},{48,40},{56,48},{1,57}... | collective-permute-start | bytes 393224 | tf_op jit(solution)/shard_map/ppermute | solution.py:25
  125.5 4.9 %collective-permute-start.13 = (bf16[640,2048]{1,0:T(8,128)(2,1)S(1)}, bf16[640,2048]{1,0:T(8,128)(2,1)S(1)}, u32[]{:S(2)}, u32[]{:S(2)}) collective-permute-start(bf16[640,2048]{1,0:T(8,128)(2,1)S(1)} %bitcast.105), channel_id=1, source_target_pairs={{0,1},{1,0},{2,3},{3,2},{4,5},{5,4},{6,7},{7,6},{8,9},{9,8},{10,11... | collective-permute-start | bytes 7864328 | tf_op jit(solution)/shard_map/ppermute | solution.py:29
  141.8 5.3 %collective-permute-start.14 = (bf16[640,2048]{1,0:T(8,128)(2,1)}, bf16[640,2048]{1,0:T(8,128)(2,1)}, u32[]{:S(2)}, u32[]{:S(2)}) collective-permute-start(bf16[640,2048]{1,0:T(8,128)(2,1)} %convolution_convert_fusion.1), channel_id=1, source_target_pairs={{0,1},{1,0},{2,3},{3,2},{4,5},{5,4},{6,7},{7,6},{8,9},{9,8},{10,11... | collective-permute-start | bytes 7864328 | tf_op jit(solution)/shard_map/ppermute | solution.py:29
  155.3 42.7 %all-to-all-start.1 = ((bf16[16,40,2048]{2,1,0:T(8,128)(2,1)}), bf16[16,40,2048]{2,1,0:T(8,128)(2,1)}, u32[]{:S(2)}, u32[]{:S(2)}) async-start(bf16[16,40,2048]{2,1,0:T(8,128)(2,1)} %bitcast.108), calls=%async_computation.1 | async-start | bytes 5242880 | tf_op jit(solution)/shard_map/all_to_all | solution.py:174
  201.6 6.3 %collective-permute-start.15 = (bf16[64,1024]{1,0:T(8,128)(2,1)S(1)}, bf16[64,1024]{1,0:T(8,128)(2,1)S(1)}, u32[]{:S(2)}, u32[]{:S(2)}) collective-permute-start(bf16[64,1024]{1,0:T(8,128)(2,1)S(1)} %get-tuple-element.19), channel_id=1, source_target_pairs={{0,8},{8,16},{16,24},{24,32},{32,40},{40,48},{48,56},{56,0},{1,9},... | collective-permute-start | bytes 393224 | tf_op jit(solution)/shard_map/ppermute | solution.py:25
  201.7 6.2 %collective-permute-start.19 = (bf16[64,1024]{1,0:T(8,128)(2,1)S(1)}, bf16[64,1024]{1,0:T(8,128)(2,1)S(1)}, u32[]{:S(2)}, u32[]{:S(2)}) collective-permute-start(bf16[64,1024]{1,0:T(8,128)(2,1)S(1)} %get-tuple-element.20), channel_id=1, source_target_pairs={{0,56},{8,0},{16,8},{24,16},{32,24},{40,32},{48,40},{56,48},{1,57}... | collective-permute-start | bytes 393224 | tf_op jit(solution)/shard_map/ppermute | solution.py:25
  207.9 7.2 %collective-permute-start.20 = (bf16[64,2048]{1,0:T(8,128)(2,1)S(1)}, bf16[64,2048]{1,0:T(8,128)(2,1)S(1)}, u32[]{:S(2)}, u32[]{:S(2)}) collective-permute-start(bf16[64,2048]{1,0:T(8,128)(2,1)S(1)} %pad_maximum_fusion.7), channel_id=1, source_target_pairs={{0,56},{8,0},{16,8},{24,16},{32,24},{40,32},{48,40},{56,48},{1,57}... | collective-permute-start | bytes 786440 | tf_op jit(solution)/shard_map/ppermute | solution.py:25
  211.3 7.7 %collective-permute-start.16 = (bf16[64,2048]{1,0:T(8,128)(2,1)S(1)}, bf16[64,2048]{1,0:T(8,128)(2,1)S(1)}, u32[]{:S(2)}, u32[]{:S(2)}) collective-permute-start(bf16[64,2048]{1,0:T(8,128)(2,1)S(1)} %pad_maximum_fusion.6), channel_id=1, source_target_pairs={{0,8},{8,16},{16,24},{24,32},{32,40},{40,48},{48,56},{56,0},{1,9},... | collective-permute-start | bytes 786440 | tf_op jit(solution)/shard_map/ppermute | solution.py:25
  219.1 8.7 %collective-permute-start.17 = (bf16[64,2048]{1,0:T(8,128)(2,1)S(1)}, bf16[64,2048]{1,0:T(8,128)(2,1)S(1)}, u32[]{:S(2)}, u32[]{:S(2)}) collective-permute-start(bf16[64,2048]{1,0:T(8,128)(2,1)S(1)} %get-tuple-element.15), channel_id=1, source_target_pairs={{0,8},{8,16},{16,24},{24,32},{32,40},{40,48},{48,56},{56,0},{1,9},... | collective-permute-start | bytes 786440 | tf_op jit(solution)/shard_map/ppermute | solution.py:25
  219.2 8.6 %collective-permute-start.21 = (bf16[64,2048]{1,0:T(8,128)(2,1)S(1)}, bf16[64,2048]{1,0:T(8,128)(2,1)S(1)}, u32[]{:S(2)}, u32[]{:S(2)}) collective-permute-start(bf16[64,2048]{1,0:T(8,128)(2,1)S(1)} %get-tuple-element.16), channel_id=1, source_target_pairs={{0,56},{8,0},{16,8},{24,16},{32,24},{40,32},{48,40},{56,48},{1,57}... | collective-permute-start | bytes 786440 | tf_op jit(solution)/shard_map/ppermute | solution.py:25
  227.9 7.9 %collective-permute-start.18 = (bf16[64,2048]{1,0:T(8,128)(2,1)S(1)}, bf16[64,2048]{1,0:T(8,128)(2,1)S(1)}, u32[]{:S(2)}, u32[]{:S(2)}) collective-permute-start(bf16[64,2048]{1,0:T(8,128)(2,1)S(1)} %get-tuple-element.13), channel_id=1, source_target_pairs={{0,8},{8,16},{16,24},{24,32},{32,40},{40,48},{48,56},{56,0},{1,9},... | collective-permute-start | bytes 786440 | tf_op jit(solution)/shard_map/ppermute | solution.py:25
  228.0 7.8 %collective-permute-start.22 = (bf16[64,2048]{1,0:T(8,128)(2,1)S(1)}, bf16[64,2048]{1,0:T(8,128)(2,1)S(1)}, u32[]{:S(2)}, u32[]{:S(2)}) collective-permute-start(bf16[64,2048]{1,0:T(8,128)(2,1)S(1)} %get-tuple-element.14), channel_id=1, source_target_pairs={{0,56},{8,0},{16,8},{24,16},{32,24},{40,32},{48,40},{56,48},{1,57}... | collective-permute-start | bytes 786440 | tf_op jit(solution)/shard_map/ppermute | solution.py:25
  (10 other events, 120.4 us)

commit v2 on v1

--- a/solution.py
+++ b/solution.py
@@ -3,6 +3,8 @@
 import jax
 import jax.numpy as jnp
 from jax import lax
+from jax.experimental import pallas as pl
+from jax.experimental.pallas import tpu as pltpu
 from jax.sharding import Mesh, PartitionSpec as P
 
 HQ = 32
@@ -136,20 +138,29 @@
     return blocks[0].astype(F32) + right.astype(F32) + left.astype(F32)
 
 
+def across_planes(own):
+    z = lax.axis_index("z")
+    held = own[None]
+    for bit in (1, 2, 4):
+        other = lax.ppermute(held, "z", [(i, i ^ bit) for i in range(NZ)])
+        held = jnp.concatenate([held, other], axis=0)
+    order = z ^ ((z + jnp.array(RING, jnp.int32)) % NZ)
+    return jnp.take(held, order, axis=0)
+
+
 def slots_of(expert_ids, gate_weights):
     z = lax.axis_index("z")
-    own = jnp.concatenate([expert_ids.astype(F32), gate_weights], axis=1)
-    everywhere = lax.all_gather(own, "z", axis=0, tiled=False)
-    order = (z + jnp.array(RING, jnp.int32)) % NZ
-    everywhere = jnp.take(everywhere, order, axis=0)
     top = expert_ids.shape[1]
-    ids = everywhere[:, :, :top].astype(jnp.int32)
-    gates = everywhere[:, :, top:]
+    everywhere = across_planes(
+        jnp.concatenate([expert_ids.T.astype(F32), gate_weights.T], axis=0)
+    )
+    ids = everywhere[:, :top].astype(jnp.int32)
+    gates = everywhere[:, top:]
     place = jnp.arange(PLANE, dtype=jnp.int32)
     experts = (place // NY * NZ + z) * NY + place % NY
     match = ids[None] == experts[:, None, None, None]
-    named = jnp.any(match, axis=3)
-    gate = jnp.sum(jnp.where(match, gates[None], 0.0), axis=3)
+    named = jnp.any(match, axis=2)
+    gate = jnp.sum(jnp.where(match, gates[None], 0.0), axis=2)
     before = jnp.triu(jnp.ones((ROWS, ROWS), BF), 1)
     rank = jnp.dot(
         named.astype(BF).reshape(PLANE * NZ, ROWS), before, preferred_element_type=F32
@@ -162,11 +173,67 @@
     return one_hot, weighted.reshape(PLANE * SLOTS, NZ * ROWS)
 
 
-def expert_rows(rows, w_gate, w_up, w_down):
-    gate_act = jnp.dot(rows, w_gate, preferred_element_type=F32)
-    up_act = jnp.dot(rows, w_up, preferred_element_type=F32)
-    hidden = (jax.nn.silu(gate_act) * up_act).astype(BF)
-    return jnp.dot(hidden, w_down, preferred_element_type=F32).astype(BF)
+def expert_body(rows_ref, g0, g1, u0, u1, d0, d1, out_ref, g_all, u_all, d_all, hidden, sems):
+    half = g0.shape[2]
+    copies = [
+        pltpu.make_async_copy(g0.at[0], g_all.at[:, :half], sems.at[0]),
+        pltpu.make_async_copy(g1.at[0], g_all.at[:, half:], sems.at[1]),
+        pltpu.make_async_copy(u0.at[0], u_all.at[:, :half], sems.at[2]),
+        pltpu.make_async_copy(u1.at[0], u_all.at[:, half:], sems.at[3]),
+        pltpu.make_async_copy(d0.at[0], d_all.at[:half], sems.at[4]),
+        pltpu.make_async_copy(d1.at[0], d_all.at[half:], sems.at[5]),
+    ]
+    for copy in copies:
+        copy.start()
+    tile = 256
+    for copy in copies[:4]:
+        copy.wait()
+
+    def inner(i, carry):
+        at = pl.ds(pl.multiple_of(i * tile, tile), tile)
+        gate_act = jnp.dot(rows_ref[...], g_all[:, at], preferred_element_type=F32)
+        up_act = jnp.dot(rows_ref[...], u_all[:, at], preferred_element_type=F32)
+        hidden[:, at] = (gate_act / (1.0 + jnp.exp(-gate_act)) * up_act).astype(BF)
+        return carry
+
+    lax.fori_loop(0, g_all.shape[1] // tile, inner, 0)
+    for copy in copies[4:]:
+        copy.wait()
+
+    def outer(i, carry):
+        at = pl.ds(pl.multiple_of(i * tile, tile), tile)
+        out_ref[:, at] = jnp.dot(
+            hidden[...], d_all[:, at], preferred_element_type=F32
+        ).astype(BF)
+        return carry
+
+    lax.fori_loop(0, d_all.shape[1] // tile, outer, 0)
+
+
+def expert_rows(rows, gate_pair, up_pair, down_pair):
+    count, width = rows.shape
+    hid = 2 * gate_pair[0].shape[2]
+    whole = pl.BlockSpec(memory_space=pltpu.VMEM)
+    there = pl.BlockSpec(memory_space=pltpu.HBM)
+    return pl.pallas_call(
+        expert_body,
+        out_shape=jax.ShapeDtypeStruct((count, width), BF),
+        in_specs=[whole] + [there] * 6,
+        out_specs=whole,
+        scratch_shapes=[
+            pltpu.VMEM((width, hid), BF),
+            pltpu.VMEM((width, hid), BF),
+            pltpu.VMEM((hid, width), BF),
+            pltpu.VMEM((count, hid), BF),
+            pltpu.SemaphoreType.DMA((6,)),
+        ],
+        compiler_params=pltpu.CompilerParams(vmem_limit_bytes=28 * 1024 * 1024),
+        cost_estimate=pl.CostEstimate(
+            flops=6 * count * width * hid,
+            bytes_accessed=6 * width * hid + 4 * count * width,
+            transcendentals=count * hid,
+        ),
+    )(rows, *gate_pair, *up_pair, *down_pair)
 
 
 def exchange(rows):
@@ -191,20 +258,20 @@
     w_up,
     w_down,
 ):
+    pairs = [(w, swap_cores(w)) for w in (w_gate, w_up, w_down)]
     one_hot, weighted = slots_of(expert_ids, gate_weights)
     attn_rows = attend(queries, key_rows, value_rows, doc_lengths)
     mid = residual_in.astype(F32) + project(attn_rows, out_weight)
     spread = jnp.mean(mid * mid, axis=1, keepdims=True)
     normed = (mid * lax.rsqrt(spread + 1e-06) * norm_gain[None, :]).astype(BF)
 
+    normed, pairs, one_hot, weighted = lax.optimization_barrier(
+        (normed, pairs, one_hot, weighted)
+    )
     tokens = ring_gather(normed)
     outgoing = jnp.dot(one_hot, tokens, preferred_element_type=F32).astype(BF)
     mine = exchange(outgoing)
-    theirs = swap_cores(mine)
-    part_mine = expert_rows(mine, w_gate[0], w_up[0], w_down[0])
-    part_theirs = expert_rows(theirs, w_gate[0], w_up[0], w_down[0])
-    other_half = swap_cores(part_theirs)
-    pair_out = (part_mine.astype(F32) + other_half.astype(F32)).astype(BF)
+    pair_out = expert_rows(mine, *pairs)
     returned = exchange(pair_out)
     plane_sum = lax.dot_general(
         weighted, returned, (((0,), (0,)), ((), ())), preferred_element_type=F32

time: 238 us -> 207 us (0.87)
  waiting for transfers between devices: 82.4 us -> 55.1 us
  matrix products: 39 us -> 14.3 us
  Pallas kernels: 0 us -> 10.3 us
  local copies, waits for them, and re-layouts: 12 us -> 6.32 us
  starting transfers between devices: 43.2 us -> 48.3 us
  blocking collectives: 52.6 us -> 57.4 us
  other arithmetic: 6.9 us -> 11 us
    all_to_all x1 -> x0, waiting for transfers between devices: 35.7 us -> none  [exchange(): lax.all_to_all(rows.reshape(PLANE, SLOTS, width), ('x', 'y'), split_axis=...]
    all_to_all x1 -> x2, blocking collectives: 28.1 us -> 57.4 us  [exchange(): lax.all_to_all(rows.reshape(PLANE, SLOTS, width), ('x', 'y'), split_axis=...]
    all_gather x1 -> x0, blocking collectives: 24.6 us -> none  [slots_of(): everywhere = lax.all_gather(own, 'z', axis=0, tiled=False)]
    dot_general x4 -> x0, matrix products: 22.8 us -> none  [the longest x2 15.6 us: expert_rows(): return jnp.dot(hidden, w_down, preferred_element_type=F32).astype(BF)]
    ppermute x19, waiting for transfers between devices: 38.3 us -> 51 us  [shift(): lax.ppermute(value, axis, [(i, (i + by) % size) for i in range(size)])]
    ppermute x0 -> x3, starting transfers between devices: none -> 10.3 us  [across_planes(): other = lax.ppermute(held, 'z', [(i, i ^ bit) for i in range(NZ)])]
    pallas_call x0 -> x1, Pallas kernels: none -> 10.3 us  [expert_rows(): pl.pallas_call(expert_body, out_shape=jax.ShapeDtypeStruct((count, width)...]
    unnamed x27 -> x28, local copies, waits for them, and re-layouts: 7.3 us -> 0.18 us
  transfers between devices with their start and end apart: 24 -> 27, of which waited for: 15 -> 19; matrix products, arithmetic and copies ran while one was open for 7% -> 13% of each run, Pallas kernels for 0% -> 0%
where the time goes in v2:
time: 207 us; the launch traced here: 203 us
  blocking collectives  57.4 us (28%)
  waiting for transfers between devices  55.1 us (27%)
  starting transfers between devices  48.3 us (23%)
  matrix products  14.3 us (7%)
  other arithmetic  11 us (5%)
  Pallas kernels  10.3 us (5%)
  local copies, waits for them, and re-layouts  6.32 us (3%)
    all_to_all x2, blocking collectives, exchange(): lax.all_to_all(rows.reshape(PLANE, SLOTS, width), ('x', 'y'), split_axis=...  57.4 us
    ppermute x19, waiting for transfers between devices, shift(): lax.ppermute(value, axis, [(i, (i + by) % size) for i in range(size)])  51 us
    ppermute x19, starting transfers between devices, shift(): lax.ppermute(value, axis, [(i, (i + by) % size) for i in range(size)])  33.1 us
    ppermute x3, starting transfers between devices, across_planes(): other = lax.ppermute(held, 'z', [(i, i ^ bit) for i in range(NZ)])  10.3 us
    pallas_call x1, Pallas kernels, expert_rows(): pl.pallas_call(expert_body, out_shape=jax.ShapeDtypeStruct((count, width)...  10.3 us
    sub x1, matrix products, attend(): weights = jnp.exp(jnp.where(visible, scores - row_top, masked_low))  4.41 us
  transfers between devices with their start and end apart: 27, of which 19 were waited for; matrix products, arithmetic and copies ran while one was open for 13% of the time, Pallas kernels for 0%

profile of v2, /device:TPU:2, one launch (start us, length us, event | category | flops | bytes accessed | tf_op | source)
XLA Modules:
  0.0 203.3 jit_solution(14654246333710779419)
XLA Ops:
  1.2 3.8 %collective-permute-start = (bf16[2,256,128]{2,1,0:T(8,128)(2,1)S(1)}, bf16[2,256,128]{2,1,0:T(8,128)(2,1)S(1)}, u32[]{:S(2)}, u32[]{:S(2)}) collective-permute-start(bf16[2,256,128]{2,1,0:T(8,128)(2,1)S(1)} %fusion.43), channel_id=1, source_target_pairs={{0,8},{8,16},{16,24},{24,32},{32,40},{40,48},{48,56},{56,64},{64,7... | collective-permute-start | bytes 393224 | tf_op jit(solution)/shard_map/ppermute | solution.py:36
  13.2 4.4 %fusion.72 = (f32[2,4,256]{2,1,0:T(4,128)S(1)}, bf16[2,4,256,512]{2,3,1,0:T(8,128)(2,1)}) fusion(pred[2,256,512]{1,2,0:T(8,128)(4,1)} %and_and_fusion, bf16[2,256,4,128]{3,2,1,0:T(4,128)(2,1)S(1)} %reshape.208, bf16[2,1,512,128]{3,2,1,0:T(8,128)(2,1)S(1)} %get-tuple-element.51, bf16[2,1,512,128]{3,2,1,0:T(8,128)(2,1)S(1)} %get-tuple-element.50), kind=kOutput, calls=%fused_computation.134 | convolution fusion | flops 545260032 | bytes 4726784 | tf_op jit(solution)/shard_map/sub | solution.py:77
  17.6 2.6 %fusion.18 = bf16[2,256,4,128]{3,1,2,0:T(8,128)(2,1)S(1)} fusion(bf16[2,4,256,512]{2,3,1,0:T(8,128)(2,1)} %get-tuple-element.57, f32[2,256,4]{1,2,0:T(4,128)S(1)} %bitcast.96, bf16[2,1,512,128]{3,2,1,0:T(8,128)(2,1)S(1)} %get-tuple-element.50, bf16[2,1,512,128]{3,2,1,0:T(8,128)(2,1)S(1)} %get-tuple-element.51), kind=kOutput, calls=%fused_computation.23 | convolution fusion | flops 269090816 | bytes 3153920 | tf_op jit(solution)/shard_map/zvoe,zey->zvoy/dot_general | solution.py:79
  24.3 4.6 %collective-permute-start.9 = (f32[2,16,64]{2,1,0:T(8,128)S(1)}, f32[2,16,64]{2,1,0:T(8,128)S(1)}, u32[]{:S(2)}, u32[]{:S(2)}) collective-permute-start(f32[2,16,64]{2,1,0:T(8,128)S(1)} %pad_maximum_fusion.10), channel_id=1, source_target_pairs={{0,16},{8,24},{16,0},{24,8},{32,48},{40,56},{48,32},{56,40},{1,17}... | collective-permute-start | bytes 24584 | tf_op jit(solution)/shard_map/ppermute | solution.py:145
  30.6 3.8 %collective-permute-start.10 = (f32[4,16,64]{2,1,0:T(8,128)S(1)}, f32[4,16,64]{2,1,0:T(8,128)}, u32[]{:S(2)}, u32[]{:S(2)}) collective-permute-start(f32[4,16,64]{2,1,0:T(8,128)S(1)} %pad_maximum_fusion.9), channel_id=1, source_target_pairs={{0,32},{8,40},{16,48},{24,56},{32,0},{40,8},{48,16},{56,24},{1,33}... | collective-permute-start | bytes 49160 | tf_op jit(solution)/shard_map/ppermute | solution.py:145
  35.7 2.9 %collective-permute-done.10 = f32[4,16,64]{2,1,0:T(8,128)} collective-permute-done((f32[4,16,64]{2,1,0:T(8,128)S(1)}, f32[4,16,64]{2,1,0:T(8,128)}, u32[]{:S(2)}, u32[]{:S(2)}) %collective-permute-start.10) | collective-permute-done | bytes 16416 | tf_op jit(solution)/shard_map/ppermute | solution.py:145
  45.6 3.0 %collective-permute-start.3 = (bf16[64,2048]{1,0:T(8,128)(2,1)}, bf16[64,2048]{1,0:T(8,128)(2,1)S(1)}, u32[]{:S(2)}, u32[]{:S(2)}) collective-permute-start(bf16[64,2048]{1,0:T(8,128)(2,1)} %get-tuple-element.41), channel_id=1, source_target_pairs={{0,4},{2,6},{4,0},{6,2},{1,5},{3,7},{5,1},{7,3},{8,12},{10,14},{12... | collective-permute-start | bytes 786440 | tf_op jit(solution)/shard_map/ppermute | solution.py:27
  48.5 4.7 %collective-permute-done.2 = bf16[64,2048]{1,0:T(8,128)(2,1)S(1)} collective-permute-done((bf16[64,2048]{1,0:T(8,128)(2,1)S(1)}, bf16[64,2048]{1,0:T(8,128)(2,1)S(1)}, u32[]{:S(2)}, u32[]{:S(2)}) %collective-permute-start.2) | collective-permute-done | bytes 262176 | tf_op jit(solution)/shard_map/ppermute | solution.py:27
  61.3 3.1 %collective-permute-start.12 = (bf16[64,2048]{1,0:T(8,128)(2,1)S(1)}, bf16[64,2048]{1,0:T(8,128)(2,1)S(1)}, u32[]{:S(2)}, u32[]{:S(2)}) collective-permute-start(bf16[64,2048]{1,0:T(8,128)(2,1)S(1)} %multiply_convert_fusion), channel_id=1, source_target_pairs={{0,56},{8,0},{16,8},{24,16},{32,24},{40,32},{48,40},{56,48},{1,57}... | collective-permute-start | bytes 786440 | tf_op jit(solution)/shard_map/ppermute | solution.py:27
  64.5 5.6 %collective-permute-done.11 = bf16[64,2048]{1,0:T(8,128)(2,1)S(1)} collective-permute-done((bf16[64,2048]{1,0:T(8,128)(2,1)S(1)}, bf16[64,2048]{1,0:T(8,128)(2,1)S(1)}, u32[]{:S(2)}, u32[]{:S(2)}) %collective-permute-start.11) | collective-permute-done | bytes 262176 | tf_op jit(solution)/shard_map/ppermute | solution.py:27
  73.7 6.5 %collective-permute-done.13 = bf16[64,2048]{1,0:T(8,128)(2,1)S(1)} collective-permute-done((bf16[64,2048]{1,0:T(8,128)(2,1)S(1)}, bf16[64,2048]{1,0:T(8,128)(2,1)S(1)}, u32[]{:S(2)}, u32[]{:S(2)}) %collective-permute-start.13) | collective-permute-done | bytes 262176 | tf_op jit(solution)/shard_map/ppermute | solution.py:27
  80.6 3.4 %collective-permute-start.16 = (bf16[64,2048]{1,0:T(8,128)(2,1)S(1)}, bf16[64,2048]{1,0:T(8,128)(2,1)S(1)}, u32[]{:S(2)}, u32[]{:S(2)}) collective-permute-start(bf16[64,2048]{1,0:T(8,128)(2,1)S(1)} %collective-permute-done.14), channel_id=1, source_target_pairs={{0,56},{8,0},{16,8},{24,16},{32,24},{40,32},{48,40},{56,48},{1,57}... | collective-permute-start | bytes 786440 | tf_op jit(solution)/shard_map/ppermute | solution.py:27
  84.0 4.4 %collective-permute-done.15 = bf16[64,2048]{1,0:T(8,128)(2,1)S(1)} collective-permute-done((bf16[64,2048]{1,0:T(8,128)(2,1)S(1)}, bf16[64,2048]{1,0:T(8,128)(2,1)S(1)}, u32[]{:S(2)}, u32[]{:S(2)}) %collective-permute-start.15) | collective-permute-done | bytes 262176 | tf_op jit(solution)/shard_map/ppermute | solution.py:27
  88.6 3.7 %collective-permute-start.18 = (bf16[64,1024]{1,0:T(8,128)(2,1)S(1)}, bf16[64,1024]{1,0:T(8,128)(2,1)S(1)}, u32[]{:S(2)}, u32[]{:S(2)}) collective-permute-start(bf16[64,1024]{1,0:T(8,128)(2,1)S(1)} %slice.129), channel_id=1, source_target_pairs={{0,56},{8,0},{16,8},{24,16},{32,24},{40,32},{48,40},{56,48},{1,57}... | collective-permute-start | bytes 393224 | tf_op jit(solution)/shard_map/ppermute | solution.py:27
  96.4 30.6 %all_to_all.10 = bf16[16,40,2048]{2,1,0:T(8,128)(2,1)S(1)} all-to-all(bf16[16,40,2048]{2,1,0:T(8,128)(2,1)S(1)} %bitcast.90), channel_id=1, replica_groups=mesh['x'=4,'z'=8,'y'=4,'c'=2] {'x','y'}, dimensions={0} | all-to-all | bytes 5242880 | tf_op jit(solution)/shard_map/all_to_all | solution.py:241
  127.0 10.3 %shard_map.127 = bf16[640,2048]{1,0:T(8,128)(2,1)S(1)} custom-call(bf16[640,2048]{1,0:T(8,128)(2,1)S(1)} %bitcast.87, bf16[1,2048,384]{2,1,0:T(8,128)(2,1)S(1)} %copy-done.1, bf16[1,2048,384]{2,1,0:T(8,128)(2,1)} %collective-permute-done.5.g1, bf16[1,2048,384]{2,1,0:T(8,128)(2,1)S(1)} %copy-done.2, bf16[1,2048,384]{2,1,0:T(8,128)(2,1)} %collective-permute-done.6.u1, ...), custom_call_target="tpu_custom_call" | custom-call | flops 6039797760 | bytes 14680064 | tf_op jit(solution)/shard_map/pallas_call | solution.py:218
  137.3 26.9 %all_to_all.11 = bf16[16,40,2048]{2,1,0:T(8,128)(2,1)S(1)} all-to-all(bf16[16,40,2048]{2,1,0:T(8,128)(2,1)S(1)} %bitcast.88), channel_id=1, replica_groups=mesh['x'=4,'z'=8,'y'=4,'c'=2] {'x','y'}, dimensions={0} | all-to-all | bytes 5242880 | tf_op jit(solution)/shard_map/all_to_all | solution.py:241
  169.4 2.9 %collective-permute-done.19 = bf16[64,1024]{1,0:T(8,128)(2,1)S(1)} collective-permute-done((bf16[64,1024]{1,0:T(8,128)(2,1)S(1)}, bf16[64,1024]{1,0:T(8,128)(2,1)S(1)}, u32[]{:S(2)}, u32[]{:S(2)}) %collective-permute-start.19) | collective-permute-done | bytes 131104 | tf_op jit(solution)/shard_map/ppermute | solution.py:27
  176.7 4.2 %collective-permute-done.24 = bf16[64,2048]{1,0:T(8,128)(2,1)S(1)} collective-permute-done((bf16[64,2048]{1,0:T(8,128)(2,1)S(1)}, bf16[64,2048]{1,0:T(8,128)(2,1)S(1)}, u32[]{:S(2)}, u32[]{:S(2)}) %collective-permute-start.24) | collective-permute-done | bytes 262176 | tf_op jit(solution)/shard_map/ppermute | solution.py:27
  181.0 4.8 %collective-permute-done.20 = bf16[64,2048]{1,0:T(8,128)(2,1)S(1)} collective-permute-done((bf16[64,2048]{1,0:T(8,128)(2,1)S(1)}, bf16[64,2048]{1,0:T(8,128)(2,1)S(1)}, u32[]{:S(2)}, u32[]{:S(2)}) %collective-permute-start.20) | collective-permute-done | bytes 262176 | tf_op jit(solution)/shard_map/ppermute | solution.py:27
  186.0 3.2 %collective-permute-start.25 = (bf16[64,2048]{1,0:T(8,128)(2,1)S(1)}, bf16[64,2048]{1,0:T(8,128)(2,1)S(1)}, u32[]{:S(2)}, u32[]{:S(2)}) collective-permute-start(bf16[64,2048]{1,0:T(8,128)(2,1)S(1)} %get-tuple-element.32), channel_id=1, source_target_pairs={{0,56},{8,0},{16,8},{24,16},{32,24},{40,32},{48,40},{56,48},{1,57}... | collective-permute-start | bytes 786440 | tf_op jit(solution)/shard_map/ppermute | solution.py:27
  189.2 4.3 %collective-permute-done.21 = bf16[64,2048]{1,0:T(8,128)(2,1)S(1)} collective-permute-done((bf16[64,2048]{1,0:T(8,128)(2,1)S(1)}, bf16[64,2048]{1,0:T(8,128)(2,1)S(1)}, u32[]{:S(2)}, u32[]{:S(2)}) %collective-permute-start.21) | collective-permute-done | bytes 262176 | tf_op jit(solution)/shard_map/ppermute | solution.py:27
  194.4 2.7 %collective-permute-start.26 = (bf16[64,2048]{1,0:T(8,128)(2,1)S(1)}, bf16[64,2048]{1,0:T(8,128)(2,1)S(1)}, u32[]{:S(2)}, u32[]{:S(2)}) collective-permute-start(bf16[64,2048]{1,0:T(8,128)(2,1)S(1)} %get-tuple-element.30), channel_id=1, source_target_pairs={{0,56},{8,0},{16,8},{24,16},{32,24},{40,32},{48,40},{56,48},{1,57}... | collective-permute-start | bytes 786440 | tf_op jit(solution)/shard_map/ppermute | solution.py:27
  197.1 4.3 %collective-permute-done.22 = bf16[64,2048]{1,0:T(8,128)(2,1)S(1)} collective-permute-done((bf16[64,2048]{1,0:T(8,128)(2,1)S(1)}, bf16[64,2048]{1,0:T(8,128)(2,1)S(1)}, u32[]{:S(2)}, u32[]{:S(2)}) %collective-permute-start.22) | collective-permute-done | bytes 262176 | tf_op jit(solution)/shard_map/ppermute | solution.py:27
  (125 shorter events, 52.1 us)
Async XLA Ops:
  1.2 12.0 %collective-permute-start = (bf16[2,256,128]{2,1,0:T(8,128)(2,1)S(1)}, bf16[2,256,128]{2,1,0:T(8,128)(2,1)S(1)}, u32[]{:S(2)}, u32[]{:S(2)}) collective-permute-start(bf16[2,256,128]{2,1,0:T(8,128)(2,1)S(1)} %fusion.43), channel_id=1, source_target_pairs={{0,8},{8,16},{16,24},{24,32},{32,40},{40,48},{48,56},{56,64},{64,7... | collective-permute-start | bytes 393224 | tf_op jit(solution)/shard_map/ppermute | solution.py:36
  6.4 17.9 %collective-permute-start.8 = (f32[1,16,64]{2,1,0:T(8,128)S(1)}, f32[1,16,64]{2,1,0:T(8,128)S(1)}, u32[]{:S(2)}, u32[]{:S(2)}) collective-permute-start(f32[1,16,64]{2,1,0:T(8,128)S(1)} %maximum_bitcast_fusion), channel_id=1, source_target_pairs={{0,8},{8,0},{16,24},{24,16},{32,40},{40,32},{48,56},{56,48},{1,9},... | collective-permute-start | bytes 12296 | tf_op jit(solution)/shard_map/ppermute | solution.py:145
  8.3 52.8 %collective-permute-start.5 = (bf16[1,2048,384]{2,1,0:T(8,128)(2,1)}, bf16[1,2048,384]{2,1,0:T(8,128)(2,1)}, u32[]{:S(2)}, u32[]{:S(2)}) collective-permute-start(bf16[1,2048,384]{2,1,0:T(8,128)(2,1)} %g0), channel_id=1, source_target_pairs={{0,1},{1,0},{2,3},{3,2},{4,5},{5,4},{6,7},{7,6},{8,9},{9,8},{10,11... | collective-permute-start | bytes 4718600 | tf_op jit(solution)/shard_map/ppermute | solution.py:31
  8.3 52.8 %collective-permute-start.6 = (bf16[1,2048,384]{2,1,0:T(8,128)(2,1)}, bf16[1,2048,384]{2,1,0:T(8,128)(2,1)}, u32[]{:S(2)}, u32[]{:S(2)}) collective-permute-start(bf16[1,2048,384]{2,1,0:T(8,128)(2,1)} %u0), channel_id=1, source_target_pairs={{0,1},{1,0},{2,3},{3,2},{4,5},{5,4},{6,7},{7,6},{8,9},{9,8},{10,11... | collective-permute-start | bytes 4718600 | tf_op jit(solution)/shard_map/ppermute | solution.py:31
  8.8 52.3 %collective-permute-start.7 = (bf16[1,384,2048]{2,1,0:T(8,128)(2,1)}, bf16[1,384,2048]{2,1,0:T(8,128)(2,1)}, u32[]{:S(2)}, u32[]{:S(2)}) collective-permute-start(bf16[1,384,2048]{2,1,0:T(8,128)(2,1)} %d0), channel_id=1, source_target_pairs={{0,1},{1,0},{2,3},{3,2},{4,5},{5,4},{6,7},{7,6},{8,9},{9,8},{10,11... | collective-permute-start | bytes 4718600 | tf_op jit(solution)/shard_map/ppermute | solution.py:31
  22.6 18.2 %collective-permute-start.1 = (bf16[256,2048]{1,0:T(8,128)(2,1)}, bf16[256,2048]{1,0:T(8,128)(2,1)S(1)}, u32[]{:S(2)}, u32[]{:S(2)}) collective-permute-start(bf16[256,2048]{1,0:T(8,128)(2,1)} %convolution_convert_fusion.2), channel_id=1, source_target_pairs={{0,1},{1,0},{2,3},{3,2},{4,5},{5,4},{6,7},{7,6},{8,9},{9,8},{10,11... | collective-permute-start | bytes 3145736 | tf_op jit(solution)/shard_map/ppermute | solution.py:31
  24.3 6.3 %collective-permute-start.9 = (f32[2,16,64]{2,1,0:T(8,128)S(1)}, f32[2,16,64]{2,1,0:T(8,128)S(1)}, u32[]{:S(2)}, u32[]{:S(2)}) collective-permute-start(f32[2,16,64]{2,1,0:T(8,128)S(1)} %pad_maximum_fusion.10), channel_id=1, source_target_pairs={{0,16},{8,24},{16,0},{24,8},{32,48},{40,56},{48,32},{56,40},{1,17}... | collective-permute-start | bytes 24584 | tf_op jit(solution)/shard_map/ppermute | solution.py:145
  30.6 7.9 %collective-permute-start.10 = (f32[4,16,64]{2,1,0:T(8,128)S(1)}, f32[4,16,64]{2,1,0:T(8,128)}, u32[]{:S(2)}, u32[]{:S(2)}) collective-permute-start(f32[4,16,64]{2,1,0:T(8,128)S(1)} %pad_maximum_fusion.9), channel_id=1, source_target_pairs={{0,32},{8,40},{16,48},{24,56},{32,0},{40,8},{48,16},{56,24},{1,33}... | collective-permute-start | bytes 49160 | tf_op jit(solution)/shard_map/ppermute | solution.py:145
  43.7 9.5 %collective-permute-start.2 = (bf16[64,2048]{1,0:T(8,128)(2,1)S(1)}, bf16[64,2048]{1,0:T(8,128)(2,1)S(1)}, u32[]{:S(2)}, u32[]{:S(2)}) collective-permute-start(bf16[64,2048]{1,0:T(8,128)(2,1)S(1)} %get-tuple-element.39), channel_id=1, source_target_pairs={{0,2},{2,4},{4,6},{6,0},{1,3},{3,5},{5,7},{7,1},{8,10},{10,12},{12... | collective-permute-start | bytes 786440 | tf_op jit(solution)/shard_map/ppermute | solution.py:27
  45.6 12.4 %collective-permute-start.3 = (bf16[64,2048]{1,0:T(8,128)(2,1)}, bf16[64,2048]{1,0:T(8,128)(2,1)S(1)}, u32[]{:S(2)}, u32[]{:S(2)}) collective-permute-start(bf16[64,2048]{1,0:T(8,128)(2,1)} %get-tuple-element.41), channel_id=1, source_target_pairs={{0,4},{2,6},{4,0},{6,2},{1,5},{3,7},{5,1},{7,3},{8,12},{10,14},{12... | collective-permute-start | bytes 786440 | tf_op jit(solution)/shard_map/ppermute | solution.py:27
  53.2 6.4 %collective-permute-start.4 = (bf16[64,2048]{1,0:T(8,128)(2,1)S(1)}, bf16[64,2048]{1,0:T(8,128)(2,1)S(1)}, u32[]{:S(2)}, u32[]{:S(2)}) collective-permute-start(bf16[64,2048]{1,0:T(8,128)(2,1)S(1)} %get-tuple-element.40), channel_id=1, source_target_pairs={{0,6},{2,0},{4,2},{6,4},{1,7},{3,1},{5,3},{7,5},{8,14},{10,8},{12,... | collective-permute-start | bytes 786440 | tf_op jit(solution)/shard_map/ppermute | solution.py:27
  61.1 8.9 %collective-permute-start.11 = (bf16[64,2048]{1,0:T(8,128)(2,1)S(1)}, bf16[64,2048]{1,0:T(8,128)(2,1)S(1)}, u32[]{:S(2)}, u32[]{:S(2)}) collective-permute-start(bf16[64,2048]{1,0:T(8,128)(2,1)S(1)} %multiply_convert_fusion), channel_id=1, source_target_pairs={{0,8},{8,16},{16,24},{24,32},{32,40},{40,48},{48,56},{56,0},{1,9},... | collective-permute-start | bytes 786440 | tf_op jit(solution)/shard_map/ppermute | solution.py:27
  61.3 10.5 %collective-permute-start.12 = (bf16[64,2048]{1,0:T(8,128)(2,1)S(1)}, bf16[64,2048]{1,0:T(8,128)(2,1)S(1)}, u32[]{:S(2)}, u32[]{:S(2)}) collective-permute-start(bf16[64,2048]{1,0:T(8,128)(2,1)S(1)} %multiply_convert_fusion), channel_id=1, source_target_pairs={{0,56},{8,0},{16,8},{24,16},{32,24},{40,32},{48,40},{56,48},{1,57}... | collective-permute-start | bytes 786440 | tf_op jit(solution)/shard_map/ppermute | solution.py:27
  70.1 10.1 %collective-permute-start.13 = (bf16[64,2048]{1,0:T(8,128)(2,1)S(1)}, bf16[64,2048]{1,0:T(8,128)(2,1)S(1)}, u32[]{:S(2)}, u32[]{:S(2)}) collective-permute-start(bf16[64,2048]{1,0:T(8,128)(2,1)S(1)} %collective-permute-done.11), channel_id=1, source_target_pairs={{0,8},{8,16},{16,24},{24,32},{32,40},{40,48},{48,56},{56,0},{1,9},... | collective-permute-start | bytes 786440 | tf_op jit(solution)/shard_map/ppermute | solution.py:27
  71.8 8.8 %collective-permute-start.14 = (bf16[64,2048]{1,0:T(8,128)(2,1)S(1)}, bf16[64,2048]{1,0:T(8,128)(2,1)S(1)}, u32[]{:S(2)}, u32[]{:S(2)}) collective-permute-start(bf16[64,2048]{1,0:T(8,128)(2,1)S(1)} %collective-permute-done.12), channel_id=1, source_target_pairs={{0,56},{8,0},{16,8},{24,16},{32,24},{40,32},{48,40},{56,48},{1,57}... | collective-permute-start | bytes 786440 | tf_op jit(solution)/shard_map/ppermute | solution.py:27
  80.2 8.2 %collective-permute-start.15 = (bf16[64,2048]{1,0:T(8,128)(2,1)S(1)}, bf16[64,2048]{1,0:T(8,128)(2,1)S(1)}, u32[]{:S(2)}, u32[]{:S(2)}) collective-permute-start(bf16[64,2048]{1,0:T(8,128)(2,1)S(1)} %collective-permute-done.13), channel_id=1, source_target_pairs={{0,8},{8,16},{16,24},{24,32},{32,40},{40,48},{48,56},{56,0},{1,9},... | collective-permute-start | bytes 786440 | tf_op jit(solution)/shard_map/ppermute | solution.py:27
  80.6 7.9 %collective-permute-start.16 = (bf16[64,2048]{1,0:T(8,128)(2,1)S(1)}, bf16[64,2048]{1,0:T(8,128)(2,1)S(1)}, u32[]{:S(2)}, u32[]{:S(2)}) collective-permute-start(bf16[64,2048]{1,0:T(8,128)(2,1)S(1)} %collective-permute-done.14), channel_id=1, source_target_pairs={{0,56},{8,0},{16,8},{24,16},{32,24},{40,32},{48,40},{56,48},{1,57}... | collective-permute-start | bytes 786440 | tf_op jit(solution)/shard_map/ppermute | solution.py:27
  88.4 6.3 %collective-permute-start.17 = (bf16[64,1024]{1,0:T(8,128)(2,1)S(1)}, bf16[64,1024]{1,0:T(8,128)(2,1)S(1)}, u32[]{:S(2)}, u32[]{:S(2)}) collective-permute-start(bf16[64,1024]{1,0:T(8,128)(2,1)S(1)} %slice.128), channel_id=1, source_target_pairs={{0,8},{8,16},{16,24},{24,32},{32,40},{40,48},{48,56},{56,0},{1,9},... | collective-permute-start | bytes 393224 | tf_op jit(solution)/shard_map/ppermute | solution.py:27
  174.5 6.5 %collective-permute-start.24 = (bf16[64,2048]{1,0:T(8,128)(2,1)S(1)}, bf16[64,2048]{1,0:T(8,128)(2,1)S(1)}, u32[]{:S(2)}, u32[]{:S(2)}) collective-permute-start(bf16[64,2048]{1,0:T(8,128)(2,1)S(1)} %pad_maximum_fusion.7), channel_id=1, source_target_pairs={{0,56},{8,0},{16,8},{24,16},{32,24},{40,32},{48,40},{56,48},{1,57}... | collective-permute-start | bytes 786440 | tf_op jit(solution)/shard_map/ppermute | solution.py:27
  175.8 10.0 %collective-permute-start.20 = (bf16[64,2048]{1,0:T(8,128)(2,1)S(1)}, bf16[64,2048]{1,0:T(8,128)(2,1)S(1)}, u32[]{:S(2)}, u32[]{:S(2)}) collective-permute-start(bf16[64,2048]{1,0:T(8,128)(2,1)S(1)} %pad_maximum_fusion.6), channel_id=1, source_target_pairs={{0,8},{8,16},{16,24},{24,32},{32,40},{40,48},{48,56},{56,0},{1,9},... | collective-permute-start | bytes 786440 | tf_op jit(solution)/shard_map/ppermute | solution.py:27
  185.9 7.7 %collective-permute-start.21 = (bf16[64,2048]{1,0:T(8,128)(2,1)S(1)}, bf16[64,2048]{1,0:T(8,128)(2,1)S(1)}, u32[]{:S(2)}, u32[]{:S(2)}) collective-permute-start(bf16[64,2048]{1,0:T(8,128)(2,1)S(1)} %get-tuple-element.31), channel_id=1, source_target_pairs={{0,8},{8,16},{16,24},{24,32},{32,40},{40,48},{48,56},{56,0},{1,9},... | collective-permute-start | bytes 786440 | tf_op jit(solution)/shard_map/ppermute | solution.py:27
  186.0 7.6 %collective-permute-start.25 = (bf16[64,2048]{1,0:T(8,128)(2,1)S(1)}, bf16[64,2048]{1,0:T(8,128)(2,1)S(1)}, u32[]{:S(2)}, u32[]{:S(2)}) collective-permute-start(bf16[64,2048]{1,0:T(8,128)(2,1)S(1)} %get-tuple-element.32), channel_id=1, source_target_pairs={{0,56},{8,0},{16,8},{24,16},{32,24},{40,32},{48,40},{56,48},{1,57}... | collective-permute-start | bytes 786440 | tf_op jit(solution)/shard_map/ppermute | solution.py:27
  193.7 7.7 %collective-permute-start.22 = (bf16[64,2048]{1,0:T(8,128)(2,1)S(1)}, bf16[64,2048]{1,0:T(8,128)(2,1)S(1)}, u32[]{:S(2)}, u32[]{:S(2)}) collective-permute-start(bf16[64,2048]{1,0:T(8,128)(2,1)S(1)} %get-tuple-element.29), channel_id=1, source_target_pairs={{0,8},{8,16},{16,24},{24,32},{32,40},{40,48},{48,56},{56,0},{1,9},... | collective-permute-start | bytes 786440 | tf_op jit(solution)/shard_map/ppermute | solution.py:27
  194.4 8.0 %collective-permute-start.26 = (bf16[64,2048]{1,0:T(8,128)(2,1)S(1)}, bf16[64,2048]{1,0:T(8,128)(2,1)S(1)}, u32[]{:S(2)}, u32[]{:S(2)}) collective-permute-start(bf16[64,2048]{1,0:T(8,128)(2,1)S(1)} %get-tuple-element.30), channel_id=1, source_target_pairs={{0,56},{8,0},{16,8},{24,16},{32,24},{40,32},{48,40},{56,48},{1,57}... | collective-permute-start | bytes 786440 | tf_op jit(solution)/shard_map/ppermute | solution.py:27
  (13 other events, 200.9 us)

commit v3 on v2

--- a/solution.py
+++ b/solution.py
@@ -7,9 +7,8 @@
 from jax.experimental.pallas import tpu as pltpu
 from jax.sharding import Mesh, PartitionSpec as P
 
-HQ = 32
-KVH = 4
 HD = 128
+NDOCS = 128
 NX, NZ, NY, NC = 4, 8, 4, 2
 ROWS = 64
 CAP = 5
@@ -36,73 +35,160 @@
     return lax.ppermute(value, ("x", "z"), [(i, i + 1) for i in range(devices - 1)])
 
 
-def doc_of(positions, doc_lengths):
-    doc_ends = jnp.cumsum(doc_lengths)
-    return jnp.sum((positions[:, None] >= doc_ends[None, :]).astype(jnp.int32), axis=1)
-
-
-def attend(queries, key_rows, value_rows, doc_lengths):
-    tok_rows = queries.shape[0]
-    half_rows = tok_rows // 2
-    heads_here = queries.shape[1] // HD
-    seq_index = lax.axis_index(("x", "z"))
-    group_index = lax.axis_index("y")
-    query_block_list = queries.reshape(2, half_rows, heads_here, HD)
-    query_pos = seq_index * tok_rows + jnp.arange(tok_rows, dtype=jnp.int32)
-    query_doc = doc_of(query_pos, doc_lengths).reshape(2, half_rows)
-    query_pos = query_pos.reshape(2, half_rows)
-    key_head = lax.dynamic_slice_in_dim(key_rows, group_index * HD, HD, 1)
-    value_head = lax.dynamic_slice_in_dim(value_rows, group_index * HD, HD, 1)
-    own_pair = jnp.stack([key_head, value_head])
-    previous_tail = from_behind(own_pair[:, half_rows:])
-    joined = jnp.concatenate([previous_tail, own_pair], axis=1)
-    windows = jnp.stack([joined[:, :tok_rows], joined[:, half_rows:]], axis=1)
-    key_pos = (
-        seq_index * tok_rows
-        - half_rows
-        + jnp.arange(2, dtype=jnp.int32)[:, None] * half_rows
-        + jnp.arange(tok_rows, dtype=jnp.int32)[None, :]
-    )
-    key_doc = doc_of(key_pos.reshape(-1), doc_lengths).reshape(2, tok_rows)
-    scores = jnp.einsum(
-        "fiza,fla->fzil", query_block_list, windows[0], preferred_element_type=F32
-    ) * (1.0 / math.sqrt(HD))
-    visible = (
-        (key_pos[:, None, :] <= query_pos[:, :, None])
-        & (key_doc[:, None, :] == query_doc[:, :, None])
-        & (key_pos[:, None, :] >= 0)
-    )
-    visible = visible[:, None]
-    row_top = jnp.max(jnp.where(visible, scores, masked_low), axis=3, keepdims=True)
-    weights = jnp.exp(jnp.where(visible, scores - row_top, masked_low))
-    totals = jnp.sum(weights, axis=3)
-    mixture = jnp.einsum(
-        "zvoe,zey->zvoy", weights.astype(BF), windows[1], preferred_element_type=F32
-    )
-    result = (mixture / totals[:, :, :, None]).astype(BF)
-    return result.transpose(0, 2, 1, 3).reshape(tok_rows, heads_here * HD)
-
-
-def project(attn_rows, out_weight):
-    width = out_weight.shape[1]
+def attend_half(base, queries, keys, values, lengths, store):
+    rows = queries.shape[0]
+    place = lax.broadcasted_iota(jnp.int32, (NDOCS, NDOCS), 0)
+    upto = place <= lax.broadcasted_iota(jnp.int32, (NDOCS, NDOCS), 1)
+    spread = jnp.broadcast_to(lengths.astype(F32), (8, NDOCS)).astype(BF)
+    ends = jnp.dot(spread, jnp.where(upto, 1.0, 0.0).astype(BF), preferred_element_type=F32)[:1]
+    query_pos = base + lax.broadcasted_iota(jnp.int32, (rows, 1), 0)
+    ended = ends <= query_pos.astype(F32)
+    start = jnp.max(jnp.where(ended, ends, 0.0), axis=1, keepdims=True).astype(jnp.int32)
+    span = 2 * keys[0].shape[0]
+    key_pos = base - keys[0].shape[0] + lax.broadcasted_iota(jnp.int32, (1, span), 1)
+    visible = (key_pos <= query_pos) & (key_pos >= start)
+    key_window = jnp.concatenate(keys, axis=0)
+    value_window = jnp.concatenate(values, axis=0)
+    for head in range(queries.shape[1] // HD):
+        at = slice(head * HD, (head + 1) * HD)
+        scores = lax.dot_general(
+            queries[:, at], key_window, (((1,), (1,)), ((), ())), preferred_element_type=F32
+        ) * (1.0 / math.sqrt(HD))
+        scores = jnp.where(visible, scores, masked_low)
+        weights = jnp.exp(scores - jnp.max(scores, axis=1, keepdims=True))
+        total = jnp.sum(weights, axis=1, keepdims=True)
+        mixture = jnp.dot(weights.astype(BF), value_window, preferred_element_type=F32)
+        store(at, (mixture / total).astype(BF))
+
+
+def late_body(where, q_ref, ka, kb, va, vb, len_ref, out_ref):
+    def store(at, value):
+        out_ref[:, at] = value
+
+    attend_half(
+        where[0] + q_ref.shape[0], q_ref[...], [ka[...], kb[...]], [va[...], vb[...]], len_ref[...], store
+    )
+
+
+def early_body(
+    where, q_ref, tails, kb, vb, len_ref, late_ref, w_ref, theirs_ref, mine_ref, held, picked
+):
+    rows = q_ref.shape[0]
+
+    def store(at, value):
+        held[:rows, at] = value
+
+    held[rows:] = late_ref[...]
+    attend_half(
+        where[0], q_ref[...], [tails[0], kb[...]], [tails[1], vb[...]], len_ref[...], store
+    )
+    y, c = where[1], where[2]
+    for k in range(NY):
+        block = lax.rem(y + k, NY) * (NC * ROWS)
+        here = pl.ds(pl.multiple_of(block + c * ROWS, ROWS), ROWS)
+        there = pl.ds(pl.multiple_of(block + (1 - c) * ROWS, ROWS), ROWS)
+        mine_ref[k * ROWS : (k + 1) * ROWS] = held[here]
+        picked[k * ROWS : (k + 1) * ROWS] = held[there]
+    tile = 512
+
+    def column(i, carry):
+        at = pl.ds(pl.multiple_of(i * tile, tile), tile)
+        theirs_ref[:, at] = jnp.dot(
+            picked[...], w_ref[:, at], preferred_element_type=F32
+        ).astype(BF)
+        return carry
+
+    lax.fori_loop(0, w_ref.shape[1] // tile, column, 0)
+
+
+def attend(queries, key_rows, value_rows, doc_lengths, out_weight, held):
+    tok_rows, width = queries.shape
+    half = tok_rows // 2
+    out_width = out_weight.shape[1]
     y, c = lax.axis_index("y"), lax.axis_index("c")
-    blocks = attn_rows.reshape(NY, NC, ROWS, -1)
-
-    def rows_for(core):
-        picked = [
-            lax.dynamic_slice(blocks, ((y + k) % NY, core, 0, 0), (1, 1, ROWS, blocks.shape[3]))
-            for k in range(NY)
-        ]
-        return jnp.concatenate(picked, axis=0).reshape(NY * ROWS, -1)
-
-    theirs = jnp.dot(rows_for(1 - c), out_weight, preferred_element_type=F32).astype(BF)
-    arrived = swap_cores(theirs)
-    mine = jnp.dot(rows_for(c), out_weight, preferred_element_type=F32)
-    both = (mine + arrived.astype(F32)).reshape(NY, ROWS, width)
-    total = both[0]
-    for k in range(1, NY):
-        total = total + shift(both[k].astype(BF), "y", NY, k).astype(F32)
-    return total
+    where = jnp.stack([lax.axis_index(("x", "z")) * tok_rows, y, c]).astype(jnp.int32)
+    lengths = doc_lengths.reshape(1, -1)
+    tails = from_behind(
+        jnp.stack(
+            [
+                lax.dynamic_slice(rows, (half, y * HD), (half, HD))
+                for rows in (key_rows, value_rows)
+            ]
+        )
+    )
+
+    def part(i):
+        return pl.BlockSpec((half, HD), lambda g, where: (i, where[1]))
+
+    def all_of(*shape):
+        return pl.BlockSpec(shape, lambda g, where: (0,) * len(shape))
+
+    lens = all_of(1, doc_lengths.shape[0])
+    params = pltpu.CompilerParams(vmem_limit_bytes=56 * 1024 * 1024)
+    scores = tok_rows * tok_rows * (width // HD) // 2
+    late = pl.pallas_call(
+        late_body,
+        out_shape=jax.ShapeDtypeStruct((half, width), BF),
+        grid_spec=pltpu.PrefetchScalarGridSpec(
+            num_scalar_prefetch=1,
+            grid=(1,),
+            in_specs=[
+                pl.BlockSpec((half, width), lambda g, where: (1, 0)),
+                part(0),
+                part(1),
+                part(0),
+                part(1),
+                lens,
+            ],
+            out_specs=all_of(half, width),
+        ),
+        compiler_params=params,
+        cost_estimate=pl.CostEstimate(
+            flops=16 * scores * HD, bytes_accessed=6 * half * width, transcendentals=8 * scores
+        ),
+    )(where, queries, key_rows, key_rows, value_rows, value_rows, lengths)
+    late, held = lax.optimization_barrier((late, double(held, 1)))
+    theirs, mine = pl.pallas_call(
+        early_body,
+        out_shape=(
+            jax.ShapeDtypeStruct((half, out_width), BF),
+            jax.ShapeDtypeStruct((half, width), BF),
+        ),
+        grid_spec=pltpu.PrefetchScalarGridSpec(
+            num_scalar_prefetch=1,
+            grid=(1,),
+            in_specs=[
+                pl.BlockSpec((half, width), lambda g, where: (0, 0)),
+                all_of(2, half, HD),
+                part(0),
+                part(0),
+                lens,
+                all_of(half, width),
+                all_of(*out_weight.shape),
+            ],
+            out_specs=(all_of(half, out_width), all_of(half, width)),
+            scratch_shapes=[pltpu.VMEM((tok_rows, width), BF), pltpu.VMEM((half, width), BF)],
+        ),
+        compiler_params=params,
+        cost_estimate=pl.CostEstimate(
+            flops=16 * scores * HD + 2 * half * width * out_width,
+            bytes_accessed=6 * half * width + 2 * width * out_width,
+            transcendentals=8 * scores,
+        ),
+    )(where, queries, tails, key_rows, value_rows, lengths, late, out_weight)
+    theirs, held = lax.optimization_barrier((theirs, double(held, 2)))
+    return theirs, mine, held
+
+
+def project(theirs, attn_mine, out_weight, held):
+    arrived, held = lax.optimization_barrier((swap_cores(theirs), double(held, 4)))
+    mine = lax.optimization_barrier(
+        jnp.dot(attn_mine, out_weight, preferred_element_type=F32)
+    )
+    both = (mine + arrived.astype(F32)).reshape(NY, ROWS, out_weight.shape[1])
+    sent = both.astype(BF)
+    moved = [shift(sent[k], "y", NY, k) for k in range(1, NY)]
+    return both[0] + sum(block.astype(F32) for block in moved), held
 
 
 def ring_gather(own):
@@ -130,30 +216,25 @@
     b = shift(blocks[4][:, half:], "z", NZ, -1)
     right = jnp.concatenate([add(blocks[3][:, :half], a), blocks[3][:, half:]], axis=1)
     left = jnp.concatenate([blocks[-3][:, :half], add(blocks[-3][:, half:], b)], axis=1)
+    right, left = lax.optimization_barrier(right), lax.optimization_barrier(left)
     for step in (2, 1):
-        right = add(shift(right, "z", NZ, 1), blocks[step])
-        left = add(shift(left, "z", NZ, -1), blocks[-step])
+        right = lax.optimization_barrier(add(shift(right, "z", NZ, 1), blocks[step]))
+        left = lax.optimization_barrier(add(shift(left, "z", NZ, -1), blocks[-step]))
     right = shift(right, "z", NZ, 1)
     left = shift(left, "z", NZ, -1)
     return blocks[0].astype(F32) + right.astype(F32) + left.astype(F32)
 
 
-def across_planes(own):
+def double(held, bit):
+    other = lax.ppermute(held, "z", [(i, i ^ bit) for i in range(NZ)])
+    return jnp.concatenate([held, other], axis=0)
+
+
+def slots_of(held):
     z = lax.axis_index("z")
-    held = own[None]
-    for bit in (1, 2, 4):
-        other = lax.ppermute(held, "z", [(i, i ^ bit) for i in range(NZ)])
-        held = jnp.concatenate([held, other], axis=0)
     order = z ^ ((z + jnp.array(RING, jnp.int32)) % NZ)
-    return jnp.take(held, order, axis=0)
-
-
-def slots_of(expert_ids, gate_weights):
-    z = lax.axis_index("z")
-    top = expert_ids.shape[1]
-    everywhere = across_planes(
-        jnp.concatenate([expert_ids.T.astype(F32), gate_weights.T], axis=0)
-    )
+    everywhere = jnp.take(held, order, axis=0)
+    top = held.shape[1] // 2
     ids = everywhere[:, :top].astype(jnp.int32)
     gates = everywhere[:, top:]
     place = jnp.arange(PLANE, dtype=jnp.int32)
@@ -183,20 +264,20 @@
         pltpu.make_async_copy(d0.at[0], d_all.at[:half], sems.at[4]),
         pltpu.make_async_copy(d1.at[0], d_all.at[half:], sems.at[5]),
     ]
-    for copy in copies:
-        copy.start()
+    for which in (0, 2, 1, 3, 4, 5):
+        copies[which].start()
     tile = 256
-    for copy in copies[:4]:
-        copy.wait()
-
-    def inner(i, carry):
-        at = pl.ds(pl.multiple_of(i * tile, tile), tile)
+    for i in range(g_all.shape[1] // tile):
+        if i == 0:
+            copies[0].wait()
+            copies[2].wait()
+        if i == half // tile:
+            copies[1].wait()
+            copies[3].wait()
+        at = slice(i * tile, (i + 1) * tile)
         gate_act = jnp.dot(rows_ref[...], g_all[:, at], preferred_element_type=F32)
         up_act = jnp.dot(rows_ref[...], u_all[:, at], preferred_element_type=F32)
         hidden[:, at] = (gate_act / (1.0 + jnp.exp(-gate_act)) * up_act).astype(BF)
-        return carry
-
-    lax.fori_loop(0, g_all.shape[1] // tile, inner, 0)
     for copy in copies[4:]:
         copy.wait()
 
@@ -259,16 +340,19 @@
     w_down,
 ):
     pairs = [(w, swap_cores(w)) for w in (w_gate, w_up, w_down)]
-    one_hot, weighted = slots_of(expert_ids, gate_weights)
-    attn_rows = attend(queries, key_rows, value_rows, doc_lengths)
-    mid = residual_in.astype(F32) + project(attn_rows, out_weight)
+    held = jnp.concatenate([expert_ids.T.astype(F32), gate_weights.T], axis=0)[None]
+    theirs, attn_mine, held = attend(
+        queries, key_rows, value_rows, doc_lengths, out_weight, held
+    )
+    projected, held = project(theirs, attn_mine, out_weight, held)
+    mid = residual_in.astype(F32) + projected
+    one_hot, weighted = slots_of(held)
     spread = jnp.mean(mid * mid, axis=1, keepdims=True)
     normed = (mid * lax.rsqrt(spread + 1e-06) * norm_gain[None, :]).astype(BF)
 
-    normed, pairs, one_hot, weighted = lax.optimization_barrier(
-        (normed, pairs, one_hot, weighted)
-    )
-    tokens = ring_gather(normed)
+    tokens, one_hot, weighted, pairs = lax.optimization_barrier(
+        (ring_gather(normed), one_hot, weighted, pairs)
+    )
     outgoing = jnp.dot(one_hot, tokens, preferred_element_type=F32).astype(BF)
     mine = exchange(outgoing)
     pair_out = expert_rows(mine, *pairs)

time: 207 us -> 213 us (1.029); the launches traced: 203 us -> 212 us
  blocking collectives: 57.4 us -> 70.8 us
  waiting for transfers between devices: 55.1 us -> 44.2 us
  Pallas kernels: 10.3 us -> 19.1 us
  matrix products: 14.3 us -> 7.47 us
  local copies, waits for them, and re-layouts: 6.32 us -> 9.4 us
  other arithmetic: 11 us -> 13.3 us
    all_to_all x2, blocking collectives: 57.4 us -> 70.8 us  [exchange(): lax.all_to_all(rows.reshape(PLANE, SLOTS, width), ('x', 'y'), split_axis=...]
    pallas_call x0 -> x2, Pallas kernels: none -> 10.4 us  [the longest x1 6.49 us: attend(): pl.pallas_call(early_body, out_shape=(jax.ShapeDtypeStruct((half, out_wid...]
    ppermute x19, waiting for transfers between devices: 51 us -> 40.9 us  [shift(): lax.ppermute(value, axis, [(i, (i + by) % size) for i in range(size)])]
    unnamed x28, local copies, waits for them, and re-layouts: 0.18 us -> 6.7 us
    sub x1 -> x0, matrix products: 4.41 us -> none  [attend(): weights = jnp.exp(jnp.where(visible, scores - row_top, masked_low))]
    dot_general x3 -> x1, matrix products: 6.41 us -> 2.4 us  [project(): jnp.dot(attn_mine, out_weight, preferred_element_type=F32)]
    convert_element_type x2, other arithmetic: 0.81 us -> 3.65 us  [the longest x1 2.96 us: project(): sent = both.astype(BF)]
  transfers between devices with their start and end apart: 27 -> 27, of which waited for: 19 -> 15; matrix products, arithmetic and copies ran while one was open for 13% -> 10% of each run, Pallas kernels for 0% -> 2%
where the time goes in v3:
time: 213 us; the launch traced here: 212 us
  blocking collectives  70.8 us (33%)
  starting transfers between devices  47.3 us (22%)
  waiting for transfers between devices  44.2 us (21%)
  Pallas kernels  19.1 us (9%)
  other arithmetic  13.3 us (6%)
  local copies, waits for them, and re-layouts  9.4 us (4%)
  matrix products  7.47 us (4%)
    all_to_all x2, blocking collectives, exchange(): lax.all_to_all(rows.reshape(PLANE, SLOTS, width), ('x', 'y'), split_axis=...  70.8 us
    ppermute x19, waiting for transfers between devices, shift(): lax.ppermute(value, axis, [(i, (i + by) % size) for i in range(size)])  40.9 us
    ppermute x19, starting transfers between devices, shift(): lax.ppermute(value, axis, [(i, (i + by) % size) for i in range(size)])  32.5 us
    ppermute x3, starting transfers between devices, double(): other = lax.ppermute(held, 'z', [(i, i ^ bit) for i in range(NZ)])  10.3 us
    pallas_call x1, Pallas kernels, expert_rows(): pl.pallas_call(expert_body, out_shape=jax.ShapeDtypeStruct((count, width)...  8.66 us
    unnamed x28, local copies, waits for them, and re-layouts  6.7 us
    pallas_call x1, Pallas kernels, attend(): pl.pallas_call(early_body, out_shape=(jax.ShapeDtypeStruct((half, out_wid...  6.49 us
  transfers between devices with their start and end apart: 27, of which 15 were waited for; matrix products, arithmetic and copies ran while one was open for 10% of the time, Pallas kernels for 2%

profile of v3, /device:TPU:2, one launch (start us, length us, event | category | flops | bytes accessed | tf_op | source)
XLA Modules:
  0.0 211.9 jit_solution(2779356725578177310)
XLA Ops:
  0.9 3.8 %collective-permute-start = (bf16[2,256,128]{2,1,0:T(8,128)(2,1)S(1)}, bf16[2,256,128]{2,1,0:T(8,128)(2,1)S(1)}, u32[]{:S(2)}, u32[]{:S(2)}) collective-permute-start(bf16[2,256,128]{2,1,0:T(8,128)(2,1)S(1)} %pad_maximum_fusion.2), channel_id=1, source_target_pairs={{0,8},{8,16},{16,24},{24,32},{32,40},{40,48},{48,56},{56,64},{64,7... | collective-permute-start | bytes 393224 | tf_op jit(solution)/shard_map/ppermute | solution.py:35
  8.6 3.9 %shard_map.127.late_ref = bf16[256,512]{1,0:T(8,128)(2,1)} custom-call(s32[3]{0:T(128)} %pad_add_fusion.where, bf16[512,512]{1,0:T(8,128)(2,1)} %q_ref.3, bf16[512,512]{1,0:T(8,128)(2,1)} %kb.3, bf16[512,512]{1,0:T(8,128)(2,1)} %kb.3, bf16[512,512]{1,0:T(8,128)(2,1)} %vb.3, bf16[512,512]{1,0:T(8,128)(2,1)} %vb.3, s32[1,128]{1,0:T(1,128)} %bitcast.41), custom_call_target="tpu_custom_call" | custom-call | flops 1073741824 | bytes 786432 | tf_op jit(solution)/shard_map/pallas_call | solution.py:129
  12.6 4.6 %collective-permute-start.2 = (f32[2,16,64]{2,1,0:T(8,128)S(1)}, f32[2,16,64]{2,1,0:T(8,128)S(1)}, u32[]{:S(2)}, u32[]{:S(2)}) collective-permute-start(f32[2,16,64]{2,1,0:T(8,128)S(1)} %pad_maximum_fusion.5), channel_id=1, source_target_pairs={{0,16},{8,24},{16,0},{24,8},{32,48},{40,56},{48,32},{56,40},{1,17}... | collective-permute-start | bytes 24584 | tf_op jit(solution)/shard_map/ppermute | solution.py:229
  19.5 6.5 %shard_map.128 = (bf16[256,2048]{1,0:T(8,128)(2,1)}, bf16[256,512]{1,0:T(8,128)(2,1)}) custom-call(s32[3]{0:T(128)} %pad_add_fusion.where, bf16[512,512]{1,0:T(8,128)(2,1)} %q_ref.3, bf16[2,256,128]{2,1,0:T(8,128)(2,1)} %copy-done.9, bf16[512,512]{1,0:T(8,128)(2,1)} %kb.3, bf16[512,512]{1,0:T(8,128)(2,1)} %vb.3, s32[1,128]{1,0:T(1,128)} %bitcast.42, ...), custom_call_target="tpu_custom_call" | custom-call | flops 1610612736 | bytes 2883584 | tf_op jit(solution)/shard_map/pallas_call | solution.py:151
  28.5 3.8 %collective-permute-start.4 = (f32[4,16,64]{2,1,0:T(8,128)S(1)}, f32[4,16,64]{2,1,0:T(8,128)S(1)}, u32[]{:S(2)}, u32[]{:S(2)}) collective-permute-start(f32[4,16,64]{2,1,0:T(8,128)S(1)} %pad_maximum_fusion.4), channel_id=1, source_target_pairs={{0,32},{8,40},{16,48},{24,56},{32,0},{40,8},{48,16},{56,24},{1,33}... | collective-permute-start | bytes 49160 | tf_op jit(solution)/shard_map/ppermute | solution.py:229
  36.3 3.0 %fusion.21 = (bf16[256,2048]{1,0:T(8,128)(2,1)S(1)}, f32[256,2048]{1,0:T(8,128)}) fusion(f32[256,2048]{1,0:T(8,128)S(1)} %fusion.25, bf16[256,2048]{1,0:T(8,128)(2,1)} %collective-permute-done.3), kind=kLoop, calls=%fused_computation.73 | loop fusion | flops 1572864 | bytes 6291456 | tf_op jit(solution)/shard_map/convert_element_type | solution.py:189
  49.9 6.2 %collective-permute-done.6 = bf16[64,2048]{1,0:T(8,128)(2,1)} collective-permute-done((bf16[64,2048]{1,0:T(8,128)(2,1)}, bf16[64,2048]{1,0:T(8,128)(2,1)}, u32[]{:S(2)}, u32[]{:S(2)}) %collective-permute-start.6) | collective-permute-done | bytes 262176 | tf_op jit(solution)/shard_map/ppermute | solution.py:26
  59.7 2.9 %collective-permute-start.9 = (bf16[64,2048]{1,0:T(8,128)(2,1)}, bf16[64,2048]{1,0:T(8,128)(2,1)S(1)}, u32[]{:S(2)}, u32[]{:S(2)}) collective-permute-start(bf16[64,2048]{1,0:T(8,128)(2,1)} %get-tuple-element.42), channel_id=1, source_target_pairs={{0,56},{8,0},{16,8},{24,16},{32,24},{40,32},{48,40},{56,48},{1,57}... | collective-permute-start | bytes 786440 | tf_op jit(solution)/shard_map/ppermute | solution.py:26
  63.6 4.8 %collective-permute-done.8 = bf16[64,2048]{1,0:T(8,128)(2,1)} collective-permute-done((bf16[64,2048]{1,0:T(8,128)(2,1)}, bf16[64,2048]{1,0:T(8,128)(2,1)}, u32[]{:S(2)}, u32[]{:S(2)}) %collective-permute-start.8) | collective-permute-done | bytes 262176 | tf_op jit(solution)/shard_map/ppermute | solution.py:26
  76.3 3.2 %collective-permute-start.13 = (bf16[64,2048]{1,0:T(8,128)(2,1)S(1)}, bf16[64,2048]{1,0:T(8,128)(2,1)S(1)}, u32[]{:S(2)}, u32[]{:S(2)}) collective-permute-start(bf16[64,2048]{1,0:T(8,128)(2,1)S(1)} %collective-permute-done.11), channel_id=1, source_target_pairs={{0,56},{8,0},{16,8},{24,16},{32,24},{40,32},{48,40},{56,48},{1,57}... | collective-permute-start | bytes 786440 | tf_op jit(solution)/shard_map/ppermute | solution.py:26
  81.0 2.9 %collective-permute-done.12 = bf16[64,2048]{1,0:T(8,128)(2,1)S(1)} collective-permute-done((bf16[64,2048]{1,0:T(8,128)(2,1)S(1)}, bf16[64,2048]{1,0:T(8,128)(2,1)S(1)}, u32[]{:S(2)}, u32[]{:S(2)}) %collective-permute-start.12) | collective-permute-done | bytes 262176 | tf_op jit(solution)/shard_map/ppermute | solution.py:26
  84.0 3.3 %collective-permute-start.15 = (bf16[64,1024]{1,0:T(8,128)(2,1)S(1)}, bf16[64,1024]{1,0:T(8,128)(2,1)S(1)}, u32[]{:S(2)}, u32[]{:S(2)}) collective-permute-start(bf16[64,1024]{1,0:T(8,128)(2,1)S(1)} %slice.104), channel_id=1, source_target_pairs={{0,56},{8,0},{16,8},{24,16},{32,24},{40,32},{48,40},{56,48},{1,57}... | collective-permute-start | bytes 393224 | tf_op jit(solution)/shard_map/ppermute | solution.py:26
  90.9 3.1 %convolution_convert_fusion = bf16[640,2048]{1,0:T(8,128)(2,1)S(1)} fusion(bf16[640,512]{1,0:T(8,128)(2,1)S(1)} %fusion.1, bf16[512,2048]{1,0:T(8,128)(2,1)} %maximum_dynamic-update-slice_fusion), kind=kOutput, calls=%fused_computation.1 | convolution fusion | flops 1343488000 | bytes 5373952 | tf_op jit(solution)/shard_map/dot_general | solution.py:356
  94.0 37.2 %all_to_all.10 = bf16[16,40,2048]{2,1,0:T(8,128)(2,1)S(1)} all-to-all(bf16[16,40,2048]{2,1,0:T(8,128)(2,1)S(1)} %bitcast.39), channel_id=1, replica_groups=mesh['x'=4,'z'=8,'y'=4,'c'=2] {'x','y'}, dimensions={0} | all-to-all | bytes 5242880 | tf_op jit(solution)/shard_map/all_to_all | solution.py:322
  131.3 8.7 %shard_map.129 = bf16[640,2048]{1,0:T(8,128)(2,1)S(1)} custom-call(bf16[640,2048]{1,0:T(8,128)(2,1)S(1)} %bitcast.36, bf16[1,2048,384]{2,1,0:T(8,128)(2,1)S(1)} %copy-done, bf16[1,2048,384]{2,1,0:T(8,128)(2,1)} %collective-permute-done.16.g1, bf16[1,2048,384]{2,1,0:T(8,128)(2,1)S(1)} %copy-done.1, bf16[1,2048,384]{2,1,0:T(8,128)(2,1)} %collective-permute-done.17.u1, ...), custom_call_target="tpu_custom_call" | custom-call | flops 6039797760 | bytes 14680064 | tf_op jit(solution)/shard_map/pallas_call | solution.py:299
  140.0 33.6 %all_to_all.11 = bf16[16,40,2048]{2,1,0:T(8,128)(2,1)S(1)} all-to-all(bf16[16,40,2048]{2,1,0:T(8,128)(2,1)S(1)} %bitcast.37), channel_id=1, replica_groups=mesh['x'=4,'z'=8,'y'=4,'c'=2] {'x','y'}, dimensions={0} | all-to-all | bytes 5242880 | tf_op jit(solution)/shard_map/all_to_all | solution.py:322
  175.7 3.2 %collective-permute-start.23 = (bf16[64,1024]{1,0:T(8,128)(2,1)S(1)}, bf16[64,1024]{1,0:T(8,128)(2,1)S(1)}, u32[]{:S(2)}, u32[]{:S(2)}) collective-permute-start(bf16[64,1024]{1,0:T(8,128)(2,1)S(1)} %get-tuple-element.54), channel_id=1, source_target_pairs={{0,56},{8,0},{16,8},{24,16},{32,24},{40,32},{48,40},{56,48},{1,57}... | collective-permute-start | bytes 393224 | tf_op jit(solution)/shard_map/ppermute | solution.py:26
  179.0 3.0 %collective-permute-done.19 = bf16[64,1024]{1,0:T(8,128)(2,1)S(1)} collective-permute-done((bf16[64,1024]{1,0:T(8,128)(2,1)S(1)}, bf16[64,1024]{1,0:T(8,128)(2,1)S(1)}, u32[]{:S(2)}, u32[]{:S(2)}) %collective-permute-start.19) | collective-permute-done | bytes 131104 | tf_op jit(solution)/shard_map/ppermute | solution.py:26
  182.6 3.8 %collective-permute-start.24 = (bf16[64,2048]{1,0:T(8,128)(2,1)S(1)}, bf16[64,2048]{1,0:T(8,128)(2,1)S(1)}, u32[]{:S(2)}, u32[]{:S(2)}) collective-permute-start(bf16[64,2048]{1,0:T(8,128)(2,1)S(1)} %pad_maximum_fusion.1), channel_id=1, source_target_pairs={{0,56},{8,0},{16,8},{24,16},{32,24},{40,32},{48,40},{56,48},{1,57}... | collective-permute-start | bytes 786440 | tf_op jit(solution)/shard_map/ppermute | solution.py:26
  186.5 6.3 %collective-permute-done.24 = bf16[64,2048]{1,0:T(8,128)(2,1)S(1)} collective-permute-done((bf16[64,2048]{1,0:T(8,128)(2,1)S(1)}, bf16[64,2048]{1,0:T(8,128)(2,1)S(1)}, u32[]{:S(2)}, u32[]{:S(2)}) %collective-permute-start.24) | collective-permute-done | bytes 262176 | tf_op jit(solution)/shard_map/ppermute | solution.py:26
  194.4 3.2 %collective-permute-start.25 = (bf16[64,2048]{1,0:T(8,128)(2,1)S(1)}, bf16[64,2048]{1,0:T(8,128)(2,1)S(1)}, u32[]{:S(2)}, u32[]{:S(2)}) collective-permute-start(bf16[64,2048]{1,0:T(8,128)(2,1)S(1)} %get-tuple-element.50), channel_id=1, source_target_pairs={{0,56},{8,0},{16,8},{24,16},{32,24},{40,32},{48,40},{56,48},{1,57}... | collective-permute-start | bytes 786440 | tf_op jit(solution)/shard_map/ppermute | solution.py:26
  197.6 5.7 %collective-permute-done.21 = bf16[64,2048]{1,0:T(8,128)(2,1)S(1)} collective-permute-done((bf16[64,2048]{1,0:T(8,128)(2,1)S(1)}, bf16[64,2048]{1,0:T(8,128)(2,1)S(1)}, u32[]{:S(2)}, u32[]{:S(2)}) %collective-permute-start.21) | collective-permute-done | bytes 262176 | tf_op jit(solution)/shard_map/ppermute | solution.py:26
  203.5 3.2 %collective-permute-start.26 = (bf16[64,2048]{1,0:T(8,128)(2,1)S(1)}, bf16[64,2048]{1,0:T(8,128)(2,1)S(1)}, u32[]{:S(2)}, u32[]{:S(2)}) collective-permute-start(bf16[64,2048]{1,0:T(8,128)(2,1)S(1)} %get-tuple-element.48), channel_id=1, source_target_pairs={{0,56},{8,0},{16,8},{24,16},{32,24},{40,32},{48,40},{56,48},{1,57}... | collective-permute-start | bytes 786440 | tf_op jit(solution)/shard_map/ppermute | solution.py:26
  206.7 4.3 %collective-permute-done.22 = bf16[64,2048]{1,0:T(8,128)(2,1)S(1)} collective-permute-done((bf16[64,2048]{1,0:T(8,128)(2,1)S(1)}, bf16[64,2048]{1,0:T(8,128)(2,1)S(1)}, u32[]{:S(2)}, u32[]{:S(2)}) %collective-permute-start.22) | collective-permute-done | bytes 262176 | tf_op jit(solution)/shard_map/ppermute | solution.py:26
  (106 shorter events, 47.3 us)
Async XLA Ops:
  0.9 18.0 %collective-permute-start = (bf16[2,256,128]{2,1,0:T(8,128)(2,1)S(1)}, bf16[2,256,128]{2,1,0:T(8,128)(2,1)S(1)}, u32[]{:S(2)}, u32[]{:S(2)}) collective-permute-start(bf16[2,256,128]{2,1,0:T(8,128)(2,1)S(1)} %pad_maximum_fusion.2), channel_id=1, source_target_pairs={{0,8},{8,16},{16,24},{24,32},{32,40},{40,48},{48,56},{56,64},{64,7... | collective-permute-start | bytes 393224 | tf_op jit(solution)/shard_map/ppermute | solution.py:35
  6.1 6.4 %collective-permute-start.1 = (f32[1,16,64]{2,1,0:T(8,128)S(1)}, f32[1,16,64]{2,1,0:T(8,128)S(1)}, u32[]{:S(2)}, u32[]{:S(2)}) collective-permute-start(f32[1,16,64]{2,1,0:T(8,128)S(1)} %maximum_bitcast_fusion), channel_id=1, source_target_pairs={{0,8},{8,0},{16,24},{24,16},{32,40},{40,32},{48,56},{56,48},{1,9},... | collective-permute-start | bytes 12296 | tf_op jit(solution)/shard_map/ppermute | solution.py:229
  26.0 10.3 %collective-permute-start.3 = (bf16[256,2048]{1,0:T(8,128)(2,1)}, bf16[256,2048]{1,0:T(8,128)(2,1)}, u32[]{:S(2)}, u32[]{:S(2)}) collective-permute-start(bf16[256,2048]{1,0:T(8,128)(2,1)} %get-tuple-element.26), channel_id=1, source_target_pairs={{0,1},{1,0},{2,3},{3,2},{4,5},{5,4},{6,7},{7,6},{8,9},{9,8},{10,11... | collective-permute-start | bytes 3145736 | tf_op jit(solution)/shard_map/ppermute | solution.py:30
  26.0 64.9 %collective-permute-start.16 = (bf16[1,2048,384]{2,1,0:T(8,128)(2,1)S(1)}, bf16[1,2048,384]{2,1,0:T(8,128)(2,1)}, u32[]{:S(2)}, u32[]{:S(2)}) collective-permute-start(bf16[1,2048,384]{2,1,0:T(8,128)(2,1)S(1)} %copy-done), channel_id=1, source_target_pairs={{0,1},{1,0},{2,3},{3,2},{4,5},{5,4},{6,7},{7,6},{8,9},{9,8},{10,11... | collective-permute-start | bytes 4718600 | tf_op jit(solution)/shard_map/ppermute | solution.py:30
  26.5 64.4 %collective-permute-start.17 = (bf16[1,2048,384]{2,1,0:T(8,128)(2,1)S(1)}, bf16[1,2048,384]{2,1,0:T(8,128)(2,1)}, u32[]{:S(2)}, u32[]{:S(2)}) collective-permute-start(bf16[1,2048,384]{2,1,0:T(8,128)(2,1)S(1)} %copy-done.1), channel_id=1, source_target_pairs={{0,1},{1,0},{2,3},{3,2},{4,5},{5,4},{6,7},{7,6},{8,9},{9,8},{10,11... | collective-permute-start | bytes 4718600 | tf_op jit(solution)/shard_map/ppermute | solution.py:30
  28.5 7.9 %collective-permute-start.4 = (f32[4,16,64]{2,1,0:T(8,128)S(1)}, f32[4,16,64]{2,1,0:T(8,128)S(1)}, u32[]{:S(2)}, u32[]{:S(2)}) collective-permute-start(f32[4,16,64]{2,1,0:T(8,128)S(1)} %pad_maximum_fusion.4), channel_id=1, source_target_pairs={{0,32},{8,40},{16,48},{24,56},{32,0},{40,8},{48,16},{56,24},{1,33}... | collective-permute-start | bytes 49160 | tf_op jit(solution)/shard_map/ppermute | solution.py:229
  40.2 9.6 %collective-permute-start.5 = (bf16[64,2048]{1,0:T(8,128)(2,1)}, bf16[64,2048]{1,0:T(8,128)(2,1)}, u32[]{:S(2)}, u32[]{:S(2)}) collective-permute-start(bf16[64,2048]{1,0:T(8,128)(2,1)} %get-tuple-element.57), channel_id=1, source_target_pairs={{0,2},{2,4},{4,6},{6,0},{1,3},{3,5},{5,7},{7,1},{8,10},{10,12},{12... | collective-permute-start | bytes 786440 | tf_op jit(solution)/shard_map/ppermute | solution.py:26
  41.8 14.3 %collective-permute-start.6 = (bf16[64,2048]{1,0:T(8,128)(2,1)}, bf16[64,2048]{1,0:T(8,128)(2,1)}, u32[]{:S(2)}, u32[]{:S(2)}) collective-permute-start(bf16[64,2048]{1,0:T(8,128)(2,1)} %get-tuple-element.59), channel_id=1, source_target_pairs={{0,4},{2,6},{4,0},{6,2},{1,5},{3,7},{5,1},{7,3},{8,12},{10,14},{12... | collective-permute-start | bytes 786440 | tf_op jit(solution)/shard_map/ppermute | solution.py:26
  44.7 11.4 %collective-permute-start.7 = (bf16[64,2048]{1,0:T(8,128)(2,1)}, bf16[64,2048]{1,0:T(8,128)(2,1)}, u32[]{:S(2)}, u32[]{:S(2)}) collective-permute-start(bf16[64,2048]{1,0:T(8,128)(2,1)} %get-tuple-element.58), channel_id=1, source_target_pairs={{0,6},{2,0},{4,2},{6,4},{1,7},{3,1},{5,3},{7,5},{8,14},{10,8},{12,... | collective-permute-start | bytes 786440 | tf_op jit(solution)/shard_map/ppermute | solution.py:26
  49.9 41.0 %collective-permute-start.18 = (bf16[1,384,2048]{2,1,0:T(8,128)(2,1)}, bf16[1,384,2048]{2,1,0:T(8,128)(2,1)}, u32[]{:S(2)}, u32[]{:S(2)}) collective-permute-start(bf16[1,384,2048]{2,1,0:T(8,128)(2,1)} %d0), channel_id=1, source_target_pairs={{0,1},{1,0},{2,3},{3,2},{4,5},{5,4},{6,7},{7,6},{8,9},{9,8},{10,11... | collective-permute-start | bytes 4718600 | tf_op jit(solution)/shard_map/ppermute | solution.py:30
  59.4 9.0 %collective-permute-start.8 = (bf16[64,2048]{1,0:T(8,128)(2,1)}, bf16[64,2048]{1,0:T(8,128)(2,1)}, u32[]{:S(2)}, u32[]{:S(2)}) collective-permute-start(bf16[64,2048]{1,0:T(8,128)(2,1)} %get-tuple-element.42), channel_id=1, source_target_pairs={{0,8},{8,16},{16,24},{24,32},{32,40},{40,48},{48,56},{56,0},{1,9},... | collective-permute-start | bytes 786440 | tf_op jit(solution)/shard_map/ppermute | solution.py:26
  59.7 9.4 %collective-permute-start.9 = (bf16[64,2048]{1,0:T(8,128)(2,1)}, bf16[64,2048]{1,0:T(8,128)(2,1)S(1)}, u32[]{:S(2)}, u32[]{:S(2)}) collective-permute-start(bf16[64,2048]{1,0:T(8,128)(2,1)} %get-tuple-element.42), channel_id=1, source_target_pairs={{0,56},{8,0},{16,8},{24,16},{32,24},{40,32},{48,40},{56,48},{1,57}... | collective-permute-start | bytes 786440 | tf_op jit(solution)/shard_map/ppermute | solution.py:26
  68.4 8.0 %collective-permute-start.10 = (bf16[64,2048]{1,0:T(8,128)(2,1)}, bf16[64,2048]{1,0:T(8,128)(2,1)S(1)}, u32[]{:S(2)}, u32[]{:S(2)}) collective-permute-start(bf16[64,2048]{1,0:T(8,128)(2,1)} %collective-permute-done.8), channel_id=1, source_target_pairs={{0,8},{8,16},{16,24},{24,32},{32,40},{40,48},{48,56},{56,0},{1,9},... | collective-permute-start | bytes 786440 | tf_op jit(solution)/shard_map/ppermute | solution.py:26
  69.1 7.2 %collective-permute-start.11 = (bf16[64,2048]{1,0:T(8,128)(2,1)S(1)}, bf16[64,2048]{1,0:T(8,128)(2,1)S(1)}, u32[]{:S(2)}, u32[]{:S(2)}) collective-permute-start(bf16[64,2048]{1,0:T(8,128)(2,1)S(1)} %collective-permute-done.9), channel_id=1, source_target_pairs={{0,56},{8,0},{16,8},{24,16},{32,24},{40,32},{48,40},{56,48},{1,57}... | collective-permute-start | bytes 786440 | tf_op jit(solution)/shard_map/ppermute | solution.py:26
  76.3 7.6 %collective-permute-start.12 = (bf16[64,2048]{1,0:T(8,128)(2,1)S(1)}, bf16[64,2048]{1,0:T(8,128)(2,1)S(1)}, u32[]{:S(2)}, u32[]{:S(2)}) collective-permute-start(bf16[64,2048]{1,0:T(8,128)(2,1)S(1)} %collective-permute-done.10), channel_id=1, source_target_pairs={{0,8},{8,16},{16,24},{24,32},{32,40},{40,48},{48,56},{56,0},{1,9},... | collective-permute-start | bytes 786440 | tf_op jit(solution)/shard_map/ppermute | solution.py:26
  76.3 7.7 %collective-permute-start.13 = (bf16[64,2048]{1,0:T(8,128)(2,1)S(1)}, bf16[64,2048]{1,0:T(8,128)(2,1)S(1)}, u32[]{:S(2)}, u32[]{:S(2)}) collective-permute-start(bf16[64,2048]{1,0:T(8,128)(2,1)S(1)} %collective-permute-done.11), channel_id=1, source_target_pairs={{0,56},{8,0},{16,8},{24,16},{32,24},{40,32},{48,40},{56,48},{1,57}... | collective-permute-start | bytes 786440 | tf_op jit(solution)/shard_map/ppermute | solution.py:26
  175.4 6.5 %collective-permute-start.19 = (bf16[64,1024]{1,0:T(8,128)(2,1)S(1)}, bf16[64,1024]{1,0:T(8,128)(2,1)S(1)}, u32[]{:S(2)}, u32[]{:S(2)}) collective-permute-start(bf16[64,1024]{1,0:T(8,128)(2,1)S(1)} %get-tuple-element.53), channel_id=1, source_target_pairs={{0,8},{8,16},{16,24},{24,32},{32,40},{40,48},{48,56},{56,0},{1,9},... | collective-permute-start | bytes 393224 | tf_op jit(solution)/shard_map/ppermute | solution.py:26
  175.7 6.8 %collective-permute-start.23 = (bf16[64,1024]{1,0:T(8,128)(2,1)S(1)}, bf16[64,1024]{1,0:T(8,128)(2,1)S(1)}, u32[]{:S(2)}, u32[]{:S(2)}) collective-permute-start(bf16[64,1024]{1,0:T(8,128)(2,1)S(1)} %get-tuple-element.54), channel_id=1, source_target_pairs={{0,56},{8,0},{16,8},{24,16},{32,24},{40,32},{48,40},{56,48},{1,57}... | collective-permute-start | bytes 393224 | tf_op jit(solution)/shard_map/ppermute | solution.py:26
  182.6 10.1 %collective-permute-start.24 = (bf16[64,2048]{1,0:T(8,128)(2,1)S(1)}, bf16[64,2048]{1,0:T(8,128)(2,1)S(1)}, u32[]{:S(2)}, u32[]{:S(2)}) collective-permute-start(bf16[64,2048]{1,0:T(8,128)(2,1)S(1)} %pad_maximum_fusion.1), channel_id=1, source_target_pairs={{0,56},{8,0},{16,8},{24,16},{32,24},{40,32},{48,40},{56,48},{1,57}... | collective-permute-start | bytes 786440 | tf_op jit(solution)/shard_map/ppermute | solution.py:26
  186.4 7.7 %collective-permute-start.20 = (bf16[64,2048]{1,0:T(8,128)(2,1)S(1)}, bf16[64,2048]{1,0:T(8,128)(2,1)S(1)}, u32[]{:S(2)}, u32[]{:S(2)}) collective-permute-start(bf16[64,2048]{1,0:T(8,128)(2,1)S(1)} %pad_maximum_fusion), channel_id=1, source_target_pairs={{0,8},{8,16},{16,24},{24,32},{32,40},{40,48},{48,56},{56,0},{1,9},... | collective-permute-start | bytes 786440 | tf_op jit(solution)/shard_map/ppermute | solution.py:26
  194.3 9.0 %collective-permute-start.21 = (bf16[64,2048]{1,0:T(8,128)(2,1)S(1)}, bf16[64,2048]{1,0:T(8,128)(2,1)S(1)}, u32[]{:S(2)}, u32[]{:S(2)}) collective-permute-start(bf16[64,2048]{1,0:T(8,128)(2,1)S(1)} %get-tuple-element.49), channel_id=1, source_target_pairs={{0,8},{8,16},{16,24},{24,32},{32,40},{40,48},{48,56},{56,0},{1,9},... | collective-permute-start | bytes 786440 | tf_op jit(solution)/shard_map/ppermute | solution.py:26
  194.4 8.9 %collective-permute-start.25 = (bf16[64,2048]{1,0:T(8,128)(2,1)S(1)}, bf16[64,2048]{1,0:T(8,128)(2,1)S(1)}, u32[]{:S(2)}, u32[]{:S(2)}) collective-permute-start(bf16[64,2048]{1,0:T(8,128)(2,1)S(1)} %get-tuple-element.50), channel_id=1, source_target_pairs={{0,56},{8,0},{16,8},{24,16},{32,24},{40,32},{48,40},{56,48},{1,57}... | collective-permute-start | bytes 786440 | tf_op jit(solution)/shard_map/ppermute | solution.py:26
  203.4 7.7 %collective-permute-start.22 = (bf16[64,2048]{1,0:T(8,128)(2,1)S(1)}, bf16[64,2048]{1,0:T(8,128)(2,1)S(1)}, u32[]{:S(2)}, u32[]{:S(2)}) collective-permute-start(bf16[64,2048]{1,0:T(8,128)(2,1)S(1)} %get-tuple-element.47), channel_id=1, source_target_pairs={{0,8},{8,16},{16,24},{24,32},{32,40},{40,48},{48,56},{56,0},{1,9},... | collective-permute-start | bytes 786440 | tf_op jit(solution)/shard_map/ppermute | solution.py:26
  203.5 7.6 %collective-permute-start.26 = (bf16[64,2048]{1,0:T(8,128)(2,1)S(1)}, bf16[64,2048]{1,0:T(8,128)(2,1)S(1)}, u32[]{:S(2)}, u32[]{:S(2)}) collective-permute-start(bf16[64,2048]{1,0:T(8,128)(2,1)S(1)} %get-tuple-element.48), channel_id=1, source_target_pairs={{0,56},{8,0},{16,8},{24,16},{32,24},{40,32},{48,40},{56,48},{1,57}... | collective-permute-start | bytes 786440 | tf_op jit(solution)/shard_map/ppermute | solution.py:26
  (14 other events, 178.1 us)

commit v4 on v3

--- a/solution.py
+++ b/solution.py
@@ -12,6 +12,8 @@
 NX, NZ, NY, NC = 4, 8, 4, 2
 ROWS = 64
 CAP = 5
+TOP = 8
+META = 128
 PLANE = NX * NY
 SLOTS = NZ * CAP
 
@@ -70,9 +72,7 @@
     )
 
 
-def early_body(
-    where, q_ref, tails, kb, vb, len_ref, late_ref, w_ref, theirs_ref, mine_ref, held, picked
-):
+def early_body(where, q_ref, tails, kb, vb, len_ref, late_ref, theirs_ref, mine_ref, held):
     rows = q_ref.shape[0]
 
     def store(at, value):
@@ -88,23 +88,12 @@
         here = pl.ds(pl.multiple_of(block + c * ROWS, ROWS), ROWS)
         there = pl.ds(pl.multiple_of(block + (1 - c) * ROWS, ROWS), ROWS)
         mine_ref[k * ROWS : (k + 1) * ROWS] = held[here]
-        picked[k * ROWS : (k + 1) * ROWS] = held[there]
-    tile = 512
-
-    def column(i, carry):
-        at = pl.ds(pl.multiple_of(i * tile, tile), tile)
-        theirs_ref[:, at] = jnp.dot(
-            picked[...], w_ref[:, at], preferred_element_type=F32
-        ).astype(BF)
-        return carry
-
-    lax.fori_loop(0, w_ref.shape[1] // tile, column, 0)
-
-
-def attend(queries, key_rows, value_rows, doc_lengths, out_weight, held):
+        theirs_ref[k * ROWS : (k + 1) * ROWS] = held[there]
+
+
+def attend(queries, key_rows, value_rows, doc_lengths):
     tok_rows, width = queries.shape
     half = tok_rows // 2
-    out_width = out_weight.shape[1]
     y, c = lax.axis_index("y"), lax.axis_index("c")
     where = jnp.stack([lax.axis_index(("x", "z")) * tok_rows, y, c]).astype(jnp.int32)
     lengths = doc_lengths.reshape(1, -1)
@@ -124,7 +113,7 @@
         return pl.BlockSpec(shape, lambda g, where: (0,) * len(shape))
 
     lens = all_of(1, doc_lengths.shape[0])
-    params = pltpu.CompilerParams(vmem_limit_bytes=56 * 1024 * 1024)
+    params = pltpu.CompilerParams(vmem_limit_bytes=57 * 1024 * 1024)
     scores = tok_rows * tok_rows * (width // HD) // 2
     late = pl.pallas_call(
         late_body,
@@ -147,11 +136,10 @@
             flops=16 * scores * HD, bytes_accessed=6 * half * width, transcendentals=8 * scores
         ),
     )(where, queries, key_rows, key_rows, value_rows, value_rows, lengths)
-    late, held = lax.optimization_barrier((late, double(held, 1)))
-    theirs, mine = pl.pallas_call(
+    return pl.pallas_call(
         early_body,
         out_shape=(
-            jax.ShapeDtypeStruct((half, out_width), BF),
+            jax.ShapeDtypeStruct((half, width), BF),
             jax.ShapeDtypeStruct((half, width), BF),
         ),
         grid_spec=pltpu.PrefetchScalarGridSpec(
@@ -164,46 +152,37 @@
                 part(0),
                 lens,
                 all_of(half, width),
-                all_of(*out_weight.shape),
             ],
-            out_specs=(all_of(half, out_width), all_of(half, width)),
-            scratch_shapes=[pltpu.VMEM((tok_rows, width), BF), pltpu.VMEM((half, width), BF)],
+            out_specs=(all_of(half, width), all_of(half, width)),
+            scratch_shapes=[pltpu.VMEM((tok_rows, width), BF)],
         ),
         compiler_params=params,
         cost_estimate=pl.CostEstimate(
-            flops=16 * scores * HD + 2 * half * width * out_width,
-            bytes_accessed=6 * half * width + 2 * width * out_width,
-            transcendentals=8 * scores,
-        ),
-    )(where, queries, tails, key_rows, value_rows, lengths, late, out_weight)
-    theirs, held = lax.optimization_barrier((theirs, double(held, 2)))
-    return theirs, mine, held
-
-
-def project(theirs, attn_mine, out_weight, held):
-    arrived, held = lax.optimization_barrier((swap_cores(theirs), double(held, 4)))
+            flops=16 * scores * HD, bytes_accessed=8 * half * width, transcendentals=8 * scores
+        ),
+    )(where, queries, tails, key_rows, value_rows, lengths, late)
+
+
+def project(attn_theirs, attn_mine, out_weight):
+    theirs = jnp.dot(attn_theirs, out_weight, preferred_element_type=F32).astype(BF)
+    arrived = swap_cores(theirs)
     mine = lax.optimization_barrier(
         jnp.dot(attn_mine, out_weight, preferred_element_type=F32)
     )
     both = (mine + arrived.astype(F32)).reshape(NY, ROWS, out_weight.shape[1])
     sent = both.astype(BF)
     moved = [shift(sent[k], "y", NY, k) for k in range(1, NY)]
-    return both[0] + sum(block.astype(F32) for block in moved), held
-
-
-def ring_gather(own):
-    width = own.shape[1]
-    half = width // 2
+    return both[0] + sum(block.astype(F32) for block in moved)
+
+
+def ring_gather(own, half):
     right = left = own
     blocks = [own]
     for _ in range(3):
         right = shift(right, "z", NZ, 1)
         left = shift(left, "z", NZ, -1)
         blocks += [right, left]
-    a = shift(right[:, :half], "z", NZ, 1)
-    b = shift(left[:, half:], "z", NZ, -1)
-    blocks.append(jnp.concatenate([a, b], axis=1))
-    return jnp.concatenate(blocks, axis=0)
+    return blocks + [shift(right[:, :half], "z", NZ, 1), shift(left[:, half:], "z", NZ, -1)]
 
 
 def ring_sum(blocks):
@@ -216,42 +195,91 @@
     b = shift(blocks[4][:, half:], "z", NZ, -1)
     right = jnp.concatenate([add(blocks[3][:, :half], a), blocks[3][:, half:]], axis=1)
     left = jnp.concatenate([blocks[-3][:, :half], add(blocks[-3][:, half:], b)], axis=1)
-    right, left = lax.optimization_barrier(right), lax.optimization_barrier(left)
     for step in (2, 1):
-        right = lax.optimization_barrier(add(shift(right, "z", NZ, 1), blocks[step]))
-        left = lax.optimization_barrier(add(shift(left, "z", NZ, -1), blocks[-step]))
+        right = add(shift(right, "z", NZ, 1), blocks[step])
+        own = lax.optimization_barrier((blocks[-step], right))[0]
+        left = add(shift(left, "z", NZ, -1), own)
     right = shift(right, "z", NZ, 1)
     left = shift(left, "z", NZ, -1)
     return blocks[0].astype(F32) + right.astype(F32) + left.astype(F32)
 
 
-def double(held, bit):
-    other = lax.ppermute(held, "z", [(i, i ^ bit) for i in range(NZ)])
-    return jnp.concatenate([held, other], axis=0)
-
-
-def slots_of(held):
-    z = lax.axis_index("z")
-    order = z ^ ((z + jnp.array(RING, jnp.int32)) % NZ)
-    everywhere = jnp.take(held, order, axis=0)
-    top = held.shape[1] // 2
-    ids = everywhere[:, :top].astype(jnp.int32)
-    gates = everywhere[:, top:]
-    place = jnp.arange(PLANE, dtype=jnp.int32)
-    experts = (place // NY * NZ + z) * NY + place % NY
-    match = ids[None] == experts[:, None, None, None]
-    named = jnp.any(match, axis=2)
-    gate = jnp.sum(jnp.where(match, gates[None], 0.0), axis=2)
-    before = jnp.triu(jnp.ones((ROWS, ROWS), BF), 1)
+def dispatch_body(z_ref, *refs):
+    blocks, (out_ref, weight_ref, tokens, meta, one_hot) = refs[:-5], refs[-5:]
+    width = tokens.shape[1]
+    count = tokens.shape[0]
+    cut = blocks[-2].shape[1]
+    for i, block in enumerate(blocks[:-2]):
+        at = slice(i * ROWS, (i + 1) * ROWS)
+        tokens[at] = block[:, :width]
+        meta[at] = block[:, width:]
+    at = slice(count - ROWS, count)
+    tokens[at, :cut] = blocks[-2][...]
+    tokens[at, cut:] = blocks[-1][:, : width - cut]
+    meta[at] = blocks[-1][:, width - cut :]
+
+    turned = meta[...].astype(F32).T
+    ids, gates = turned[:TOP], turned[TOP : 2 * TOP]
+    named, gate = [], []
+    for place in range(PLANE):
+        expert = (place // NY * NZ + z_ref[0]) * NY + place % NY
+        match = ids == expert.astype(F32)
+        named.append(jnp.max(jnp.where(match, 1.0, 0.0), axis=0, keepdims=True))
+        gate.append(jnp.sum(jnp.where(match, gates, 0.0), axis=0, keepdims=True))
+    first = lax.broadcasted_iota(jnp.int32, (count, count), 0)
+    second = lax.broadcasted_iota(jnp.int32, (count, count), 1)
+    before = (first < second) & (first // ROWS == second // ROWS)
+    all_named = jnp.concatenate(named, axis=0)
     rank = jnp.dot(
-        named.astype(BF).reshape(PLANE * NZ, ROWS), before, preferred_element_type=F32
-    ).reshape(PLANE, NZ, ROWS)
-    slot = rank.astype(jnp.int32) + jnp.arange(NZ, dtype=jnp.int32)[None, :, None] * CAP
-    slot = jnp.where(named, slot, -1).reshape(PLANE, 1, NZ * ROWS)
-    hit = slot == jnp.arange(SLOTS, dtype=jnp.int32)[None, :, None]
-    one_hot = hit.astype(BF).reshape(PLANE * SLOTS, NZ * ROWS)
-    weighted = jnp.where(hit, gate.reshape(PLANE, 1, NZ * ROWS), 0.0).astype(BF)
-    return one_hot, weighted.reshape(PLANE * SLOTS, NZ * ROWS)
+        all_named.astype(BF), jnp.where(before, 1.0, 0.0).astype(BF), preferred_element_type=F32
+    )
+    block_start = lax.broadcasted_iota(jnp.int32, (1, count), 1) // ROWS * CAP
+    slot = jnp.where(all_named > 0.0, rank + block_start.astype(F32), -1.0)
+    slots = lax.broadcasted_iota(jnp.int32, (SLOTS, 1), 0).astype(F32)
+    for pair in range(PLANE // 2):
+        hits, weights = [], []
+        for place in (2 * pair, 2 * pair + 1):
+            hit = slot[place : place + 1] == slots
+            hits.append(jnp.where(hit, 1.0, 0.0))
+            weights.append(jnp.where(hit, gate[place], 0.0))
+        at = slice(2 * pair * SLOTS, (2 * pair + 2) * SLOTS)
+        one_hot[at] = jnp.concatenate(hits, axis=0).astype(BF)
+        weight_ref[at] = jnp.concatenate(weights, axis=0).astype(BF)
+    tile = 256
+
+    def column(i, carry):
+        at = pl.ds(pl.multiple_of(i * tile, tile), tile)
+        out_ref[:, at] = jnp.dot(
+            one_hot[...], tokens[:, at], preferred_element_type=F32
+        ).astype(BF)
+        return carry
+
+    lax.fori_loop(0, width // tile, column, 0)
+
+
+def dispatch(blocks, width):
+    count = NZ * ROWS
+    whole = pl.BlockSpec(memory_space=pltpu.VMEM)
+    return pl.pallas_call(
+        dispatch_body,
+        out_shape=(
+            jax.ShapeDtypeStruct((PLANE * SLOTS, width), BF),
+            jax.ShapeDtypeStruct((PLANE * SLOTS, count), BF),
+        ),
+        in_specs=[pl.BlockSpec(memory_space=pltpu.SMEM)] + [whole] * len(blocks),
+        out_specs=(whole, whole),
+        scratch_shapes=[
+            pltpu.VMEM((count, width), BF),
+            pltpu.VMEM((count, META), BF),
+            pltpu.VMEM((PLANE * SLOTS, count), BF),
+        ],
+        compiler_params=pltpu.CompilerParams(vmem_limit_bytes=24 * 1024 * 1024),
+        cost_estimate=pl.CostEstimate(
+            flops=2 * PLANE * SLOTS * count * width,
+            bytes_accessed=4 * count * width,
+            transcendentals=0,
+        ),
+    )(lax.axis_index("z").astype(jnp.int32).reshape(1), *blocks)
 
 
 def expert_body(rows_ref, g0, g1, u0, u1, d0, d1, out_ref, g_all, u_all, d_all, hidden, sems):
@@ -340,20 +368,24 @@
     w_down,
 ):
     pairs = [(w, swap_cores(w)) for w in (w_gate, w_up, w_down)]
-    held = jnp.concatenate([expert_ids.T.astype(F32), gate_weights.T], axis=0)[None]
-    theirs, attn_mine, held = attend(
-        queries, key_rows, value_rows, doc_lengths, out_weight, held
-    )
-    projected, held = project(theirs, attn_mine, out_weight, held)
-    mid = residual_in.astype(F32) + projected
-    one_hot, weighted = slots_of(held)
+    attn_theirs, attn_mine = attend(queries, key_rows, value_rows, doc_lengths)
+    mid = residual_in.astype(F32) + project(attn_theirs, attn_mine, out_weight)
     spread = jnp.mean(mid * mid, axis=1, keepdims=True)
     normed = (mid * lax.rsqrt(spread + 1e-06) * norm_gain[None, :]).astype(BF)
 
-    tokens, one_hot, weighted, pairs = lax.optimization_barrier(
-        (ring_gather(normed), one_hot, weighted, pairs)
-    )
-    outgoing = jnp.dot(one_hot, tokens, preferred_element_type=F32).astype(BF)
+    rows, width = normed.shape
+    meta = jnp.concatenate(
+        [
+            expert_ids.astype(BF),
+            gate_weights.astype(BF),
+            jnp.zeros((rows, META - 2 * TOP), BF),
+        ],
+        axis=1,
+    )
+    blocks, pairs = lax.optimization_barrier(
+        (ring_gather(jnp.concatenate([normed, meta], axis=1), width // 2), pairs)
+    )
+    outgoing, weighted = dispatch(blocks, width)
     mine = exchange(outgoing)
     pair_out = expert_rows(mine, *pairs)
     returned = exchange(pair_out)

time: 213 us -> 199 us (0.934); the launches traced: 212 us -> 196 us
  starting transfers between devices: 47.3 us -> 34.7 us
  waiting for transfers between devices: 44.2 us -> 56 us
  other arithmetic: 13.3 us -> 5.1 us
  local copies, waits for them, and re-layouts: 9.4 us -> 3.65 us
  matrix products: 7.47 us -> 4.26 us
  Pallas kernels: 19.1 us -> 21.3 us
    ppermute x19, waiting for transfers between devices: 40.9 us -> 51.3 us  [shift(): lax.ppermute(value, axis, [(i, (i + by) % size) for i in range(size)])]
    ppermute x3 -> x0, starting transfers between devices: 10.3 us -> none  [double(): other = lax.ppermute(held, 'z', [(i, i ^ bit) for i in range(NZ)])]
    unnamed x28 -> x18, local copies, waits for them, and re-layouts: 6.7 us -> 1.39 us
    ppermute x3 -> x0, waiting for transfers between devices: 3.35 us -> none  [double(): other = lax.ppermute(held, 'z', [(i, i ^ bit) for i in range(NZ)])]
    ppermute x1, waiting for transfers between devices: 0.01 us -> 2.84 us  [from_behind(): lax.ppermute(value, ('x', 'z'), [(i, i + 1) for i in range(devices - 1)])]
    ppermute x19, starting transfers between devices: 32.5 us -> 30.3 us  [shift(): lax.ppermute(value, axis, [(i, (i + by) % size) for i in range(size)])]
    pallas_call x1 -> x2, Pallas kernels: 6.49 us -> 7.52 us  [the longest x1 4.16 us: attend(): pl.pallas_call(early_body, out_shape=(jax.ShapeDtypeStruct((half, width),...]
  transfers between devices with their start and end apart: 27 -> 24, of which waited for: 15 -> 14; matrix products, arithmetic and copies ran while one was open for 10% -> 2% of each run, Pallas kernels for 2% -> 2%
where the time goes in v4:
time: 199 us; the launch traced here: 196 us
  blocking collectives  70.3 us (35%)
  waiting for transfers between devices  56 us (28%)
  starting transfers between devices  34.7 us (17%)
  Pallas kernels  21.3 us (11%)
  other arithmetic  5.1 us (3%)
  matrix products  4.26 us (2%)
  local copies, waits for them, and re-layouts  3.65 us (2%)
    all_to_all x2, blocking collectives, exchange(): lax.all_to_all(rows.reshape(PLANE, SLOTS, width), ('x', 'y'), split_axis=...  70.3 us
    ppermute x19, waiting for transfers between devices, shift(): lax.ppermute(value, axis, [(i, (i + by) % size) for i in range(size)])  51.3 us
    ppermute x19, starting transfers between devices, shift(): lax.ppermute(value, axis, [(i, (i + by) % size) for i in range(size)])  30.3 us
    pallas_call x1, Pallas kernels, expert_rows(): pl.pallas_call(expert_body, out_shape=jax.ShapeDtypeStruct((count, width)...  9.88 us
    pallas_call x1, Pallas kernels, attend(): pl.pallas_call(early_body, out_shape=(jax.ShapeDtypeStruct((half, width),...  4.16 us
  transfers between devices with their start and end apart: 24, of which 14 were waited for; matrix products, arithmetic and copies ran while one was open for 2% of the time, Pallas kernels for 2%

profile of v4, /device:TPU:2, one launch (start us, length us, event | category | flops | bytes accessed | tf_op | source)
XLA Modules:
  0.0 195.7 jit_solution(3744207847820977578)
XLA Ops:
  1.1 3.8 %collective-permute-start = (bf16[2,256,128]{2,1,0:T(8,128)(2,1)S(1)}, bf16[2,256,128]{2,1,0:T(8,128)(2,1)S(1)}, u32[]{:S(2)}, u32[]{:S(2)}) collective-permute-start(bf16[2,256,128]{2,1,0:T(8,128)(2,1)S(1)} %pad_maximum_fusion.2), channel_id=1, source_target_pairs={{0,8},{8,16},{16,24},{24,32},{32,40},{40,48},{48,56},{56,64},{64,7... | collective-permute-start | bytes 393224 | tf_op jit(solution)/shard_map/ppermute | solution.py:37
  5.5 3.9 %shard_map.118.late_ref = bf16[256,512]{1,0:T(8,128)(2,1)} custom-call(s32[3]{0:T(128)} %pad_add_fusion.where, bf16[512,512]{1,0:T(8,128)(2,1)} %q_ref.3, bf16[512,512]{1,0:T(8,128)(2,1)} %kb.3, bf16[512,512]{1,0:T(8,128)(2,1)} %kb.3, bf16[512,512]{1,0:T(8,128)(2,1)} %vb.3, bf16[512,512]{1,0:T(8,128)(2,1)} %vb.3, s32[1,128]{1,0:T(1,128)} %bitcast.23), custom_call_target="tpu_custom_call" | custom-call | flops 1073741824 | bytes 786432 | tf_op jit(solution)/shard_map/pallas_call | solution.py:118
  9.4 2.8 %collective-permute-done.tails = bf16[2,256,128]{2,1,0:T(8,128)(2,1)S(1)} collective-permute-done((bf16[2,256,128]{2,1,0:T(8,128)(2,1)S(1)}, bf16[2,256,128]{2,1,0:T(8,128)(2,1)S(1)}, u32[]{:S(2)}, u32[]{:S(2)}) %collective-permute-start) | collective-permute-done | bytes 131104 | tf_op jit(solution)/shard_map/ppermute | solution.py:37
  12.9 4.2 %shard_map.119 = (bf16[256,512]{1,0:T(8,128)(2,1)}, bf16[256,512]{1,0:T(8,128)(2,1)}) custom-call(s32[3]{0:T(128)} %pad_add_fusion.where, bf16[512,512]{1,0:T(8,128)(2,1)} %q_ref.3, bf16[2,256,128]{2,1,0:T(8,128)(2,1)} %copy-done.8, bf16[512,512]{1,0:T(8,128)(2,1)} %kb.3, bf16[512,512]{1,0:T(8,128)(2,1)} %vb.3, s32[1,128]{1,0:T(1,128)} %bitcast.24, ...), custom_call_target="tpu_custom_call" | custom-call | flops 1073741824 | bytes 1048576 | tf_op jit(solution)/shard_map/pallas_call | solution.py:139
  30.1 3.9 %collective-permute-done.2 = bf16[64,2048]{1,0:T(8,128)(2,1)S(1)} collective-permute-done((bf16[64,2048]{1,0:T(8,128)(2,1)}, bf16[64,2048]{1,0:T(8,128)(2,1)S(1)}, u32[]{:S(2)}, u32[]{:S(2)}) %collective-permute-start.2) | collective-permute-done | bytes 262176 | tf_op jit(solution)/shard_map/ppermute | solution.py:28
  35.1 5.6 %collective-permute-done.3 = bf16[64,2048]{1,0:T(8,128)(2,1)S(1)} collective-permute-done((bf16[64,2048]{1,0:T(8,128)(2,1)S(1)}, bf16[64,2048]{1,0:T(8,128)(2,1)S(1)}, u32[]{:S(2)}, u32[]{:S(2)}) %collective-permute-start.3) | collective-permute-done | bytes 262176 | tf_op jit(solution)/shard_map/ppermute | solution.py:28
  45.2 5.8 %collective-permute-done.6.refs_2_ = bf16[64,2176]{1,0:T(8,128)(2,1)S(1)} collective-permute-done((bf16[64,2176]{1,0:T(8,128)(2,1)S(1)}, bf16[64,2176]{1,0:T(8,128)(2,1)S(1)}, u32[]{:S(2)}, u32[]{:S(2)}) %collective-permute-start.6) | collective-permute-done | bytes 278560 | tf_op jit(solution)/shard_map/ppermute | solution.py:28
  51.1 3.0 %collective-permute-start.8 = (bf16[64,2176]{1,0:T(8,128)(2,1)S(1)}, bf16[64,2176]{1,0:T(8,128)(2,1)S(1)}, u32[]{:S(2)}, u32[]{:S(2)}) collective-permute-start(bf16[64,2176]{1,0:T(8,128)(2,1)S(1)} %collective-permute-done.6.refs_2_), channel_id=1, source_target_pairs={{0,56},{8,0},{16,8},{24,16},{32,24},{40,32},{48,40},{56,48},{1,57}... | collective-permute-start | bytes 835592 | tf_op jit(solution)/shard_map/ppermute | solution.py:28
  54.1 4.5 %collective-permute-done.8.refs_4_ = bf16[64,2176]{1,0:T(8,128)(2,1)S(1)} collective-permute-done((bf16[64,2176]{1,0:T(8,128)(2,1)S(1)}, bf16[64,2176]{1,0:T(8,128)(2,1)S(1)}, u32[]{:S(2)}, u32[]{:S(2)}) %collective-permute-start.8) | collective-permute-done | bytes 278560 | tf_op jit(solution)/shard_map/ppermute | solution.py:28
  58.5 3.7 %collective-permute-start.10 = (bf16[64,2176]{1,0:T(8,128)(2,1)S(1)}, bf16[64,2176]{1,0:T(8,128)(2,1)S(1)}, u32[]{:S(2)}, u32[]{:S(2)}) collective-permute-start(bf16[64,2176]{1,0:T(8,128)(2,1)S(1)} %collective-permute-done.8.refs_4_), channel_id=1, source_target_pairs={{0,56},{8,0},{16,8},{24,16},{32,24},{40,32},{48,40},{56,48},{1,57}... | collective-permute-start | bytes 835592 | tf_op jit(solution)/shard_map/ppermute | solution.py:28
  62.2 4.1 %collective-permute-done.10.refs_6_ = bf16[64,2176]{1,0:T(8,128)(2,1)S(1)} collective-permute-done((bf16[64,2176]{1,0:T(8,128)(2,1)S(1)}, bf16[64,2176]{1,0:T(8,128)(2,1)S(1)}, u32[]{:S(2)}, u32[]{:S(2)}) %collective-permute-start.10) | collective-permute-done | bytes 278560 | tf_op jit(solution)/shard_map/ppermute | solution.py:28
  66.3 3.8 %collective-permute-start.12 = (bf16[64,1152]{1,0:T(8,128)(2,1)S(1)}, bf16[64,1152]{1,0:T(8,128)(2,1)S(1)}, u32[]{:S(2)}, u32[]{:S(2)}) collective-permute-start(bf16[64,1152]{1,0:T(8,128)(2,1)S(1)} %slice.94), channel_id=1, source_target_pairs={{0,56},{8,0},{16,8},{24,16},{32,24},{40,32},{48,40},{56,48},{1,57}... | collective-permute-start | bytes 442376 | tf_op jit(solution)/shard_map/ppermute | solution.py:28
  70.2 6.1 %collective-permute-done.11.refs_7_ = bf16[64,1024]{1,0:T(8,128)(2,1)S(1)} collective-permute-done((bf16[64,1024]{1,0:T(8,128)(2,1)S(1)}, bf16[64,1024]{1,0:T(8,128)(2,1)S(1)}, u32[]{:S(2)}, u32[]{:S(2)}) %collective-permute-start.11) | collective-permute-done | bytes 131104 | tf_op jit(solution)/shard_map/ppermute | solution.py:28
  76.3 3.4 %shard_map.120 = (bf16[640,2048]{1,0:T(8,128)(2,1)S(1)}, bf16[640,512]{1,0:T(8,128)(2,1)S(1)}) custom-call(s32[1]{0:T(128)} %bitcast.6.z_ref, bf16[64,2176]{1,0:T(8,128)(2,1)S(1)} %concatenate.9.refs_0_, bf16[64,2176]{1,0:T(8,128)(2,1)S(1)} %collective-permute-done.5.refs_1_, bf16[64,2176]{1,0:T(8,128)(2,1)S(1)} %collective-permute-done.6.refs_2_, ...), custom_call_target="tpu_custom_call" | custom-call | flops 1342177280 | bytes 4194304 | tf_op jit(solution)/shard_map/pallas_call | solution.py:263
  79.7 36.7 %all_to_all.10 = bf16[16,40,2048]{2,1,0:T(8,128)(2,1)S(1)} all-to-all(bf16[16,40,2048]{2,1,0:T(8,128)(2,1)S(1)} %bitcast.19), channel_id=1, replica_groups=mesh['x'=4,'z'=8,'y'=4,'c'=2] {'x','y'}, dimensions={0} | all-to-all | bytes 5242880 | tf_op jit(solution)/shard_map/all_to_all | solution.py:350
  116.5 9.9 %shard_map.121 = bf16[640,2048]{1,0:T(8,128)(2,1)S(1)} custom-call(bf16[640,2048]{1,0:T(8,128)(2,1)S(1)} %bitcast.20, bf16[1,2048,384]{2,1,0:T(8,128)(2,1)} %g0, bf16[1,2048,384]{2,1,0:T(8,128)(2,1)} %collective-permute-done.13.g1, bf16[1,2048,384]{2,1,0:T(8,128)(2,1)} %u0, bf16[1,2048,384]{2,1,0:T(8,128)(2,1)} %collective-permute-done.14.u1, ...), custom_call_target="tpu_custom_call" | custom-call | flops 6039797760 | bytes 14680064 | tf_op jit(solution)/shard_map/pallas_call | solution.py:327
  126.3 33.6 %all_to_all.11 = bf16[16,40,2048]{2,1,0:T(8,128)(2,1)S(1)} all-to-all(bf16[16,40,2048]{2,1,0:T(8,128)(2,1)S(1)} %bitcast.21), channel_id=1, replica_groups=mesh['x'=4,'z'=8,'y'=4,'c'=2] {'x','y'}, dimensions={0} | all-to-all | bytes 5242880 | tf_op jit(solution)/shard_map/all_to_all | solution.py:350
  163.9 4.3 %collective-permute-done.20 = bf16[64,1024]{1,0:T(8,128)(2,1)S(1)} collective-permute-done((bf16[64,1024]{1,0:T(8,128)(2,1)S(1)}, bf16[64,1024]{1,0:T(8,128)(2,1)S(1)}, u32[]{:S(2)}, u32[]{:S(2)}) %collective-permute-start.20) | collective-permute-done | bytes 131104 | tf_op jit(solution)/shard_map/ppermute | solution.py:28
  169.8 3.5 %collective-permute-start.21 = (bf16[64,2048]{1,0:T(8,128)(2,1)S(1)}, bf16[64,2048]{1,0:T(8,128)(2,1)S(1)}, u32[]{:S(2)}, u32[]{:S(2)}) collective-permute-start(bf16[64,2048]{1,0:T(8,128)(2,1)S(1)} %pad_maximum_fusion.1), channel_id=1, source_target_pairs={{0,56},{8,0},{16,8},{24,16},{32,24},{40,32},{48,40},{56,48},{1,57}... | collective-permute-start | bytes 786440 | tf_op jit(solution)/shard_map/ppermute | solution.py:28
  173.3 5.5 %collective-permute-done.17 = bf16[64,2048]{1,0:T(8,128)(2,1)S(1)} collective-permute-done((bf16[64,2048]{1,0:T(8,128)(2,1)S(1)}, bf16[64,2048]{1,0:T(8,128)(2,1)S(1)}, u32[]{:S(2)}, u32[]{:S(2)}) %collective-permute-start.17) | collective-permute-done | bytes 262176 | tf_op jit(solution)/shard_map/ppermute | solution.py:28
  179.1 3.3 %collective-permute-start.22 = (bf16[64,2048]{1,0:T(8,128)(2,1)S(1)}, bf16[64,2048]{1,0:T(8,128)(2,1)S(1)}, u32[]{:S(2)}, u32[]{:S(2)}) collective-permute-start(bf16[64,2048]{1,0:T(8,128)(2,1)S(1)} %add_convert_fusion.2), channel_id=1, source_target_pairs={{0,56},{8,0},{16,8},{24,16},{32,24},{40,32},{48,40},{56,48},{1,57}... | collective-permute-start | bytes 786440 | tf_op jit(solution)/shard_map/ppermute | solution.py:28
  182.4 4.8 %collective-permute-done.18 = bf16[64,2048]{1,0:T(8,128)(2,1)S(1)} collective-permute-done((bf16[64,2048]{1,0:T(8,128)(2,1)S(1)}, bf16[64,2048]{1,0:T(8,128)(2,1)S(1)}, u32[]{:S(2)}, u32[]{:S(2)}) %collective-permute-start.18) | collective-permute-done | bytes 262176 | tf_op jit(solution)/shard_map/ppermute | solution.py:28
  187.4 3.3 %collective-permute-start.23 = (bf16[64,2048]{1,0:T(8,128)(2,1)S(1)}, bf16[64,2048]{1,0:T(8,128)(2,1)S(1)}, u32[]{:S(2)}, u32[]{:S(2)}) collective-permute-start(bf16[64,2048]{1,0:T(8,128)(2,1)S(1)} %add_convert_fusion.1), channel_id=1, source_target_pairs={{0,56},{8,0},{16,8},{24,16},{32,24},{40,32},{48,40},{56,48},{1,57}... | collective-permute-start | bytes 786440 | tf_op jit(solution)/shard_map/ppermute | solution.py:28
  190.7 4.2 %collective-permute-done.19 = bf16[64,2048]{1,0:T(8,128)(2,1)S(1)} collective-permute-done((bf16[64,2048]{1,0:T(8,128)(2,1)S(1)}, bf16[64,2048]{1,0:T(8,128)(2,1)S(1)}, u32[]{:S(2)}, u32[]{:S(2)}) %collective-permute-start.19) | collective-permute-done | bytes 262176 | tf_op jit(solution)/shard_map/ppermute | solution.py:28
  (77 shorter events, 27.7 us)
Async XLA Ops:
  1.1 11.2 %collective-permute-start = (bf16[2,256,128]{2,1,0:T(8,128)(2,1)S(1)}, bf16[2,256,128]{2,1,0:T(8,128)(2,1)S(1)}, u32[]{:S(2)}, u32[]{:S(2)}) collective-permute-start(bf16[2,256,128]{2,1,0:T(8,128)(2,1)S(1)} %pad_maximum_fusion.2), channel_id=1, source_target_pairs={{0,8},{8,16},{16,24},{24,32},{32,40},{40,48},{48,56},{56,64},{64,7... | collective-permute-start | bytes 393224 | tf_op jit(solution)/shard_map/ppermute | solution.py:37
  18.8 2.7 %collective-permute-start.1 = (bf16[256,2048]{1,0:T(8,128)(2,1)S(1)}, bf16[256,2048]{1,0:T(8,128)(2,1)S(1)}, u32[]{:S(2)}, u32[]{:S(2)}) collective-permute-start(bf16[256,2048]{1,0:T(8,128)(2,1)S(1)} %convolution_convert_fusion.1), channel_id=1, source_target_pairs={{0,1},{1,0},{2,3},{3,2},{4,5},{5,4},{6,7},{7,6},{8,9},{9,8},{10,11... | collective-permute-start | bytes 3145736 | tf_op jit(solution)/shard_map/ppermute | solution.py:32
  24.1 9.8 %collective-permute-start.2 = (bf16[64,2048]{1,0:T(8,128)(2,1)}, bf16[64,2048]{1,0:T(8,128)(2,1)S(1)}, u32[]{:S(2)}, u32[]{:S(2)}) collective-permute-start(bf16[64,2048]{1,0:T(8,128)(2,1)} %get-tuple-element.59), channel_id=1, source_target_pairs={{0,2},{2,4},{4,6},{6,0},{1,3},{3,5},{5,7},{7,1},{8,10},{10,12},{12... | collective-permute-start | bytes 786440 | tf_op jit(solution)/shard_map/ppermute | solution.py:28
  25.7 9.4 %collective-permute-start.4 = (bf16[64,2048]{1,0:T(8,128)(2,1)}, bf16[64,2048]{1,0:T(8,128)(2,1)S(1)}, u32[]{:S(2)}, u32[]{:S(2)}) collective-permute-start(bf16[64,2048]{1,0:T(8,128)(2,1)} %get-tuple-element.60), channel_id=1, source_target_pairs={{0,6},{2,0},{4,2},{6,4},{1,7},{3,1},{5,3},{7,5},{8,14},{10,8},{12,... | collective-permute-start | bytes 786440 | tf_op jit(solution)/shard_map/ppermute | solution.py:28
  27.4 13.4 %collective-permute-start.3 = (bf16[64,2048]{1,0:T(8,128)(2,1)S(1)}, bf16[64,2048]{1,0:T(8,128)(2,1)S(1)}, u32[]{:S(2)}, u32[]{:S(2)}) collective-permute-start(bf16[64,2048]{1,0:T(8,128)(2,1)S(1)} %get-tuple-element.61), channel_id=1, source_target_pairs={{0,4},{2,6},{4,0},{6,2},{1,5},{3,7},{5,1},{7,3},{8,12},{10,14},{12... | collective-permute-start | bytes 786440 | tf_op jit(solution)/shard_map/ppermute | solution.py:28
  29.4 40.8 %collective-permute-start.13 = (bf16[1,2048,384]{2,1,0:T(8,128)(2,1)}, bf16[1,2048,384]{2,1,0:T(8,128)(2,1)}, u32[]{:S(2)}, u32[]{:S(2)}) collective-permute-start(bf16[1,2048,384]{2,1,0:T(8,128)(2,1)} %g0), channel_id=1, source_target_pairs={{0,1},{1,0},{2,3},{3,2},{4,5},{5,4},{6,7},{7,6},{8,9},{9,8},{10,11... | collective-permute-start | bytes 4718600 | tf_op jit(solution)/shard_map/ppermute | solution.py:32
  29.4 40.8 %collective-permute-start.14 = (bf16[1,2048,384]{2,1,0:T(8,128)(2,1)}, bf16[1,2048,384]{2,1,0:T(8,128)(2,1)}, u32[]{:S(2)}, u32[]{:S(2)}) collective-permute-start(bf16[1,2048,384]{2,1,0:T(8,128)(2,1)} %u0), channel_id=1, source_target_pairs={{0,1},{1,0},{2,3},{3,2},{4,5},{5,4},{6,7},{7,6},{8,9},{9,8},{10,11... | collective-permute-start | bytes 4718600 | tf_op jit(solution)/shard_map/ppermute | solution.py:32
  34.0 36.2 %collective-permute-start.15 = (bf16[1,384,2048]{2,1,0:T(8,128)(2,1)}, bf16[1,384,2048]{2,1,0:T(8,128)(2,1)}, u32[]{:S(2)}, u32[]{:S(2)}) collective-permute-start(bf16[1,384,2048]{2,1,0:T(8,128)(2,1)} %d0), channel_id=1, source_target_pairs={{0,1},{1,0},{2,3},{3,2},{4,5},{5,4},{6,7},{7,6},{8,9},{9,8},{10,11... | collective-permute-start | bytes 4718600 | tf_op jit(solution)/shard_map/ppermute | solution.py:32
  43.1 7.9 %collective-permute-start.6 = (bf16[64,2176]{1,0:T(8,128)(2,1)S(1)}, bf16[64,2176]{1,0:T(8,128)(2,1)S(1)}, u32[]{:S(2)}, u32[]{:S(2)}) collective-permute-start(bf16[64,2176]{1,0:T(8,128)(2,1)S(1)} %concatenate.9.refs_0_), channel_id=1, source_target_pairs={{0,56},{8,0},{16,8},{24,16},{32,24},{40,32},{48,40},{56,48},{1,57}... | collective-permute-start | bytes 835592 | tf_op jit(solution)/shard_map/ppermute | solution.py:28
  45.0 9.1 %collective-permute-start.5 = (bf16[64,2176]{1,0:T(8,128)(2,1)S(1)}, bf16[64,2176]{1,0:T(8,128)(2,1)S(1)}, u32[]{:S(2)}, u32[]{:S(2)}) collective-permute-start(bf16[64,2176]{1,0:T(8,128)(2,1)S(1)} %concatenate.9.refs_0_), channel_id=1, source_target_pairs={{0,8},{8,16},{16,24},{24,32},{32,40},{40,48},{48,56},{56,0},{1,9},... | collective-permute-start | bytes 835592 | tf_op jit(solution)/shard_map/ppermute | solution.py:28
  51.1 7.4 %collective-permute-start.8 = (bf16[64,2176]{1,0:T(8,128)(2,1)S(1)}, bf16[64,2176]{1,0:T(8,128)(2,1)S(1)}, u32[]{:S(2)}, u32[]{:S(2)}) collective-permute-start(bf16[64,2176]{1,0:T(8,128)(2,1)S(1)} %collective-permute-done.6.refs_2_), channel_id=1, source_target_pairs={{0,56},{8,0},{16,8},{24,16},{32,24},{40,32},{48,40},{56,48},{1,57}... | collective-permute-start | bytes 835592 | tf_op jit(solution)/shard_map/ppermute | solution.py:28
  54.1 8.2 %collective-permute-start.7 = (bf16[64,2176]{1,0:T(8,128)(2,1)S(1)}, bf16[64,2176]{1,0:T(8,128)(2,1)S(1)}, u32[]{:S(2)}, u32[]{:S(2)}) collective-permute-start(bf16[64,2176]{1,0:T(8,128)(2,1)S(1)} %collective-permute-done.5.refs_1_), channel_id=1, source_target_pairs={{0,8},{8,16},{16,24},{24,32},{32,40},{40,48},{48,56},{56,0},{1,9},... | collective-permute-start | bytes 835592 | tf_op jit(solution)/shard_map/ppermute | solution.py:28
  58.5 7.8 %collective-permute-start.10 = (bf16[64,2176]{1,0:T(8,128)(2,1)S(1)}, bf16[64,2176]{1,0:T(8,128)(2,1)S(1)}, u32[]{:S(2)}, u32[]{:S(2)}) collective-permute-start(bf16[64,2176]{1,0:T(8,128)(2,1)S(1)} %collective-permute-done.8.refs_4_), channel_id=1, source_target_pairs={{0,56},{8,0},{16,8},{24,16},{32,24},{40,32},{48,40},{56,48},{1,57}... | collective-permute-start | bytes 835592 | tf_op jit(solution)/shard_map/ppermute | solution.py:28
  62.2 7.9 %collective-permute-start.9 = (bf16[64,2176]{1,0:T(8,128)(2,1)S(1)}, bf16[64,2176]{1,0:T(8,128)(2,1)S(1)}, u32[]{:S(2)}, u32[]{:S(2)}) collective-permute-start(bf16[64,2176]{1,0:T(8,128)(2,1)S(1)} %collective-permute-done.7.refs_3_), channel_id=1, source_target_pairs={{0,8},{8,16},{16,24},{24,32},{32,40},{40,48},{48,56},{56,0},{1,9},... | collective-permute-start | bytes 835592 | tf_op jit(solution)/shard_map/ppermute | solution.py:28
  66.3 10.0 %collective-permute-start.12 = (bf16[64,1152]{1,0:T(8,128)(2,1)S(1)}, bf16[64,1152]{1,0:T(8,128)(2,1)S(1)}, u32[]{:S(2)}, u32[]{:S(2)}) collective-permute-start(bf16[64,1152]{1,0:T(8,128)(2,1)S(1)} %slice.94), channel_id=1, source_target_pairs={{0,56},{8,0},{16,8},{24,16},{32,24},{40,32},{48,40},{56,48},{1,57}... | collective-permute-start | bytes 442376 | tf_op jit(solution)/shard_map/ppermute | solution.py:28
  70.1 6.3 %collective-permute-start.11 = (bf16[64,1024]{1,0:T(8,128)(2,1)S(1)}, bf16[64,1024]{1,0:T(8,128)(2,1)S(1)}, u32[]{:S(2)}, u32[]{:S(2)}) collective-permute-start(bf16[64,1024]{1,0:T(8,128)(2,1)S(1)} %slice.93), channel_id=1, source_target_pairs={{0,8},{8,16},{16,24},{24,32},{32,40},{40,48},{48,56},{56,0},{1,9},... | collective-permute-start | bytes 393224 | tf_op jit(solution)/shard_map/ppermute | solution.py:28
  161.8 6.4 %collective-permute-start.20 = (bf16[64,1024]{1,0:T(8,128)(2,1)S(1)}, bf16[64,1024]{1,0:T(8,128)(2,1)S(1)}, u32[]{:S(2)}, u32[]{:S(2)}) collective-permute-start(bf16[64,1024]{1,0:T(8,128)(2,1)S(1)} %get-tuple-element.52), channel_id=1, source_target_pairs={{0,56},{8,0},{16,8},{24,16},{32,24},{40,32},{48,40},{56,48},{1,57}... | collective-permute-start | bytes 393224 | tf_op jit(solution)/shard_map/ppermute | solution.py:28
  162.3 7.2 %collective-permute-start.16 = (bf16[64,1024]{1,0:T(8,128)(2,1)S(1)}, bf16[64,1024]{1,0:T(8,128)(2,1)S(1)}, u32[]{:S(2)}, u32[]{:S(2)}) collective-permute-start(bf16[64,1024]{1,0:T(8,128)(2,1)S(1)} %get-tuple-element.54), channel_id=1, source_target_pairs={{0,8},{8,16},{16,24},{24,32},{32,40},{40,48},{48,56},{56,0},{1,9},... | collective-permute-start | bytes 393224 | tf_op jit(solution)/shard_map/ppermute | solution.py:28
  169.6 9.2 %collective-permute-start.17 = (bf16[64,2048]{1,0:T(8,128)(2,1)S(1)}, bf16[64,2048]{1,0:T(8,128)(2,1)S(1)}, u32[]{:S(2)}, u32[]{:S(2)}) collective-permute-start(bf16[64,2048]{1,0:T(8,128)(2,1)S(1)} %pad_maximum_fusion), channel_id=1, source_target_pairs={{0,8},{8,16},{16,24},{24,32},{32,40},{40,48},{48,56},{56,0},{1,9},... | collective-permute-start | bytes 786440 | tf_op jit(solution)/shard_map/ppermute | solution.py:28
  169.8 9.2 %collective-permute-start.21 = (bf16[64,2048]{1,0:T(8,128)(2,1)S(1)}, bf16[64,2048]{1,0:T(8,128)(2,1)S(1)}, u32[]{:S(2)}, u32[]{:S(2)}) collective-permute-start(bf16[64,2048]{1,0:T(8,128)(2,1)S(1)} %pad_maximum_fusion.1), channel_id=1, source_target_pairs={{0,56},{8,0},{16,8},{24,16},{32,24},{40,32},{48,40},{56,48},{1,57}... | collective-permute-start | bytes 786440 | tf_op jit(solution)/shard_map/ppermute | solution.py:28
  178.9 8.3 %collective-permute-start.18 = (bf16[64,2048]{1,0:T(8,128)(2,1)S(1)}, bf16[64,2048]{1,0:T(8,128)(2,1)S(1)}, u32[]{:S(2)}, u32[]{:S(2)}) collective-permute-start(bf16[64,2048]{1,0:T(8,128)(2,1)S(1)} %add_convert_fusion.4), channel_id=1, source_target_pairs={{0,8},{8,16},{16,24},{24,32},{32,40},{40,48},{48,56},{56,0},{1,9},... | collective-permute-start | bytes 786440 | tf_op jit(solution)/shard_map/ppermute | solution.py:28
  179.1 8.3 %collective-permute-start.22 = (bf16[64,2048]{1,0:T(8,128)(2,1)S(1)}, bf16[64,2048]{1,0:T(8,128)(2,1)S(1)}, u32[]{:S(2)}, u32[]{:S(2)}) collective-permute-start(bf16[64,2048]{1,0:T(8,128)(2,1)S(1)} %add_convert_fusion.2), channel_id=1, source_target_pairs={{0,56},{8,0},{16,8},{24,16},{32,24},{40,32},{48,40},{56,48},{1,57}... | collective-permute-start | bytes 786440 | tf_op jit(solution)/shard_map/ppermute | solution.py:28
  187.2 7.7 %collective-permute-start.19 = (bf16[64,2048]{1,0:T(8,128)(2,1)S(1)}, bf16[64,2048]{1,0:T(8,128)(2,1)S(1)}, u32[]{:S(2)}, u32[]{:S(2)}) collective-permute-start(bf16[64,2048]{1,0:T(8,128)(2,1)S(1)} %add_convert_fusion.3), channel_id=1, source_target_pairs={{0,8},{8,16},{16,24},{24,32},{32,40},{40,48},{48,56},{56,0},{1,9},... | collective-permute-start | bytes 786440 | tf_op jit(solution)/shard_map/ppermute | solution.py:28
  187.4 7.5 %collective-permute-start.23 = (bf16[64,2048]{1,0:T(8,128)(2,1)S(1)}, bf16[64,2048]{1,0:T(8,128)(2,1)S(1)}, u32[]{:S(2)}, u32[]{:S(2)}) collective-permute-start(bf16[64,2048]{1,0:T(8,128)(2,1)S(1)} %add_convert_fusion.1), channel_id=1, source_target_pairs={{0,56},{8,0},{16,8},{24,16},{32,24},{40,32},{48,40},{56,48},{1,57}... | collective-permute-start | bytes 786440 | tf_op jit(solution)/shard_map/ppermute | solution.py:28
  (9 other events, 118.9 us)

commit v5 on v4

--- a/solution.py
+++ b/solution.py
@@ -1,3 +1,4 @@
+import functools
 import math
 
 import jax
@@ -16,6 +17,8 @@
 META = 128
 PLANE = NX * NY
 SLOTS = NZ * CAP
+NEAR = 5
+NEAR_SLOTS = 24
 
 BF = jnp.bfloat16
 F32 = jnp.float32
@@ -185,38 +188,46 @@
     return blocks + [shift(right[:, :half], "z", NZ, 1), shift(left[:, half:], "z", NZ, -1)]
 
 
-def ring_sum(blocks):
-    half = blocks[0].shape[1] // 2
-
-    def add(a, b):
-        return (a.astype(F32) + b.astype(F32)).astype(BF)
-
+def add(a, b):
+    return (a.astype(F32) + b.astype(F32)).astype(BF)
+
+
+def ring_sum_far(blocks):
+    half = blocks[4].shape[1] // 2
     a = shift(blocks[4][:, :half], "z", NZ, 1)
     b = shift(blocks[4][:, half:], "z", NZ, -1)
     right = jnp.concatenate([add(blocks[3][:, :half], a), blocks[3][:, half:]], axis=1)
     left = jnp.concatenate([blocks[-3][:, :half], add(blocks[-3][:, half:], b)], axis=1)
+    return shift(right, "z", NZ, 1), shift(left, "z", NZ, -1)
+
+
+def ring_sum_near(right, left, blocks):
     for step in (2, 1):
-        right = add(shift(right, "z", NZ, 1), blocks[step])
+        right = add(right, blocks[step])
         own = lax.optimization_barrier((blocks[-step], right))[0]
-        left = add(shift(left, "z", NZ, -1), own)
-    right = shift(right, "z", NZ, 1)
-    left = shift(left, "z", NZ, -1)
+        left = add(left, own)
+        right, left = shift(right, "z", NZ, 1), shift(left, "z", NZ, -1)
     return blocks[0].astype(F32) + right.astype(F32) + left.astype(F32)
 
 
-def dispatch_body(z_ref, *refs):
+def dispatch_body(first_block, first_slot, z_ref, *refs):
     blocks, (out_ref, weight_ref, tokens, meta, one_hot) = refs[:-5], refs[-5:]
-    width = tokens.shape[1]
-    count = tokens.shape[0]
-    cut = blocks[-2].shape[1]
-    for i, block in enumerate(blocks[:-2]):
-        at = slice(i * ROWS, (i + 1) * ROWS)
-        tokens[at] = block[:, :width]
-        meta[at] = block[:, width:]
-    at = slice(count - ROWS, count)
-    tokens[at, :cut] = blocks[-2][...]
-    tokens[at, cut:] = blocks[-1][:, : width - cut]
-    meta[at] = blocks[-1][:, width - cut :]
+    count, width = tokens.shape
+    slots = out_ref.shape[0] // PLANE
+    filled = 0
+    column = 0
+    for block in blocks:
+        at = slice(filled, filled + ROWS)
+        here = min(block.shape[1], width - column)
+        tokens[at, column : column + here] = block[:, :here]
+        column += here
+        if block.shape[1] > here:
+            meta[at] = block[:, here:]
+        if column == width:
+            filled, column = filled + ROWS, 0
+    if filled < count:
+        tokens[filled:] = jnp.zeros((count - filled, width), BF)
+        meta[filled:] = jnp.full((count - filled, META), -1.0, BF)
 
     turned = meta[...].astype(F32).T
     ids, gates = turned[:TOP], turned[TOP : 2 * TOP]
@@ -233,49 +244,50 @@
     rank = jnp.dot(
         all_named.astype(BF), jnp.where(before, 1.0, 0.0).astype(BF), preferred_element_type=F32
     )
-    block_start = lax.broadcasted_iota(jnp.int32, (1, count), 1) // ROWS * CAP
-    slot = jnp.where(all_named > 0.0, rank + block_start.astype(F32), -1.0)
-    slots = lax.broadcasted_iota(jnp.int32, (SLOTS, 1), 0).astype(F32)
+    start = (lax.broadcasted_iota(jnp.int32, (1, count), 1) // ROWS + first_block) * CAP
+    slot = jnp.where(all_named > 0.0, rank + start.astype(F32), -1.0)
+    numbers = (first_slot + lax.broadcasted_iota(jnp.int32, (slots, 1), 0)).astype(F32)
     for pair in range(PLANE // 2):
         hits, weights = [], []
         for place in (2 * pair, 2 * pair + 1):
-            hit = slot[place : place + 1] == slots
+            hit = slot[place : place + 1] == numbers
             hits.append(jnp.where(hit, 1.0, 0.0))
             weights.append(jnp.where(hit, gate[place], 0.0))
-        at = slice(2 * pair * SLOTS, (2 * pair + 2) * SLOTS)
+        at = slice(2 * pair * slots, (2 * pair + 2) * slots)
         one_hot[at] = jnp.concatenate(hits, axis=0).astype(BF)
         weight_ref[at] = jnp.concatenate(weights, axis=0).astype(BF)
     tile = 256
 
-    def column(i, carry):
+    def fill(i, carry):
         at = pl.ds(pl.multiple_of(i * tile, tile), tile)
         out_ref[:, at] = jnp.dot(
             one_hot[...], tokens[:, at], preferred_element_type=F32
         ).astype(BF)
         return carry
 
-    lax.fori_loop(0, width // tile, column, 0)
-
-
-def dispatch(blocks, width):
-    count = NZ * ROWS
+    lax.fori_loop(0, width // tile, fill, 0)
+
+
+def dispatch(blocks, first_block, first_slot, slots, width):
+    filled = ROWS * (sum(block.shape[1] for block in blocks) // width)
+    count = -(-filled // 128) * 128
     whole = pl.BlockSpec(memory_space=pltpu.VMEM)
     return pl.pallas_call(
-        dispatch_body,
+        functools.partial(dispatch_body, first_block, first_slot),
         out_shape=(
-            jax.ShapeDtypeStruct((PLANE * SLOTS, width), BF),
-            jax.ShapeDtypeStruct((PLANE * SLOTS, count), BF),
+            jax.ShapeDtypeStruct((PLANE * slots, width), BF),
+            jax.ShapeDtypeStruct((PLANE * slots, count), BF),
         ),
         in_specs=[pl.BlockSpec(memory_space=pltpu.SMEM)] + [whole] * len(blocks),
         out_specs=(whole, whole),
         scratch_shapes=[
             pltpu.VMEM((count, width), BF),
             pltpu.VMEM((count, META), BF),
-            pltpu.VMEM((PLANE * SLOTS, count), BF),
+            pltpu.VMEM((PLANE * slots, count), BF),
         ],
         compiler_params=pltpu.CompilerParams(vmem_limit_bytes=24 * 1024 * 1024),
         cost_estimate=pl.CostEstimate(
-            flops=2 * PLANE * SLOTS * count * width,
+            flops=2 * PLANE * slots * count * width,
             bytes_accessed=4 * count * width,
             transcendentals=0,
         ),
@@ -336,7 +348,7 @@
             pltpu.VMEM((count, hid), BF),
             pltpu.SemaphoreType.DMA((6,)),
         ],
-        compiler_params=pltpu.CompilerParams(vmem_limit_bytes=28 * 1024 * 1024),
+        compiler_params=pltpu.CompilerParams(vmem_limit_bytes=57 * 1024 * 1024),
         cost_estimate=pl.CostEstimate(
             flops=6 * count * width * hid,
             bytes_accessed=6 * width * hid + 4 * count * width,
@@ -346,11 +358,19 @@
 
 
 def exchange(rows):
-    width = rows.shape[1]
+    count, width = rows.shape
     out = lax.all_to_all(
-        rows.reshape(PLANE, SLOTS, width), ("x", "y"), split_axis=0, concat_axis=0, tiled=True
-    )
-    return out.reshape(PLANE * SLOTS, width)
+        rows.reshape(PLANE, count // PLANE, width),
+        ("x", "y"),
+        split_axis=0,
+        concat_axis=0,
+        tiled=True,
+    )
+    return out.reshape(count, width)
+
+
+def weighted_sum(weights, rows):
+    return lax.dot_general(weights, rows, (((0,), (0,)), ((), ())), preferred_element_type=F32)
 
 
 def local(
@@ -382,18 +402,29 @@
         ],
         axis=1,
     )
-    blocks, pairs = lax.optimization_barrier(
-        (ring_gather(jnp.concatenate([normed, meta], axis=1), width // 2), pairs)
-    )
-    outgoing, weighted = dispatch(blocks, width)
-    mine = exchange(outgoing)
-    pair_out = expert_rows(mine, *pairs)
-    returned = exchange(pair_out)
-    plane_sum = lax.dot_general(
-        weighted, returned, (((0,), (0,)), ((), ())), preferred_element_type=F32
-    ).astype(BF)
-    blocks = plane_sum.reshape(NZ, ROWS, -1)
-    expert_sum = ring_sum({offset: blocks[i] for i, offset in enumerate(RING)})
+    blocks = ring_gather(jnp.concatenate([normed, meta], axis=1), width // 2)
+    out_near, weight_near = dispatch(blocks[:NEAR], 0, 0, NEAR_SLOTS, width)
+    arrived_near = exchange(out_near)
+    far_blocks, pairs = lax.optimization_barrier((blocks[NEAR - 1 :], pairs))
+    out_far, weight_far = dispatch(
+        far_blocks, NEAR - 1, NEAR_SLOTS, SLOTS - NEAR_SLOTS, width
+    )
+    out_far, arrived_near = lax.optimization_barrier((out_far, arrived_near))
+    arrived_far = exchange(out_far)
+    pair_near = expert_rows(arrived_near, *pairs)
+    arrived_far, pair_near = lax.optimization_barrier((arrived_far, pair_near))
+    pair_far = expert_rows(arrived_far, *pairs)
+
+    returned_far = exchange(pair_far)
+    returned_far, pair_near = lax.optimization_barrier((returned_far, pair_near))
+    returned_near = exchange(pair_near)
+    far = weighted_sum(weight_far, returned_far).reshape(-1, ROWS, width)
+    terms = {offset: far[1 + i].astype(BF) for i, offset in enumerate(RING[NEAR:])}
+    right, left = ring_sum_far(terms)
+    near = weighted_sum(weight_near, returned_near)[: NEAR * ROWS].reshape(NEAR, ROWS, width)
+    terms = {offset: near[i].astype(BF) for i, offset in enumerate(RING[: NEAR - 1])}
+    terms[RING[NEAR - 1]] = (near[NEAR - 1] + far[0]).astype(BF)
+    expert_sum = ring_sum_near(right, left, terms)
     return (mid + expert_sum).astype(BF)
 
 

time: 199 us -> 190 us (0.955); the launches traced: 196 us -> 189 us
  blocking collectives: 70.3 us -> 16.9 us
  starting transfers between devices: 34.7 us -> 52.6 us
  waiting for transfers between devices: 56 us -> 68.5 us
  Pallas kernels: 21.3 us -> 32.1 us
  matrix products: 4.26 us -> 7.84 us
    all_to_all x2 -> x1, blocking collectives: 70.3 us -> 16.9 us  [exchange(): lax.all_to_all(rows.reshape(PLANE, count // PLANE, width), ('x', 'y'), sp...]
    all_to_all x0 -> x3, starting transfers between devices: none -> 20.3 us  [exchange(): lax.all_to_all(rows.reshape(PLANE, count // PLANE, width), ('x', 'y'), sp...]
    pallas_call x1 -> x2, Pallas kernels: 9.88 us -> 18.6 us  [expert_rows(): pl.pallas_call(expert_body, out_shape=jax.ShapeDtypeStruct((count, width)...]
    all_to_all x0 -> x3, waiting for transfers between devices: none -> 6.63 us  [exchange(): lax.all_to_all(rows.reshape(PLANE, count // PLANE, width), ('x', 'y'), sp...]
    ppermute x19, waiting for transfers between devices: 51.3 us -> 57.1 us  [shift(): lax.ppermute(value, axis, [(i, (i + by) % size) for i in range(size)])]
    dot_general x1 -> x2, matrix products: 1.85 us -> 5.43 us  [weighted_sum(): lax.dot_general(weights, rows, (((0,), (0,)), ((), ())), preferred_elemen...]
    ppermute x19, starting transfers between devices: 30.3 us -> 27.7 us  [shift(): lax.ppermute(value, axis, [(i, (i + by) % size) for i in range(size)])]
    pallas_call x1 -> x2, Pallas kernels: 3.35 us -> 5.41 us  [dispatch(): pl.pallas_call(functools.partial(dispatch_body, first_block, first_slot),...]
  transfers between devices with their start and end apart: 24 -> 27, of which waited for: 14 -> 18; matrix products, arithmetic and copies ran while one was open for 2% -> 4% of each run, Pallas kernels for 2% -> 10%
where the time goes in v5:
time: 190 us; the launch traced here: 189 us
  waiting for transfers between devices  68.5 us (36%)
  starting transfers between devices  52.6 us (28%)
  Pallas kernels  32.1 us (17%)
  blocking collectives  16.9 us (9%)
  matrix products  7.84 us (4%)
  other arithmetic  6.04 us (3%)
  local copies, waits for them, and re-layouts  4.8 us (3%)
    ppermute x19, waiting for transfers between devices, shift(): lax.ppermute(value, axis, [(i, (i + by) % size) for i in range(size)])  57.1 us
    ppermute x19, starting transfers between devices, shift(): lax.ppermute(value, axis, [(i, (i + by) % size) for i in range(size)])  27.7 us
    all_to_all x3, starting transfers between devices, exchange(): lax.all_to_all(rows.reshape(PLANE, count // PLANE, width), ('x', 'y'), sp...  20.3 us
    pallas_call x2, Pallas kernels, expert_rows(): pl.pallas_call(expert_body, out_shape=jax.ShapeDtypeStruct((count, width)...  18.6 us
    all_to_all x1, blocking collectives, exchange(): lax.all_to_all(rows.reshape(PLANE, count // PLANE, width), ('x', 'y'), sp...  16.9 us
    all_to_all x3, waiting for transfers between devices, exchange(): lax.all_to_all(rows.reshape(PLANE, count // PLANE, width), ('x', 'y'), sp...  6.63 us
    dot_general x2, matrix products, weighted_sum(): lax.dot_general(weights, rows, (((0,), (0,)), ((), ())), preferred_elemen...  5.43 us
    pallas_call x2, Pallas kernels, dispatch(): pl.pallas_call(functools.partial(dispatch_body, first_block, first_slot),...  5.41 us
  transfers between devices with their start and end apart: 27, of which 18 were waited for; matrix products, arithmetic and copies ran while one was open for 4% of the time, Pallas kernels for 10%

profile of v5, /device:TPU:2, one launch (start us, length us, event | category | flops | bytes accessed | tf_op | source)
XLA Modules:
  0.0 189.1 jit_solution(7235615851667275561)
XLA Ops:
  1.1 3.8 %collective-permute-start = (bf16[2,256,128]{2,1,0:T(8,128)(2,1)S(1)}, bf16[2,256,128]{2,1,0:T(8,128)(2,1)S(1)}, u32[]{:S(2)}, u32[]{:S(2)}) collective-permute-start(bf16[2,256,128]{2,1,0:T(8,128)(2,1)S(1)} %pad_maximum_fusion.2), channel_id=1, source_target_pairs={{0,8},{8,16},{16,24},{24,32},{32,40},{40,48},{48,56},{56,64},{64,7... | collective-permute-start | bytes 393224 | tf_op jit(solution)/shard_map/ppermute | solution.py:40
  5.5 3.9 %shard_map.118.late_ref = bf16[256,512]{1,0:T(8,128)(2,1)} custom-call(s32[3]{0:T(128)} %pad_add_fusion.where, bf16[512,512]{1,0:T(8,128)(2,1)} %q_ref.3, bf16[512,512]{1,0:T(8,128)(2,1)} %kb.3, bf16[512,512]{1,0:T(8,128)(2,1)} %kb.3, bf16[512,512]{1,0:T(8,128)(2,1)} %vb.3, bf16[512,512]{1,0:T(8,128)(2,1)} %vb.3, s32[1,128]{1,0:T(1,128)} %bitcast.29), custom_call_target="tpu_custom_call" | custom-call | flops 1073741824 | bytes 786432 | tf_op jit(solution)/shard_map/pallas_call | solution.py:121
  12.9 4.2 %shard_map.119 = (bf16[256,512]{1,0:T(8,128)(2,1)}, bf16[256,512]{1,0:T(8,128)(2,1)}) custom-call(s32[3]{0:T(128)} %pad_add_fusion.where, bf16[512,512]{1,0:T(8,128)(2,1)} %q_ref.3, bf16[2,256,128]{2,1,0:T(8,128)(2,1)} %copy-done.9, bf16[512,512]{1,0:T(8,128)(2,1)} %kb.3, bf16[512,512]{1,0:T(8,128)(2,1)} %vb.3, s32[1,128]{1,0:T(1,128)} %bitcast.30, ...), custom_call_target="tpu_custom_call" | custom-call | flops 1073741824 | bytes 1048576 | tf_op jit(solution)/shard_map/pallas_call | solution.py:142
  30.2 3.8 %collective-permute-done.2 = bf16[64,2048]{1,0:T(8,128)(2,1)S(1)} collective-permute-done((bf16[64,2048]{1,0:T(8,128)(2,1)}, bf16[64,2048]{1,0:T(8,128)(2,1)S(1)}, u32[]{:S(2)}, u32[]{:S(2)}) %collective-permute-start.2) | collective-permute-done | bytes 262176 | tf_op jit(solution)/shard_map/ppermute | solution.py:31
  34.0 6.8 %collective-permute-done.3 = bf16[64,2048]{1,0:T(8,128)(2,1)S(1)} collective-permute-done((bf16[64,2048]{1,0:T(8,128)(2,1)}, bf16[64,2048]{1,0:T(8,128)(2,1)S(1)}, u32[]{:S(2)}, u32[]{:S(2)}) %collective-permute-start.3) | collective-permute-done | bytes 262176 | tf_op jit(solution)/shard_map/ppermute | solution.py:31
  45.1 5.8 %collective-permute-done.6.refs_2_ = bf16[64,2176]{1,0:T(8,128)(2,1)S(1)} collective-permute-done((bf16[64,2176]{1,0:T(8,128)(2,1)S(1)}, bf16[64,2176]{1,0:T(8,128)(2,1)S(1)}, u32[]{:S(2)}, u32[]{:S(2)}) %collective-permute-start.6) | collective-permute-done | bytes 278560 | tf_op jit(solution)/shard_map/ppermute | solution.py:31
  51.0 3.0 %collective-permute-start.8 = (bf16[64,2176]{1,0:T(8,128)(2,1)S(1)}, bf16[64,2176]{1,0:T(8,128)(2,1)S(1)}, u32[]{:S(2)}, u32[]{:S(2)}) collective-permute-start(bf16[64,2176]{1,0:T(8,128)(2,1)S(1)} %collective-permute-done.6.refs_2_), channel_id=1, source_target_pairs={{0,56},{8,0},{16,8},{24,16},{32,24},{40,32},{48,40},{56,48},{1,57}... | collective-permute-start | bytes 835592 | tf_op jit(solution)/shard_map/ppermute | solution.py:31
  54.6 3.9 %collective-permute-done.8.refs_4_.refs_0_ = bf16[64,2176]{1,0:T(8,128)(2,1)S(1)} collective-permute-done((bf16[64,2176]{1,0:T(8,128)(2,1)S(1)}, bf16[64,2176]{1,0:T(8,128)(2,1)S(1)}, u32[]{:S(2)}, u32[]{:S(2)}) %collective-permute-start.8) | collective-permute-done | bytes 278560 | tf_op jit(solution)/shard_map/ppermute | solution.py:31
  58.4 3.4 %collective-permute-done.7.refs_3_ = bf16[64,2176]{1,0:T(8,128)(2,1)S(1)} collective-permute-done((bf16[64,2176]{1,0:T(8,128)(2,1)S(1)}, bf16[64,2176]{1,0:T(8,128)(2,1)S(1)}, u32[]{:S(2)}, u32[]{:S(2)}) %collective-permute-start.7) | collective-permute-done | bytes 278560 | tf_op jit(solution)/shard_map/ppermute | solution.py:31
  65.6 7.8 %all-to-all-start = ((bf16[16,24,2048]{2,1,0:T(8,128)(2,1)}), bf16[16,24,2048]{2,1,0:T(8,128)(2,1)}, u32[]{:S(2)}, u32[]{:S(2)}) async-start(bf16[16,24,2048]{2,1,0:T(8,128)(2,1)} %bitcast.25), calls=%async_computation | async-start | bytes 3145728 | tf_op jit(solution)/shard_map/all_to_all | solution.py:362
  75.4 5.1 %collective-permute-done.10.refs_2_ = bf16[64,2176]{1,0:T(8,128)(2,1)S(1)} collective-permute-done((bf16[64,2176]{1,0:T(8,128)(2,1)S(1)}, bf16[64,2176]{1,0:T(8,128)(2,1)S(1)}, u32[]{:S(2)}, u32[]{:S(2)}) %collective-permute-start.10) | collective-permute-done | bytes 278560 | tf_op jit(solution)/shard_map/ppermute | solution.py:31
  82.9 5.0 %collective-permute-done.11.refs_3_ = bf16[64,1024]{1,0:T(8,128)(2,1)S(1)} collective-permute-done((bf16[64,1024]{1,0:T(8,128)(2,1)S(1)}, bf16[64,1024]{1,0:T(8,128)(2,1)S(1)}, u32[]{:S(2)}, u32[]{:S(2)}) %collective-permute-start.11) | collective-permute-done | bytes 131104 | tf_op jit(solution)/shard_map/ppermute | solution.py:31
  93.2 6.0 %all-to-all-start.1 = ((bf16[16,16,2048]{2,1,0:T(8,128)(2,1)}), bf16[16,16,2048]{2,1,0:T(8,128)(2,1)}, u32[]{:S(2)}, u32[]{:S(2)}) async-start(bf16[16,16,2048]{2,1,0:T(8,128)(2,1)} %bitcast.9), calls=%async_computation.1 | async-start | bytes 2097152 | tf_op jit(solution)/shard_map/all_to_all | solution.py:362
  99.1 10.0 %shard_map.122 = bf16[384,2048]{1,0:T(8,128)(2,1)} custom-call(bf16[384,2048]{1,0:T(8,128)(2,1)} %bitcast.8.rows_ref, bf16[1,2048,384]{2,1,0:T(8,128)(2,1)} %g0.1, bf16[1,2048,384]{2,1,0:T(8,128)(2,1)} %collective-permute-done.13.g1, bf16[1,2048,384]{2,1,0:T(8,128)(2,1)} %u0.1, bf16[1,2048,384]{2,1,0:T(8,128)(2,1)} %collective-permute-done.14.u1, ...), custom_call_target="tpu_custom_call" | custom-call | flops 3623878656 | bytes 12582912 | tf_op jit(solution)/shard_map/pallas_call | solution.py:339
  111.4 8.6 %shard_map.123 = bf16[256,2048]{1,0:T(8,128)(2,1)} custom-call(bf16[256,2048]{1,0:T(8,128)(2,1)} %bitcast.10.rows_ref, bf16[1,2048,384]{2,1,0:T(8,128)(2,1)} %g0.1, bf16[1,2048,384]{2,1,0:T(8,128)(2,1)} %collective-permute-done.13.g1, bf16[1,2048,384]{2,1,0:T(8,128)(2,1)} %u0.1, bf16[1,2048,384]{2,1,0:T(8,128)(2,1)} %collective-permute-done.14.u1, ...), custom_call_target="tpu_custom_call" | custom-call | flops 2415919104 | bytes 11534336 | tf_op jit(solution)/shard_map/pallas_call | solution.py:339
  120.0 16.9 %all_to_all.20 = bf16[16,16,2048]{2,1,0:T(8,128)(2,1)} all-to-all(bf16[16,16,2048]{2,1,0:T(8,128)(2,1)} %bitcast.27), channel_id=1, replica_groups=mesh['x'=4,'z'=8,'y'=4,'c'=2] {'x','y'}, dimensions={0} | all-to-all | bytes 2097152 | tf_op jit(solution)/shard_map/all_to_all | solution.py:362
  136.9 6.5 %all-to-all-start.3 = ((bf16[16,24,2048]{2,1,0:T(8,128)(2,1)}), bf16[16,24,2048]{2,1,0:T(8,128)(2,1)}, u32[]{:S(2)}, u32[]{:S(2)}) async-start(bf16[16,24,2048]{2,1,0:T(8,128)(2,1)} %bitcast.28), calls=%async_computation.3 | async-start | bytes 3145728 | tf_op jit(solution)/shard_map/all_to_all | solution.py:362
  143.4 3.0 %fusion.7 = (bf16[256,2048]{1,0:T(8,128)(2,1)S(1)}, f32[256,2048]{1,0:T(8,128)}) fusion(bf16[256,256]{1,0:T(8,128)(2,1)S(1)} %get-tuple-element.51, bf16[256,2048]{1,0:T(8,128)(2,1)} %bitcast.26), kind=kOutput, calls=%fused_computation.26 | convolution fusion | flops 268959744 | bytes 4325376 | tf_op jit(solution)/shard_map/dot_general | solution.py:373
  154.4 3.1 %collective-permute-start.21 = (bf16[64,2048]{1,0:T(8,128)(2,1)S(1)}, bf16[64,2048]{1,0:T(8,128)(2,1)S(1)}, u32[]{:S(2)}, u32[]{:S(2)}) collective-permute-start(bf16[64,2048]{1,0:T(8,128)(2,1)S(1)} %pad_maximum_fusion.1), channel_id=1, source_target_pairs={{0,56},{8,0},{16,8},{24,16},{32,24},{40,32},{48,40},{56,48},{1,57}... | collective-permute-start | bytes 786440 | tf_op jit(solution)/shard_map/ppermute | solution.py:31
  162.2 6.1 %collective-permute-done.17 = bf16[64,2048]{1,0:T(8,128)(2,1)S(1)} collective-permute-done((bf16[64,2048]{1,0:T(8,128)(2,1)S(1)}, bf16[64,2048]{1,0:T(8,128)(2,1)S(1)}, u32[]{:S(2)}, u32[]{:S(2)}) %collective-permute-start.17) | collective-permute-done | bytes 262176 | tf_op jit(solution)/shard_map/ppermute | solution.py:31
  169.6 3.3 %collective-permute-start.22 = (bf16[64,2048]{1,0:T(8,128)(2,1)S(1)}, bf16[64,2048]{1,0:T(8,128)(2,1)S(1)}, u32[]{:S(2)}, u32[]{:S(2)}) collective-permute-start(bf16[64,2048]{1,0:T(8,128)(2,1)S(1)} %add_convert_fusion.2), channel_id=1, source_target_pairs={{0,56},{8,0},{16,8},{24,16},{32,24},{40,32},{48,40},{56,48},{1,57}... | collective-permute-start | bytes 786440 | tf_op jit(solution)/shard_map/ppermute | solution.py:31
  172.9 5.2 %collective-permute-done.18 = bf16[64,2048]{1,0:T(8,128)(2,1)S(1)} collective-permute-done((bf16[64,2048]{1,0:T(8,128)(2,1)S(1)}, bf16[64,2048]{1,0:T(8,128)(2,1)S(1)}, u32[]{:S(2)}, u32[]{:S(2)}) %collective-permute-start.18) | collective-permute-done | bytes 262176 | tf_op jit(solution)/shard_map/ppermute | solution.py:31
  180.7 4.1 %collective-permute-done.23 = bf16[64,2048]{1,0:T(8,128)(2,1)S(1)} collective-permute-done((bf16[64,2048]{1,0:T(8,128)(2,1)S(1)}, bf16[64,2048]{1,0:T(8,128)(2,1)S(1)}, u32[]{:S(2)}, u32[]{:S(2)}) %collective-permute-start.23) | collective-permute-done | bytes 262176 | tf_op jit(solution)/shard_map/ppermute | solution.py:31
  184.7 3.5 %collective-permute-done.19 = bf16[64,2048]{1,0:T(8,128)(2,1)S(1)} collective-permute-done((bf16[64,2048]{1,0:T(8,128)(2,1)S(1)}, bf16[64,2048]{1,0:T(8,128)(2,1)S(1)}, u32[]{:S(2)}, u32[]{:S(2)}) %collective-permute-start.19) | collective-permute-done | bytes 262176 | tf_op jit(solution)/shard_map/ppermute | solution.py:31
  (87 shorter events, 56.0 us)
Async XLA Ops:
  1.1 11.2 %collective-permute-start = (bf16[2,256,128]{2,1,0:T(8,128)(2,1)S(1)}, bf16[2,256,128]{2,1,0:T(8,128)(2,1)S(1)}, u32[]{:S(2)}, u32[]{:S(2)}) collective-permute-start(bf16[2,256,128]{2,1,0:T(8,128)(2,1)S(1)} %pad_maximum_fusion.2), channel_id=1, source_target_pairs={{0,8},{8,16},{16,24},{24,32},{32,40},{40,48},{48,56},{56,64},{64,7... | collective-permute-start | bytes 393224 | tf_op jit(solution)/shard_map/ppermute | solution.py:40
  24.2 9.8 %collective-permute-start.2 = (bf16[64,2048]{1,0:T(8,128)(2,1)}, bf16[64,2048]{1,0:T(8,128)(2,1)S(1)}, u32[]{:S(2)}, u32[]{:S(2)}) collective-permute-start(bf16[64,2048]{1,0:T(8,128)(2,1)} %get-tuple-element.67), channel_id=1, source_target_pairs={{0,2},{2,4},{4,6},{6,0},{1,3},{3,5},{5,7},{7,1},{8,10},{10,12},{12... | collective-permute-start | bytes 786440 | tf_op jit(solution)/shard_map/ppermute | solution.py:31
  25.7 15.1 %collective-permute-start.3 = (bf16[64,2048]{1,0:T(8,128)(2,1)}, bf16[64,2048]{1,0:T(8,128)(2,1)S(1)}, u32[]{:S(2)}, u32[]{:S(2)}) collective-permute-start(bf16[64,2048]{1,0:T(8,128)(2,1)} %get-tuple-element.69), channel_id=1, source_target_pairs={{0,4},{2,6},{4,0},{6,2},{1,5},{3,7},{5,1},{7,3},{8,12},{10,14},{12... | collective-permute-start | bytes 786440 | tf_op jit(solution)/shard_map/ppermute | solution.py:31
  28.6 12.2 %collective-permute-start.4 = (bf16[64,2048]{1,0:T(8,128)(2,1)S(1)}, bf16[64,2048]{1,0:T(8,128)(2,1)S(1)}, u32[]{:S(2)}, u32[]{:S(2)}) collective-permute-start(bf16[64,2048]{1,0:T(8,128)(2,1)S(1)} %get-tuple-element.68), channel_id=1, source_target_pairs={{0,6},{2,0},{4,2},{6,4},{1,7},{3,1},{5,3},{7,5},{8,14},{10,8},{12,... | collective-permute-start | bytes 786440 | tf_op jit(solution)/shard_map/ppermute | solution.py:31
  43.0 7.9 %collective-permute-start.6 = (bf16[64,2176]{1,0:T(8,128)(2,1)S(1)}, bf16[64,2176]{1,0:T(8,128)(2,1)S(1)}, u32[]{:S(2)}, u32[]{:S(2)}) collective-permute-start(bf16[64,2176]{1,0:T(8,128)(2,1)S(1)} %concatenate.9.refs_0_), channel_id=1, source_target_pairs={{0,56},{8,0},{16,8},{24,16},{32,24},{40,32},{48,40},{56,48},{1,57}... | collective-permute-start | bytes 835592 | tf_op jit(solution)/shard_map/ppermute | solution.py:31
  44.9 9.1 %collective-permute-start.5 = (bf16[64,2176]{1,0:T(8,128)(2,1)S(1)}, bf16[64,2176]{1,0:T(8,128)(2,1)S(1)}, u32[]{:S(2)}, u32[]{:S(2)}) collective-permute-start(bf16[64,2176]{1,0:T(8,128)(2,1)S(1)} %concatenate.9.refs_0_), channel_id=1, source_target_pairs={{0,8},{8,16},{16,24},{24,32},{32,40},{40,48},{48,56},{56,0},{1,9},... | collective-permute-start | bytes 835592 | tf_op jit(solution)/shard_map/ppermute | solution.py:31
  51.0 7.4 %collective-permute-start.8 = (bf16[64,2176]{1,0:T(8,128)(2,1)S(1)}, bf16[64,2176]{1,0:T(8,128)(2,1)S(1)}, u32[]{:S(2)}, u32[]{:S(2)}) collective-permute-start(bf16[64,2176]{1,0:T(8,128)(2,1)S(1)} %collective-permute-done.6.refs_2_), channel_id=1, source_target_pairs={{0,56},{8,0},{16,8},{24,16},{32,24},{40,32},{48,40},{56,48},{1,57}... | collective-permute-start | bytes 835592 | tf_op jit(solution)/shard_map/ppermute | solution.py:31
  54.0 7.9 %collective-permute-start.7 = (bf16[64,2176]{1,0:T(8,128)(2,1)S(1)}, bf16[64,2176]{1,0:T(8,128)(2,1)S(1)}, u32[]{:S(2)}, u32[]{:S(2)}) collective-permute-start(bf16[64,2176]{1,0:T(8,128)(2,1)S(1)} %collective-permute-done.5.refs_1_), channel_id=1, source_target_pairs={{0,8},{8,16},{16,24},{24,32},{32,40},{40,48},{48,56},{56,0},{1,9},... | collective-permute-start | bytes 835592 | tf_op jit(solution)/shard_map/ppermute | solution.py:31
  54.0 28.9 %collective-permute-start.13 = (bf16[1,2048,384]{2,1,0:T(8,128)(2,1)}, bf16[1,2048,384]{2,1,0:T(8,128)(2,1)}, u32[]{:S(2)}, u32[]{:S(2)}) collective-permute-start(bf16[1,2048,384]{2,1,0:T(8,128)(2,1)} %g0.1), channel_id=1, source_target_pairs={{0,1},{1,0},{2,3},{3,2},{4,5},{5,4},{6,7},{7,6},{8,9},{9,8},{10,11... | collective-permute-start | bytes 4718600 | tf_op jit(solution)/shard_map/ppermute | solution.py:35
  54.0 28.9 %collective-permute-start.14 = (bf16[1,2048,384]{2,1,0:T(8,128)(2,1)}, bf16[1,2048,384]{2,1,0:T(8,128)(2,1)}, u32[]{:S(2)}, u32[]{:S(2)}) collective-permute-start(bf16[1,2048,384]{2,1,0:T(8,128)(2,1)} %u0.1), channel_id=1, source_target_pairs={{0,1},{1,0},{2,3},{3,2},{4,5},{5,4},{6,7},{7,6},{8,9},{9,8},{10,11... | collective-permute-start | bytes 4718600 | tf_op jit(solution)/shard_map/ppermute | solution.py:35
  54.5 28.4 %collective-permute-start.15 = (bf16[1,384,2048]{2,1,0:T(8,128)(2,1)}, bf16[1,384,2048]{2,1,0:T(8,128)(2,1)}, u32[]{:S(2)}, u32[]{:S(2)}) collective-permute-start(bf16[1,384,2048]{2,1,0:T(8,128)(2,1)} %d0.1), channel_id=1, source_target_pairs={{0,1},{1,0},{2,3},{3,2},{4,5},{5,4},{6,7},{7,6},{8,9},{9,8},{10,11... | collective-permute-start | bytes 4718600 | tf_op jit(solution)/shard_map/ppermute | solution.py:35
  65.6 27.6 %all-to-all-start = ((bf16[16,24,2048]{2,1,0:T(8,128)(2,1)}), bf16[16,24,2048]{2,1,0:T(8,128)(2,1)}, u32[]{:S(2)}, u32[]{:S(2)}) async-start(bf16[16,24,2048]{2,1,0:T(8,128)(2,1)} %bitcast.25), calls=%async_computation | async-start | bytes 3145728 | tf_op jit(solution)/shard_map/all_to_all | solution.py:362
  73.4 7.1 %collective-permute-start.10 = (bf16[64,2176]{1,0:T(8,128)(2,1)S(1)}, bf16[64,2176]{1,0:T(8,128)(2,1)S(1)}, u32[]{:S(2)}, u32[]{:S(2)}) collective-permute-start(bf16[64,2176]{1,0:T(8,128)(2,1)S(1)} %collective-permute-done.8.refs_4_.refs_0_), channel_id=1, source_target_pairs={{0,56},{8,0},{16,8},{24,16},{32,24},{40,32},{48,40},{56,48},{1,57}... | collective-permute-start | bytes 835592 | tf_op jit(solution)/shard_map/ppermute | solution.py:31
  73.7 7.9 %collective-permute-start.9 = (bf16[64,2176]{1,0:T(8,128)(2,1)S(1)}, bf16[64,2176]{1,0:T(8,128)(2,1)S(1)}, u32[]{:S(2)}, u32[]{:S(2)}) collective-permute-start(bf16[64,2176]{1,0:T(8,128)(2,1)S(1)} %collective-permute-done.7.refs_3_), channel_id=1, source_target_pairs={{0,8},{8,16},{16,24},{24,32},{32,40},{40,48},{48,56},{56,0},{1,9},... | collective-permute-start | bytes 835592 | tf_op jit(solution)/shard_map/ppermute | solution.py:31
  80.6 7.3 %collective-permute-start.12 = (bf16[64,1152]{1,0:T(8,128)(2,1)S(1)}, bf16[64,1152]{1,0:T(8,128)(2,1)S(1)}, u32[]{:S(2)}, u32[]{:S(2)}) collective-permute-start(bf16[64,1152]{1,0:T(8,128)(2,1)S(1)} %slice.112), channel_id=1, source_target_pairs={{0,56},{8,0},{16,8},{24,16},{32,24},{40,32},{48,40},{56,48},{1,57}... | collective-permute-start | bytes 442376 | tf_op jit(solution)/shard_map/ppermute | solution.py:31
  93.2 18.2 %all-to-all-start.1 = ((bf16[16,16,2048]{2,1,0:T(8,128)(2,1)}), bf16[16,16,2048]{2,1,0:T(8,128)(2,1)}, u32[]{:S(2)}, u32[]{:S(2)}) async-start(bf16[16,16,2048]{2,1,0:T(8,128)(2,1)} %bitcast.9), calls=%async_computation.1 | async-start | bytes 2097152 | tf_op jit(solution)/shard_map/all_to_all | solution.py:362
  136.9 22.9 %all-to-all-start.3 = ((bf16[16,24,2048]{2,1,0:T(8,128)(2,1)}), bf16[16,24,2048]{2,1,0:T(8,128)(2,1)}, u32[]{:S(2)}, u32[]{:S(2)}) async-start(bf16[16,24,2048]{2,1,0:T(8,128)(2,1)} %bitcast.28), calls=%async_computation.3 | async-start | bytes 3145728 | tf_op jit(solution)/shard_map/all_to_all | solution.py:362
  148.0 6.4 %collective-permute-start.20 = (bf16[64,1024]{1,0:T(8,128)(2,1)S(1)}, bf16[64,1024]{1,0:T(8,128)(2,1)S(1)}, u32[]{:S(2)}, u32[]{:S(2)}) collective-permute-start(bf16[64,1024]{1,0:T(8,128)(2,1)S(1)} %get-tuple-element.62), channel_id=1, source_target_pairs={{0,56},{8,0},{16,8},{24,16},{32,24},{40,32},{48,40},{56,48},{1,57}... | collective-permute-start | bytes 393224 | tf_op jit(solution)/shard_map/ppermute | solution.py:31
  154.4 15.1 %collective-permute-start.21 = (bf16[64,2048]{1,0:T(8,128)(2,1)S(1)}, bf16[64,2048]{1,0:T(8,128)(2,1)S(1)}, u32[]{:S(2)}, u32[]{:S(2)}) collective-permute-start(bf16[64,2048]{1,0:T(8,128)(2,1)S(1)} %pad_maximum_fusion.1), channel_id=1, source_target_pairs={{0,56},{8,0},{16,8},{24,16},{32,24},{40,32},{48,40},{56,48},{1,57}... | collective-permute-start | bytes 786440 | tf_op jit(solution)/shard_map/ppermute | solution.py:31
  157.6 10.7 %collective-permute-start.17 = (bf16[64,2048]{1,0:T(8,128)(2,1)S(1)}, bf16[64,2048]{1,0:T(8,128)(2,1)S(1)}, u32[]{:S(2)}, u32[]{:S(2)}) collective-permute-start(bf16[64,2048]{1,0:T(8,128)(2,1)S(1)} %pad_maximum_fusion), channel_id=1, source_target_pairs={{0,8},{8,16},{16,24},{24,32},{32,40},{40,48},{48,56},{56,0},{1,9},... | collective-permute-start | bytes 786440 | tf_op jit(solution)/shard_map/ppermute | solution.py:31
  169.4 8.7 %collective-permute-start.18 = (bf16[64,2048]{1,0:T(8,128)(2,1)S(1)}, bf16[64,2048]{1,0:T(8,128)(2,1)S(1)}, u32[]{:S(2)}, u32[]{:S(2)}) collective-permute-start(bf16[64,2048]{1,0:T(8,128)(2,1)S(1)} %add_convert_fusion.4), channel_id=1, source_target_pairs={{0,8},{8,16},{16,24},{24,32},{32,40},{40,48},{48,56},{56,0},{1,9},... | collective-permute-start | bytes 786440 | tf_op jit(solution)/shard_map/ppermute | solution.py:31
  169.6 8.6 %collective-permute-start.22 = (bf16[64,2048]{1,0:T(8,128)(2,1)S(1)}, bf16[64,2048]{1,0:T(8,128)(2,1)S(1)}, u32[]{:S(2)}, u32[]{:S(2)}) collective-permute-start(bf16[64,2048]{1,0:T(8,128)(2,1)S(1)} %add_convert_fusion.2), channel_id=1, source_target_pairs={{0,56},{8,0},{16,8},{24,16},{32,24},{40,32},{48,40},{56,48},{1,57}... | collective-permute-start | bytes 786440 | tf_op jit(solution)/shard_map/ppermute | solution.py:31
  178.3 6.5 %collective-permute-start.23 = (bf16[64,2048]{1,0:T(8,128)(2,1)S(1)}, bf16[64,2048]{1,0:T(8,128)(2,1)S(1)}, u32[]{:S(2)}, u32[]{:S(2)}) collective-permute-start(bf16[64,2048]{1,0:T(8,128)(2,1)S(1)} %add_convert_fusion.1), channel_id=1, source_target_pairs={{0,56},{8,0},{16,8},{24,16},{32,24},{40,32},{48,40},{56,48},{1,57}... | collective-permute-start | bytes 786440 | tf_op jit(solution)/shard_map/ppermute | solution.py:31
  180.6 7.6 %collective-permute-start.19 = (bf16[64,2048]{1,0:T(8,128)(2,1)S(1)}, bf16[64,2048]{1,0:T(8,128)(2,1)S(1)}, u32[]{:S(2)}, u32[]{:S(2)}) collective-permute-start(bf16[64,2048]{1,0:T(8,128)(2,1)S(1)} %add_convert_fusion.3), channel_id=1, source_target_pairs={{0,8},{8,16},{16,24},{24,32},{32,40},{40,48},{48,56},{56,0},{1,9},... | collective-permute-start | bytes 786440 | tf_op jit(solution)/shard_map/ppermute | solution.py:31
  (13 other events, 116.4 us)

commit v6 on v5

--- a/solution.py
+++ b/solution.py
@@ -24,7 +24,7 @@
 F32 = jnp.float32
 masked_low = -1e30
 
-RING = (0, -1, 1, -2, 2, -3, 3, 4)
+RING = (0, -1, -2, 2, 1, -3, 3, 4)
 
 
 def shift(value, axis, size, by):
@@ -166,26 +166,26 @@
     )(where, queries, tails, key_rows, value_rows, lengths, late)
 
 
-def project(attn_theirs, attn_mine, out_weight):
-    theirs = jnp.dot(attn_theirs, out_weight, preferred_element_type=F32).astype(BF)
-    arrived = swap_cores(theirs)
+def project(attn_theirs, attn_mine, out_weight, other_weight):
+    arrived = swap_cores(attn_theirs)
     mine = lax.optimization_barrier(
         jnp.dot(attn_mine, out_weight, preferred_element_type=F32)
     )
-    both = (mine + arrived.astype(F32)).reshape(NY, ROWS, out_weight.shape[1])
+    both = mine + jnp.dot(arrived, other_weight, preferred_element_type=F32)
+    both = both.reshape(NY, ROWS, out_weight.shape[1])
     sent = both.astype(BF)
     moved = [shift(sent[k], "y", NY, k) for k in range(1, NY)]
     return both[0] + sum(block.astype(F32) for block in moved)
 
 
 def ring_gather(own, half):
+    blocks = {0: own}
     right = left = own
-    blocks = [own]
-    for _ in range(3):
-        right = shift(right, "z", NZ, 1)
-        left = shift(left, "z", NZ, -1)
-        blocks += [right, left]
-    return blocks + [shift(right[:, :half], "z", NZ, 1), shift(left[:, half:], "z", NZ, -1)]
+    for hops in (1, 2, 3):
+        right = blocks[-hops] = shift(right, "z", NZ, 1)
+        left = blocks[hops] = shift(left, "z", NZ, -1)
+    last = [shift(right[:, :half], "z", NZ, 1), shift(left[:, half:], "z", NZ, -1)]
+    return [blocks[offset] for offset in RING[:-1]] + last
 
 
 def add(a, b):
@@ -201,13 +201,11 @@
     return shift(right, "z", NZ, 1), shift(left, "z", NZ, -1)
 
 
-def ring_sum_near(right, left, blocks):
-    for step in (2, 1):
-        right = add(right, blocks[step])
-        own = lax.optimization_barrier((blocks[-step], right))[0]
-        left = add(left, own)
-        right, left = shift(right, "z", NZ, 1), shift(left, "z", NZ, -1)
-    return blocks[0].astype(F32) + right.astype(F32) + left.astype(F32)
+def ring_step(right, left, to_right, to_left):
+    right = add(right, to_right)
+    to_left = lax.optimization_barrier((to_left, right))[0]
+    left = add(left, to_left)
+    return right, left
 
 
 def dispatch_body(first_block, first_slot, z_ref, *refs):
@@ -388,11 +386,13 @@
     w_down,
 ):
     pairs = [(w, swap_cores(w)) for w in (w_gate, w_up, w_down)]
+    other_weight = swap_cores(out_weight)
     attn_theirs, attn_mine = attend(queries, key_rows, value_rows, doc_lengths)
-    mid = residual_in.astype(F32) + project(attn_theirs, attn_mine, out_weight)
+    mid = residual_in.astype(F32) + project(attn_theirs, attn_mine, out_weight, other_weight)
     spread = jnp.mean(mid * mid, axis=1, keepdims=True)
     normed = (mid * lax.rsqrt(spread + 1e-06) * norm_gain[None, :]).astype(BF)
 
+    normed, pairs = lax.optimization_barrier((normed, pairs))
     rows, width = normed.shape
     meta = jnp.concatenate(
         [
@@ -405,9 +405,8 @@
     blocks = ring_gather(jnp.concatenate([normed, meta], axis=1), width // 2)
     out_near, weight_near = dispatch(blocks[:NEAR], 0, 0, NEAR_SLOTS, width)
     arrived_near = exchange(out_near)
-    far_blocks, pairs = lax.optimization_barrier((blocks[NEAR - 1 :], pairs))
     out_far, weight_far = dispatch(
-        far_blocks, NEAR - 1, NEAR_SLOTS, SLOTS - NEAR_SLOTS, width
+        blocks[NEAR - 1 :], NEAR - 1, NEAR_SLOTS, SLOTS - NEAR_SLOTS, width
     )
     out_far, arrived_near = lax.optimization_barrier((out_far, arrived_near))
     arrived_far = exchange(out_far)
@@ -421,10 +420,20 @@
     far = weighted_sum(weight_far, returned_far).reshape(-1, ROWS, width)
     terms = {offset: far[1 + i].astype(BF) for i, offset in enumerate(RING[NEAR:])}
     right, left = ring_sum_far(terms)
-    near = weighted_sum(weight_near, returned_near)[: NEAR * ROWS].reshape(NEAR, ROWS, width)
-    terms = {offset: near[i].astype(BF) for i, offset in enumerate(RING[: NEAR - 1])}
-    terms[RING[NEAR - 1]] = (near[NEAR - 1] + far[0]).astype(BF)
-    expert_sum = ring_sum_near(right, left, terms)
+
+    def near_terms(first, rows):
+        picked = weight_near[:, first * ROWS : (first + 2) * ROWS]
+        return weighted_sum(picked, rows).reshape(2, ROWS, width)
+
+    to_left, to_right = near_terms(2, returned_near).astype(BF)
+    right, left = ring_step(right, left, to_right, to_left)
+    returned_near = lax.optimization_barrier((returned_near, right, left))[0]
+    right, left = shift(right, "z", NZ, 1), shift(left, "z", NZ, -1)
+    own, to_left = near_terms(0, returned_near)
+    to_right = near_terms(4, returned_near)[0] + far[0]
+    right, left = ring_step(right, left, to_right.astype(BF), to_left.astype(BF))
+    right, left = shift(right, "z", NZ, 1), shift(left, "z", NZ, -1)
+    expert_sum = own + right.astype(F32) + left.astype(F32)
     return (mid + expert_sum).astype(BF)
 
 

time: 190 us -> 193 us (1.016)
  waiting for transfers between devices: 68.5 us -> 56.2 us
  starting transfers between devices: 52.6 us -> 63.6 us
  blocking collectives: 16.9 us -> 20.8 us
    all_to_all x3, starting transfers between devices: 20.3 us -> 26.5 us  [exchange(): lax.all_to_all(rows.reshape(PLANE, count // PLANE, width), ('x', 'y'), sp...]
    all_to_all x3, waiting for transfers between devices: 6.63 us -> 0.98 us  [exchange(): lax.all_to_all(rows.reshape(PLANE, count // PLANE, width), ('x', 'y'), sp...]
    ppermute x19, waiting for transfers between devices: 57.1 us -> 52.4 us  [shift(): lax.ppermute(value, axis, [(i, (i + by) % size) for i in range(size)])]
    ppermute x19, starting transfers between devices: 27.7 us -> 32.4 us  [shift(): lax.ppermute(value, axis, [(i, (i + by) % size) for i in range(size)])]
    all_to_all x1, blocking collectives: 16.9 us -> 20.8 us  [exchange(): lax.all_to_all(rows.reshape(PLANE, count // PLANE, width), ('x', 'y'), sp...]
    dot_general x2 -> x4, matrix products: 5.43 us -> 5.39 us  [weighted_sum(): lax.dot_general(weights, rows, (((0,), (0,)), ((), ())), preferred_elemen...]
  transfers between devices with their start and end apart: 27 -> 28, of which waited for: 18 -> 15; matrix products, arithmetic and copies ran while one was open for 4% -> 7% of each run, Pallas kernels for 10% -> 11%
where the time goes in v6:
time: 193 us
  starting transfers between devices  63.6 us (33%)
  waiting for transfers between devices  56.2 us (29%)
  Pallas kernels  33.4 us (17%)
  blocking collectives  20.8 us (11%)
  matrix products  7.76 us (4%)
  local copies, waits for them, and re-layouts  5.61 us (3%)
  other arithmetic  5.06 us (3%)
    ppermute x19, waiting for transfers between devices, shift(): lax.ppermute(value, axis, [(i, (i + by) % size) for i in range(size)])  52.4 us
    ppermute x19, starting transfers between devices, shift(): lax.ppermute(value, axis, [(i, (i + by) % size) for i in range(size)])  32.4 us
    all_to_all x3, starting transfers between devices, exchange(): lax.all_to_all(rows.reshape(PLANE, count // PLANE, width), ('x', 'y'), sp...  26.5 us
    all_to_all x1, blocking collectives, exchange(): lax.all_to_all(rows.reshape(PLANE, count // PLANE, width), ('x', 'y'), sp...  20.8 us
    pallas_call x2, Pallas kernels, expert_rows(): pl.pallas_call(expert_body, out_shape=jax.ShapeDtypeStruct((count, width)...  18.6 us
    pallas_call x2, Pallas kernels, dispatch(): pl.pallas_call(functools.partial(dispatch_body, first_block, first_slot),...  6.65 us
    dot_general x4, matrix products, weighted_sum(): lax.dot_general(weights, rows, (((0,), (0,)), ((), ())), preferred_elemen...  5.39 us
    pallas_call x1, Pallas kernels, attend(): pl.pallas_call(early_body, out_shape=(jax.ShapeDtypeStruct((half, width),...  4.21 us
  transfers between devices with their start and end apart: 28, of which 15 were waited for; matrix products, arithmetic and copies ran while one was open for 7% of the time, Pallas kernels for 11%

profile of v6, /device:TPU:2, one launch (start us, length us, event | category | flops | bytes accessed | tf_op | source)
XLA Modules:
  0.0 192.7 jit_solution(8258204778472878546)
XLA Ops:
  0.9 3.8 %collective-permute-start = (bf16[2,256,128]{2,1,0:T(8,128)(2,1)S(1)}, bf16[2,256,128]{2,1,0:T(8,128)(2,1)S(1)}, u32[]{:S(2)}, u32[]{:S(2)}) collective-permute-start(bf16[2,256,128]{2,1,0:T(8,128)(2,1)S(1)} %pad_maximum_fusion.2), channel_id=1, source_target_pairs={{0,8},{8,16},{16,24},{24,32},{32,40},{40,48},{48,56},{56,64},{64,7... | collective-permute-start | bytes 393224 | tf_op jit(solution)/shard_map/ppermute | solution.py:40
  6.2 3.9 %shard_map.118.late_ref = bf16[256,512]{1,0:T(8,128)(2,1)} custom-call(s32[3]{0:T(128)} %pad_add_fusion.where, bf16[512,512]{1,0:T(8,128)(2,1)} %q_ref.3, bf16[512,512]{1,0:T(8,128)(2,1)} %kb.3, bf16[512,512]{1,0:T(8,128)(2,1)} %kb.3, bf16[512,512]{1,0:T(8,128)(2,1)} %vb.3, bf16[512,512]{1,0:T(8,128)(2,1)} %vb.3, s32[1,128]{1,0:T(1,128)} %bitcast.47), custom_call_target="tpu_custom_call" | custom-call | flops 1073741824 | bytes 786432 | tf_op jit(solution)/shard_map/pallas_call | solution.py:121
  13.5 4.2 %shard_map.119 = (bf16[256,512]{1,0:T(8,128)(2,1)}, bf16[256,512]{1,0:T(8,128)(2,1)}) custom-call(s32[3]{0:T(128)} %pad_add_fusion.where, bf16[512,512]{1,0:T(8,128)(2,1)} %q_ref.3, bf16[2,256,128]{2,1,0:T(8,128)(2,1)} %copy-done.8, bf16[512,512]{1,0:T(8,128)(2,1)} %kb.3, bf16[512,512]{1,0:T(8,128)(2,1)} %vb.3, s32[1,128]{1,0:T(1,128)} %bitcast.48, ...), custom_call_target="tpu_custom_call" | custom-call | flops 1073741824 | bytes 1048576 | tf_op jit(solution)/shard_map/pallas_call | solution.py:142
  25.8 5.5 %collective-permute-done.3 = bf16[64,2048]{1,0:T(8,128)(2,1)S(1)} collective-permute-done((bf16[64,2048]{1,0:T(8,128)(2,1)S(1)}, bf16[64,2048]{1,0:T(8,128)(2,1)S(1)}, u32[]{:S(2)}, u32[]{:S(2)}) %collective-permute-start.3) | collective-permute-done | bytes 262176 | tf_op jit(solution)/shard_map/ppermute | solution.py:31
  33.7 4.4 %collective-permute-done.4 = bf16[64,2048]{1,0:T(8,128)(2,1)S(1)} collective-permute-done((bf16[64,2048]{1,0:T(8,128)(2,1)}, bf16[64,2048]{1,0:T(8,128)(2,1)S(1)}, u32[]{:S(2)}, u32[]{:S(2)}) %collective-permute-start.4) | collective-permute-done | bytes 262176 | tf_op jit(solution)/shard_map/ppermute | solution.py:31
  44.7 5.4 %collective-permute-done.9.refs_1_ = bf16[64,2176]{1,0:T(8,128)(2,1)S(1)} collective-permute-done((bf16[64,2176]{1,0:T(8,128)(2,1)S(1)}, bf16[64,2176]{1,0:T(8,128)(2,1)S(1)}, u32[]{:S(2)}, u32[]{:S(2)}) %collective-permute-start.9) | collective-permute-done | bytes 278560 | tf_op jit(solution)/shard_map/ppermute | solution.py:31
  50.1 3.2 %collective-permute-start.12 = (bf16[64,2176]{1,0:T(8,128)(2,1)S(1)}, bf16[64,2176]{1,0:T(8,128)(2,1)S(1)}, u32[]{:S(2)}, u32[]{:S(2)}) collective-permute-start(bf16[64,2176]{1,0:T(8,128)(2,1)S(1)} %collective-permute-done.11.refs_4_.refs_0_), channel_id=1, source_target_pairs={{0,56},{8,0},{16,8},{24,16},{32,24},{40,32},{48,40},{56,48},{1,57}... | collective-permute-start | bytes 835592 | tf_op jit(solution)/shard_map/ppermute | solution.py:31
  53.3 4.5 %collective-permute-done.10.refs_2_ = bf16[64,2176]{1,0:T(8,128)(2,1)S(1)} collective-permute-done((bf16[64,2176]{1,0:T(8,128)(2,1)S(1)}, bf16[64,2176]{1,0:T(8,128)(2,1)S(1)}, u32[]{:S(2)}, u32[]{:S(2)}) %collective-permute-start.10) | collective-permute-done | bytes 278560 | tf_op jit(solution)/shard_map/ppermute | solution.py:31
  57.9 3.7 %shard_map.120 = (bf16[384,2048]{1,0:T(8,128)(2,1)}, bf16[384,384]{1,0:T(8,128)(2,1)S(1)}) custom-call(s32[1]{0:T(128)} %bitcast.6.z_ref, bf16[64,2176]{1,0:T(8,128)(2,1)S(1)} %concatenate.9.refs_0_, bf16[64,2176]{1,0:T(8,128)(2,1)S(1)} %collective-permute-done.9.refs_1_, bf16[64,2176]{1,0:T(8,128)(2,1)S(1)} %collective-permute-done.10.refs_2_, ...), custom_call_target="tpu_custom_call" | custom-call | flops 603979776 | bytes 3145728 | tf_op jit(solution)/shard_map/pallas_call | solution.py:273
  61.6 11.4 %all-to-all-start = ((bf16[16,24,2048]{2,1,0:T(8,128)(2,1)}), bf16[16,24,2048]{2,1,0:T(8,128)(2,1)}, u32[]{:S(2)}, u32[]{:S(2)}) async-start(bf16[16,24,2048]{2,1,0:T(8,128)(2,1)} %bitcast.7), calls=%async_computation | async-start | bytes 3145728 | tf_op jit(solution)/shard_map/all_to_all | solution.py:360
  72.9 3.2 %collective-permute-start.14 = (bf16[64,2176]{1,0:T(8,128)(2,1)S(1)}, bf16[64,2176]{1,0:T(8,128)(2,1)S(1)}, u32[]{:S(2)}, u32[]{:S(2)}) collective-permute-start(bf16[64,2176]{1,0:T(8,128)(2,1)S(1)} %collective-permute-done.12.refs_3_), channel_id=1, source_target_pairs={{0,56},{8,0},{16,8},{24,16},{32,24},{40,32},{48,40},{56,48},{1,57}... | collective-permute-start | bytes 835592 | tf_op jit(solution)/shard_map/ppermute | solution.py:31
  76.2 4.1 %collective-permute-done.14.refs_2_ = bf16[64,2176]{1,0:T(8,128)(2,1)S(1)} collective-permute-done((bf16[64,2176]{1,0:T(8,128)(2,1)S(1)}, bf16[64,2176]{1,0:T(8,128)(2,1)S(1)}, u32[]{:S(2)}, u32[]{:S(2)}) %collective-permute-start.14) | collective-permute-done | bytes 278560 | tf_op jit(solution)/shard_map/ppermute | solution.py:31
  80.2 3.8 %collective-permute-start.16 = (bf16[64,1152]{1,0:T(8,128)(2,1)S(1)}, bf16[64,1152]{1,0:T(8,128)(2,1)S(1)}, u32[]{:S(2)}, u32[]{:S(2)}) collective-permute-start(bf16[64,1152]{1,0:T(8,128)(2,1)S(1)} %slice.99), channel_id=1, source_target_pairs={{0,56},{8,0},{16,8},{24,16},{32,24},{40,32},{48,40},{56,48},{1,57}... | collective-permute-start | bytes 442376 | tf_op jit(solution)/shard_map/ppermute | solution.py:31
  84.1 6.2 %collective-permute-done.15.refs_3_ = bf16[64,1024]{1,0:T(8,128)(2,1)S(1)} collective-permute-done((bf16[64,1024]{1,0:T(8,128)(2,1)S(1)}, bf16[64,1024]{1,0:T(8,128)(2,1)S(1)}, u32[]{:S(2)}, u32[]{:S(2)}) %collective-permute-start.15) | collective-permute-done | bytes 131104 | tf_op jit(solution)/shard_map/ppermute | solution.py:31
  93.2 7.2 %all-to-all-start.1 = ((bf16[16,16,2048]{2,1,0:T(8,128)(2,1)}), bf16[16,16,2048]{2,1,0:T(8,128)(2,1)S(1)}, u32[]{:S(2)}, u32[]{:S(2)}) async-start(bf16[16,16,2048]{2,1,0:T(8,128)(2,1)} %bitcast.9), calls=%async_computation.1 | async-start | bytes 2097152 | tf_op jit(solution)/shard_map/all_to_all | solution.py:360
  100.4 10.0 %shard_map.122 = bf16[384,2048]{1,0:T(8,128)(2,1)} custom-call(bf16[384,2048]{1,0:T(8,128)(2,1)} %bitcast.8.rows_ref, bf16[1,2048,384]{2,1,0:T(8,128)(2,1)} %g0.1, bf16[1,2048,384]{2,1,0:T(8,128)(2,1)} %collective-permute-done.6.g1, bf16[1,2048,384]{2,1,0:T(8,128)(2,1)} %u0.1, bf16[1,2048,384]{2,1,0:T(8,128)(2,1)} %collective-permute-done.7.u1, ...), custom_call_target="tpu_custom_call" | custom-call | flops 3623878656 | bytes 12582912 | tf_op jit(solution)/shard_map/pallas_call | solution.py:337
  112.5 8.6 %shard_map.123 = bf16[256,2048]{1,0:T(8,128)(2,1)} custom-call(bf16[256,2048]{1,0:T(8,128)(2,1)} %bitcast.43, bf16[1,2048,384]{2,1,0:T(8,128)(2,1)} %g0.1, bf16[1,2048,384]{2,1,0:T(8,128)(2,1)} %collective-permute-done.6.g1, bf16[1,2048,384]{2,1,0:T(8,128)(2,1)} %u0.1, bf16[1,2048,384]{2,1,0:T(8,128)(2,1)} %collective-permute-done.7.u1, ...), custom_call_target="tpu_custom_call" | custom-call | flops 2415919104 | bytes 11534336 | tf_op jit(solution)/shard_map/pallas_call | solution.py:337
  121.1 20.8 %all_to_all.20 = bf16[16,16,2048]{2,1,0:T(8,128)(2,1)} all-to-all(bf16[16,16,2048]{2,1,0:T(8,128)(2,1)} %bitcast.44), channel_id=1, replica_groups=mesh['x'=4,'z'=8,'y'=4,'c'=2] {'x','y'}, dimensions={0} | all-to-all | bytes 2097152 | tf_op jit(solution)/shard_map/all_to_all | solution.py:360
  141.9 8.0 %all-to-all-start.3 = ((bf16[16,24,2048]{2,1,0:T(8,128)(2,1)}), bf16[16,24,2048]{2,1,0:T(8,128)(2,1)S(1)}, u32[]{:S(2)}, u32[]{:S(2)}) async-start(bf16[16,24,2048]{2,1,0:T(8,128)(2,1)} %bitcast.45), calls=%async_computation.3 | async-start | bytes 3145728 | tf_op jit(solution)/shard_map/all_to_all | solution.py:360
  161.2 3.3 %collective-permute-start.20 = (bf16[64,2048]{1,0:T(8,128)(2,1)S(1)}, bf16[64,2048]{1,0:T(8,128)(2,1)S(1)}, u32[]{:S(2)}, u32[]{:S(2)}) collective-permute-start(bf16[64,2048]{1,0:T(8,128)(2,1)S(1)} %pad_maximum_fusion.1), channel_id=1, source_target_pairs={{0,56},{8,0},{16,8},{24,16},{32,24},{40,32},{48,40},{56,48},{1,57}... | collective-permute-start | bytes 786440 | tf_op jit(solution)/shard_map/ppermute | solution.py:31
  165.7 7.3 %collective-permute-done.18 = bf16[64,2048]{1,0:T(8,128)(2,1)S(1)} collective-permute-done((bf16[64,2048]{1,0:T(8,128)(2,1)}, bf16[64,2048]{1,0:T(8,128)(2,1)S(1)}, u32[]{:S(2)}, u32[]{:S(2)}) %collective-permute-start.18) | collective-permute-done | bytes 262176 | tf_op jit(solution)/shard_map/ppermute | solution.py:31
  173.3 3.3 %collective-permute-start.23 = (bf16[64,2048]{1,0:T(8,128)(2,1)S(1)}, bf16[64,2048]{1,0:T(8,128)(2,1)S(1)}, u32[]{:S(2)}, u32[]{:S(2)}) collective-permute-start(bf16[64,2048]{1,0:T(8,128)(2,1)S(1)} %add_convert_fusion.2), channel_id=1, source_target_pairs={{0,56},{8,0},{16,8},{24,16},{32,24},{40,32},{48,40},{56,48},{1,57}... | collective-permute-start | bytes 786440 | tf_op jit(solution)/shard_map/ppermute | solution.py:31
  177.1 3.6 %collective-permute-done.21 = bf16[64,2048]{1,0:T(8,128)(2,1)S(1)} collective-permute-done((bf16[64,2048]{1,0:T(8,128)(2,1)S(1)}, bf16[64,2048]{1,0:T(8,128)(2,1)S(1)}, u32[]{:S(2)}, u32[]{:S(2)}) %collective-permute-start.21) | collective-permute-done | bytes 262176 | tf_op jit(solution)/shard_map/ppermute | solution.py:31
  184.4 4.3 %collective-permute-done.24 = bf16[64,2048]{1,0:T(8,128)(2,1)S(1)} collective-permute-done((bf16[64,2048]{1,0:T(8,128)(2,1)S(1)}, bf16[64,2048]{1,0:T(8,128)(2,1)S(1)}, u32[]{:S(2)}, u32[]{:S(2)}) %collective-permute-start.24) | collective-permute-done | bytes 262176 | tf_op jit(solution)/shard_map/ppermute | solution.py:31
  (91 shorter events, 48.7 us)
Async XLA Ops:
  0.0 19.4 %collective-permute-start.2 = (bf16[512,2048]{1,0:T(8,128)(2,1)}, bf16[512,2048]{1,0:T(8,128)(2,1)S(1)}, u32[]{:S(2)}, u32[]{:S(2)}) collective-permute-start(bf16[512,2048]{1,0:T(8,128)(2,1)} %param.17), channel_id=1, source_target_pairs={{0,1},{1,0},{2,3},{3,2},{4,5},{5,4},{6,7},{7,6},{8,9},{9,8},{10,11... | collective-permute-start | bytes 6291464 | tf_op jit(solution)/shard_map/ppermute | solution.py:35
  0.9 11.9 %collective-permute-start = (bf16[2,256,128]{2,1,0:T(8,128)(2,1)S(1)}, bf16[2,256,128]{2,1,0:T(8,128)(2,1)S(1)}, u32[]{:S(2)}, u32[]{:S(2)}) collective-permute-start(bf16[2,256,128]{2,1,0:T(8,128)(2,1)S(1)} %pad_maximum_fusion.2), channel_id=1, source_target_pairs={{0,8},{8,16},{16,24},{24,32},{32,40},{40,48},{48,56},{56,64},{64,7... | collective-permute-start | bytes 393224 | tf_op jit(solution)/shard_map/ppermute | solution.py:40
  4.7 36.5 %collective-permute-start.6 = (bf16[1,2048,384]{2,1,0:T(8,128)(2,1)}, bf16[1,2048,384]{2,1,0:T(8,128)(2,1)}, u32[]{:S(2)}, u32[]{:S(2)}) collective-permute-start(bf16[1,2048,384]{2,1,0:T(8,128)(2,1)} %g0.1), channel_id=1, source_target_pairs={{0,1},{1,0},{2,3},{3,2},{4,5},{5,4},{6,7},{7,6},{8,9},{9,8},{10,11... | collective-permute-start | bytes 4718600 | tf_op jit(solution)/shard_map/ppermute | solution.py:35
  5.1 36.2 %collective-permute-start.7 = (bf16[1,2048,384]{2,1,0:T(8,128)(2,1)}, bf16[1,2048,384]{2,1,0:T(8,128)(2,1)}, u32[]{:S(2)}, u32[]{:S(2)}) collective-permute-start(bf16[1,2048,384]{2,1,0:T(8,128)(2,1)} %u0.1), channel_id=1, source_target_pairs={{0,1},{1,0},{2,3},{3,2},{4,5},{5,4},{6,7},{7,6},{8,9},{9,8},{10,11... | collective-permute-start | bytes 4718600 | tf_op jit(solution)/shard_map/ppermute | solution.py:35
  5.3 35.9 %collective-permute-start.8 = (bf16[1,384,2048]{2,1,0:T(8,128)(2,1)}, bf16[1,384,2048]{2,1,0:T(8,128)(2,1)}, u32[]{:S(2)}, u32[]{:S(2)}) collective-permute-start(bf16[1,384,2048]{2,1,0:T(8,128)(2,1)} %d0.1), channel_id=1, source_target_pairs={{0,1},{1,0},{2,3},{3,2},{4,5},{5,4},{6,7},{7,6},{8,9},{9,8},{10,11... | collective-permute-start | bytes 4718600 | tf_op jit(solution)/shard_map/ppermute | solution.py:35
  21.3 9.9 %collective-permute-start.3 = (bf16[64,2048]{1,0:T(8,128)(2,1)S(1)}, bf16[64,2048]{1,0:T(8,128)(2,1)S(1)}, u32[]{:S(2)}, u32[]{:S(2)}) collective-permute-start(bf16[64,2048]{1,0:T(8,128)(2,1)S(1)} %get-tuple-element.59), channel_id=1, source_target_pairs={{0,2},{2,4},{4,6},{6,0},{1,3},{3,5},{5,7},{7,1},{8,10},{10,12},{12... | collective-permute-start | bytes 786440 | tf_op jit(solution)/shard_map/ppermute | solution.py:31
  22.9 15.2 %collective-permute-start.4 = (bf16[64,2048]{1,0:T(8,128)(2,1)}, bf16[64,2048]{1,0:T(8,128)(2,1)S(1)}, u32[]{:S(2)}, u32[]{:S(2)}) collective-permute-start(bf16[64,2048]{1,0:T(8,128)(2,1)} %get-tuple-element.61), channel_id=1, source_target_pairs={{0,4},{2,6},{4,0},{6,2},{1,5},{3,7},{5,1},{7,3},{8,12},{10,14},{12... | collective-permute-start | bytes 786440 | tf_op jit(solution)/shard_map/ppermute | solution.py:31
  31.2 7.9 %collective-permute-start.5 = (bf16[64,2048]{1,0:T(8,128)(2,1)S(1)}, bf16[64,2048]{1,0:T(8,128)(2,1)S(1)}, u32[]{:S(2)}, u32[]{:S(2)}) collective-permute-start(bf16[64,2048]{1,0:T(8,128)(2,1)S(1)} %get-tuple-element.60), channel_id=1, source_target_pairs={{0,6},{2,0},{4,2},{6,4},{1,7},{3,1},{5,3},{7,5},{8,14},{10,8},{12,... | collective-permute-start | bytes 786440 | tf_op jit(solution)/shard_map/ppermute | solution.py:31
  41.4 8.7 %collective-permute-start.9 = (bf16[64,2176]{1,0:T(8,128)(2,1)S(1)}, bf16[64,2176]{1,0:T(8,128)(2,1)S(1)}, u32[]{:S(2)}, u32[]{:S(2)}) collective-permute-start(bf16[64,2176]{1,0:T(8,128)(2,1)S(1)} %concatenate.9.refs_0_), channel_id=1, source_target_pairs={{0,8},{8,16},{16,24},{24,32},{32,40},{40,48},{48,56},{56,0},{1,9},... | collective-permute-start | bytes 835592 | tf_op jit(solution)/shard_map/ppermute | solution.py:31
  41.5 8.6 %collective-permute-start.11 = (bf16[64,2176]{1,0:T(8,128)(2,1)S(1)}, bf16[64,2176]{1,0:T(8,128)(2,1)S(1)}, u32[]{:S(2)}, u32[]{:S(2)}) collective-permute-start(bf16[64,2176]{1,0:T(8,128)(2,1)S(1)} %concatenate.9.refs_0_), channel_id=1, source_target_pairs={{0,56},{8,0},{16,8},{24,16},{32,24},{40,32},{48,40},{56,48},{1,57}... | collective-permute-start | bytes 835592 | tf_op jit(solution)/shard_map/ppermute | solution.py:31
  50.1 7.8 %collective-permute-start.10 = (bf16[64,2176]{1,0:T(8,128)(2,1)S(1)}, bf16[64,2176]{1,0:T(8,128)(2,1)S(1)}, u32[]{:S(2)}, u32[]{:S(2)}) collective-permute-start(bf16[64,2176]{1,0:T(8,128)(2,1)S(1)} %collective-permute-done.9.refs_1_), channel_id=1, source_target_pairs={{0,8},{8,16},{16,24},{24,32},{32,40},{40,48},{48,56},{56,0},{1,9},... | collective-permute-start | bytes 835592 | tf_op jit(solution)/shard_map/ppermute | solution.py:31
  50.1 7.8 %collective-permute-start.12 = (bf16[64,2176]{1,0:T(8,128)(2,1)S(1)}, bf16[64,2176]{1,0:T(8,128)(2,1)S(1)}, u32[]{:S(2)}, u32[]{:S(2)}) collective-permute-start(bf16[64,2176]{1,0:T(8,128)(2,1)S(1)} %collective-permute-done.11.refs_4_.refs_0_), channel_id=1, source_target_pairs={{0,56},{8,0},{16,8},{24,16},{32,24},{40,32},{48,40},{56,48},{1,57}... | collective-permute-start | bytes 835592 | tf_op jit(solution)/shard_map/ppermute | solution.py:31
  61.6 31.7 %all-to-all-start = ((bf16[16,24,2048]{2,1,0:T(8,128)(2,1)}), bf16[16,24,2048]{2,1,0:T(8,128)(2,1)}, u32[]{:S(2)}, u32[]{:S(2)}) async-start(bf16[16,24,2048]{2,1,0:T(8,128)(2,1)} %bitcast.7), calls=%async_computation | async-start | bytes 3145728 | tf_op jit(solution)/shard_map/all_to_all | solution.py:360
  72.9 7.3 %collective-permute-start.14 = (bf16[64,2176]{1,0:T(8,128)(2,1)S(1)}, bf16[64,2176]{1,0:T(8,128)(2,1)S(1)}, u32[]{:S(2)}, u32[]{:S(2)}) collective-permute-start(bf16[64,2176]{1,0:T(8,128)(2,1)S(1)} %collective-permute-done.12.refs_3_), channel_id=1, source_target_pairs={{0,56},{8,0},{16,8},{24,16},{32,24},{40,32},{48,40},{56,48},{1,57}... | collective-permute-start | bytes 835592 | tf_op jit(solution)/shard_map/ppermute | solution.py:31
  76.2 7.9 %collective-permute-start.13 = (bf16[64,2176]{1,0:T(8,128)(2,1)S(1)}, bf16[64,2176]{1,0:T(8,128)(2,1)S(1)}, u32[]{:S(2)}, u32[]{:S(2)}) collective-permute-start(bf16[64,2176]{1,0:T(8,128)(2,1)S(1)} %collective-permute-done.10.refs_2_), channel_id=1, source_target_pairs={{0,8},{8,16},{16,24},{24,32},{32,40},{40,48},{48,56},{56,0},{1,9},... | collective-permute-start | bytes 835592 | tf_op jit(solution)/shard_map/ppermute | solution.py:31
  80.2 10.0 %collective-permute-start.16 = (bf16[64,1152]{1,0:T(8,128)(2,1)S(1)}, bf16[64,1152]{1,0:T(8,128)(2,1)S(1)}, u32[]{:S(2)}, u32[]{:S(2)}) collective-permute-start(bf16[64,1152]{1,0:T(8,128)(2,1)S(1)} %slice.99), channel_id=1, source_target_pairs={{0,56},{8,0},{16,8},{24,16},{32,24},{40,32},{48,40},{56,48},{1,57}... | collective-permute-start | bytes 442376 | tf_op jit(solution)/shard_map/ppermute | solution.py:31
  93.2 18.2 %all-to-all-start.1 = ((bf16[16,16,2048]{2,1,0:T(8,128)(2,1)}), bf16[16,16,2048]{2,1,0:T(8,128)(2,1)S(1)}, u32[]{:S(2)}, u32[]{:S(2)}) async-start(bf16[16,16,2048]{2,1,0:T(8,128)(2,1)} %bitcast.9), calls=%async_computation.1 | async-start | bytes 2097152 | tf_op jit(solution)/shard_map/all_to_all | solution.py:360
  141.9 23.4 %all-to-all-start.3 = ((bf16[16,24,2048]{2,1,0:T(8,128)(2,1)}), bf16[16,24,2048]{2,1,0:T(8,128)(2,1)S(1)}, u32[]{:S(2)}, u32[]{:S(2)}) async-start(bf16[16,24,2048]{2,1,0:T(8,128)(2,1)} %bitcast.45), calls=%async_computation.3 | async-start | bytes 3145728 | tf_op jit(solution)/shard_map/all_to_all | solution.py:360
  161.2 12.0 %collective-permute-start.20 = (bf16[64,2048]{1,0:T(8,128)(2,1)S(1)}, bf16[64,2048]{1,0:T(8,128)(2,1)S(1)}, u32[]{:S(2)}, u32[]{:S(2)}) collective-permute-start(bf16[64,2048]{1,0:T(8,128)(2,1)S(1)} %pad_maximum_fusion.1), channel_id=1, source_target_pairs={{0,56},{8,0},{16,8},{24,16},{32,24},{40,32},{48,40},{56,48},{1,57}... | collective-permute-start | bytes 786440 | tf_op jit(solution)/shard_map/ppermute | solution.py:31
  165.3 7.8 %collective-permute-start.18 = (bf16[64,2048]{1,0:T(8,128)(2,1)}, bf16[64,2048]{1,0:T(8,128)(2,1)S(1)}, u32[]{:S(2)}, u32[]{:S(2)}) collective-permute-start(bf16[64,2048]{1,0:T(8,128)(2,1)} %pad_maximum_fusion), channel_id=1, source_target_pairs={{0,8},{8,16},{16,24},{24,32},{32,40},{40,48},{48,56},{56,0},{1,9},... | collective-permute-start | bytes 786440 | tf_op jit(solution)/shard_map/ppermute | solution.py:31
  173.1 7.7 %collective-permute-start.21 = (bf16[64,2048]{1,0:T(8,128)(2,1)S(1)}, bf16[64,2048]{1,0:T(8,128)(2,1)S(1)}, u32[]{:S(2)}, u32[]{:S(2)}) collective-permute-start(bf16[64,2048]{1,0:T(8,128)(2,1)S(1)} %fusion.5), channel_id=1, source_target_pairs={{0,8},{8,16},{16,24},{24,32},{32,40},{40,48},{48,56},{56,0},{1,9},... | collective-permute-start | bytes 786440 | tf_op jit(solution)/shard_map/ppermute | solution.py:31
  173.3 8.9 %collective-permute-start.23 = (bf16[64,2048]{1,0:T(8,128)(2,1)S(1)}, bf16[64,2048]{1,0:T(8,128)(2,1)S(1)}, u32[]{:S(2)}, u32[]{:S(2)}) collective-permute-start(bf16[64,2048]{1,0:T(8,128)(2,1)S(1)} %add_convert_fusion.2), channel_id=1, source_target_pairs={{0,56},{8,0},{16,8},{24,16},{32,24},{40,32},{48,40},{56,48},{1,57}... | collective-permute-start | bytes 786440 | tf_op jit(solution)/shard_map/ppermute | solution.py:31
  182.3 6.5 %collective-permute-start.24 = (bf16[64,2048]{1,0:T(8,128)(2,1)S(1)}, bf16[64,2048]{1,0:T(8,128)(2,1)S(1)}, u32[]{:S(2)}, u32[]{:S(2)}) collective-permute-start(bf16[64,2048]{1,0:T(8,128)(2,1)S(1)} %add_convert_fusion), channel_id=1, source_target_pairs={{0,56},{8,0},{16,8},{24,16},{32,24},{40,32},{48,40},{56,48},{1,57}... | collective-permute-start | bytes 786440 | tf_op jit(solution)/shard_map/ppermute | solution.py:31
  184.3 7.6 %collective-permute-start.22 = (bf16[64,2048]{1,0:T(8,128)(2,1)S(1)}, bf16[64,2048]{1,0:T(8,128)(2,1)S(1)}, u32[]{:S(2)}, u32[]{:S(2)}) collective-permute-start(bf16[64,2048]{1,0:T(8,128)(2,1)S(1)} %add_convert_fusion.1), channel_id=1, source_target_pairs={{0,8},{8,16},{16,24},{24,32},{32,40},{40,48},{48,56},{56,0},{1,9},... | collective-permute-start | bytes 786440 | tf_op jit(solution)/shard_map/ppermute | solution.py:31
  (13 other events, 98.4 us)

commit v7 on v6

--- a/solution.py
+++ b/solution.py
@@ -190,15 +190,6 @@
 
 def add(a, b):
     return (a.astype(F32) + b.astype(F32)).astype(BF)
-
-
-def ring_sum_far(blocks):
-    half = blocks[4].shape[1] // 2
-    a = shift(blocks[4][:, :half], "z", NZ, 1)
-    b = shift(blocks[4][:, half:], "z", NZ, -1)
-    right = jnp.concatenate([add(blocks[3][:, :half], a), blocks[3][:, half:]], axis=1)
-    left = jnp.concatenate([blocks[-3][:, :half], add(blocks[-3][:, half:], b)], axis=1)
-    return shift(right, "z", NZ, 1), shift(left, "z", NZ, -1)
 
 
 def ring_step(right, left, to_right, to_left):
@@ -388,11 +379,11 @@
     pairs = [(w, swap_cores(w)) for w in (w_gate, w_up, w_down)]
     other_weight = swap_cores(out_weight)
     attn_theirs, attn_mine = attend(queries, key_rows, value_rows, doc_lengths)
+    attn_theirs, attn_mine, pairs = lax.optimization_barrier((attn_theirs, attn_mine, pairs))
     mid = residual_in.astype(F32) + project(attn_theirs, attn_mine, out_weight, other_weight)
     spread = jnp.mean(mid * mid, axis=1, keepdims=True)
     normed = (mid * lax.rsqrt(spread + 1e-06) * norm_gain[None, :]).astype(BF)
 
-    normed, pairs = lax.optimization_barrier((normed, pairs))
     rows, width = normed.shape
     meta = jnp.concatenate(
         [
@@ -417,20 +408,30 @@
     returned_far = exchange(pair_far)
     returned_far, pair_near = lax.optimization_barrier((returned_far, pair_near))
     returned_near = exchange(pair_near)
-    far = weighted_sum(weight_far, returned_far).reshape(-1, ROWS, width)
-    terms = {offset: far[1 + i].astype(BF) for i, offset in enumerate(RING[NEAR:])}
-    right, left = ring_sum_far(terms)
-
-    def near_terms(first, rows):
-        picked = weight_near[:, first * ROWS : (first + 2) * ROWS]
+
+    def terms(weights, first, rows):
+        picked = weights[:, first * ROWS : (first + 2) * ROWS]
         return weighted_sum(picked, rows).reshape(2, ROWS, width)
 
-    to_left, to_right = near_terms(2, returned_near).astype(BF)
+    half = width // 2
+    to_right, farthest = terms(weight_far, 2, returned_far).astype(BF)
+    returned_far, farthest = lax.optimization_barrier((returned_far, farthest))
+    right = shift(farthest[:, :half], "z", NZ, 1)
+    left = shift(farthest[:, half:], "z", NZ, -1)
+    early_right = shift(to_right[:, half:], "z", NZ, 1)
+    over, to_left = terms(weight_far, 0, returned_far)
+    to_left = to_left.astype(BF)
+    early_left = shift(to_left[:, :half], "z", NZ, -1)
+    right = shift(add(to_right[:, :half], right), "z", NZ, 1)
+    left = shift(add(to_left[:, half:], left), "z", NZ, -1)
+    right = jnp.concatenate([right, early_right], axis=1)
+    left = jnp.concatenate([early_left, left], axis=1)
+    to_left, to_right = terms(weight_near, 2, returned_near).astype(BF)
     right, left = ring_step(right, left, to_right, to_left)
     returned_near = lax.optimization_barrier((returned_near, right, left))[0]
     right, left = shift(right, "z", NZ, 1), shift(left, "z", NZ, -1)
-    own, to_left = near_terms(0, returned_near)
-    to_right = near_terms(4, returned_near)[0] + far[0]
+    own, to_left = terms(weight_near, 0, returned_near)
+    to_right = terms(weight_near, 4, returned_near)[0] + over
     right, left = ring_step(right, left, to_right.astype(BF), to_left.astype(BF))
     right, left = shift(right, "z", NZ, 1), shift(left, "z", NZ, -1)
     expert_sum = own + right.astype(F32) + left.astype(F32)

time: 193 us -> 184 us (0.953); the launches traced: 193 us -> 182 us
  starting transfers between devices: 63.6 us -> 57.5 us
  waiting for transfers between devices: 56.2 us -> 61.3 us
  blocking collectives: 20.8 us -> 16.5 us
  other arithmetic: 5.06 us -> 2.39 us
  matrix products: 7.76 us -> 5.38 us
    all_to_all x3, starting transfers between devices: 26.5 us -> 20.2 us  [exchange(): lax.all_to_all(rows.reshape(PLANE, count // PLANE, width), ('x', 'y'), sp...]
    all_to_all x1, blocking collectives: 20.8 us -> 16.5 us  [exchange(): lax.all_to_all(rows.reshape(PLANE, count // PLANE, width), ('x', 'y'), sp...]
    all_to_all x3, waiting for transfers between devices: 0.98 us -> 4.22 us  [exchange(): lax.all_to_all(rows.reshape(PLANE, count // PLANE, width), ('x', 'y'), sp...]
    dot_general x4 -> x5, matrix products: 5.39 us -> 2.99 us  [weighted_sum(): lax.dot_general(weights, rows, (((0,), (0,)), ((), ())), preferred_elemen...]
    ppermute x19 -> x21, waiting for transfers between devices: 52.4 us -> 53.9 us  [shift(): lax.ppermute(value, axis, [(i, (i + by) % size) for i in range(size)])]
    ppermute x19 -> x21, starting transfers between devices: 32.4 us -> 32.4 us  [shift(): lax.ppermute(value, axis, [(i, (i + by) % size) for i in range(size)])]
  transfers between devices with their start and end apart: 28 -> 30, of which waited for: 15 -> 15; matrix products, arithmetic and copies ran while one was open for 7% -> 4% of each run, Pallas kernels for 11% -> 12%
where the time goes in v7:
time: 184 us; the launch traced here: 182 us
  waiting for transfers between devices  61.3 us (33%)
  starting transfers between devices  57.5 us (31%)
  Pallas kernels  33.4 us (18%)
  blocking collectives  16.5 us (9%)
  matrix products  5.38 us (3%)
  local copies, waits for them, and re-layouts  4.67 us (3%)
  other arithmetic  2.39 us (1%)
    ppermute x21, waiting for transfers between devices, shift(): lax.ppermute(value, axis, [(i, (i + by) % size) for i in range(size)])  53.9 us
    ppermute x21, starting transfers between devices, shift(): lax.ppermute(value, axis, [(i, (i + by) % size) for i in range(size)])  32.4 us
    all_to_all x3, starting transfers between devices, exchange(): lax.all_to_all(rows.reshape(PLANE, count // PLANE, width), ('x', 'y'), sp...  20.2 us
    pallas_call x2, Pallas kernels, expert_rows(): pl.pallas_call(expert_body, out_shape=jax.ShapeDtypeStruct((count, width)...  18.7 us
    all_to_all x1, blocking collectives, exchange(): lax.all_to_all(rows.reshape(PLANE, count // PLANE, width), ('x', 'y'), sp...  16.5 us
    pallas_call x2, Pallas kernels, dispatch(): pl.pallas_call(functools.partial(dispatch_body, first_block, first_slot),...  6.62 us
    all_to_all x3, waiting for transfers between devices, exchange(): lax.all_to_all(rows.reshape(PLANE, count // PLANE, width), ('x', 'y'), sp...  4.22 us
    pallas_call x1, Pallas kernels, attend(): pl.pallas_call(early_body, out_shape=(jax.ShapeDtypeStruct((half, width),...  4.21 us
  transfers between devices with their start and end apart: 30, of which 15 were waited for; matrix products, arithmetic and copies ran while one was open for 4% of the time, Pallas kernels for 12%

profile of v7, /device:TPU:2, one launch (start us, length us, event | category | flops | bytes accessed | tf_op | source)
XLA Modules:
  0.0 181.5 jit_solution(3040895096309920321)
XLA Ops:
  1.9 3.8 %collective-permute-start = (bf16[2,256,128]{2,1,0:T(8,128)(2,1)S(1)}, bf16[2,256,128]{2,1,0:T(8,128)(2,1)S(1)}, u32[]{:S(2)}, u32[]{:S(2)}) collective-permute-start(bf16[2,256,128]{2,1,0:T(8,128)(2,1)S(1)} %pad_maximum_fusion), channel_id=1, source_target_pairs={{0,8},{8,16},{16,24},{24,32},{32,40},{40,48},{48,56},{56,64},{64,7... | collective-permute-start | bytes 393224 | tf_op jit(solution)/shard_map/ppermute | solution.py:40
  6.3 3.9 %shard_map.118.late_ref = bf16[256,512]{1,0:T(8,128)(2,1)} custom-call(s32[3]{0:T(128)} %pad_add_fusion.where, bf16[512,512]{1,0:T(8,128)(2,1)} %q_ref.3, bf16[512,512]{1,0:T(8,128)(2,1)} %kb.3, bf16[512,512]{1,0:T(8,128)(2,1)} %kb.3, bf16[512,512]{1,0:T(8,128)(2,1)} %vb.3, bf16[512,512]{1,0:T(8,128)(2,1)} %vb.3, s32[1,128]{1,0:T(1,128)} %bitcast.48), custom_call_target="tpu_custom_call" | custom-call | flops 1073741824 | bytes 786432 | tf_op jit(solution)/shard_map/pallas_call | solution.py:121
  10.2 3.1 %collective-permute-done.tails = bf16[2,256,128]{2,1,0:T(8,128)(2,1)S(1)} collective-permute-done((bf16[2,256,128]{2,1,0:T(8,128)(2,1)S(1)}, bf16[2,256,128]{2,1,0:T(8,128)(2,1)S(1)}, u32[]{:S(2)}, u32[]{:S(2)}) %collective-permute-start) | collective-permute-done | bytes 131104 | tf_op jit(solution)/shard_map/ppermute | solution.py:40
  14.0 4.2 %shard_map.119 = (bf16[256,512]{1,0:T(8,128)(2,1)}, bf16[256,512]{1,0:T(8,128)(2,1)}) custom-call(s32[3]{0:T(128)} %pad_add_fusion.where, bf16[512,512]{1,0:T(8,128)(2,1)} %q_ref.3, bf16[2,256,128]{2,1,0:T(8,128)(2,1)} %copy-done.9, bf16[512,512]{1,0:T(8,128)(2,1)} %kb.3, bf16[512,512]{1,0:T(8,128)(2,1)} %vb.3, s32[1,128]{1,0:T(1,128)} %bitcast.49, ...), custom_call_target="tpu_custom_call" | custom-call | flops 1073741824 | bytes 1048576 | tf_op jit(solution)/shard_map/pallas_call | solution.py:142
  28.1 4.1 %collective-permute-done.6 = bf16[64,2048]{1,0:T(8,128)(2,1)S(1)} collective-permute-done((bf16[64,2048]{1,0:T(8,128)(2,1)}, bf16[64,2048]{1,0:T(8,128)(2,1)S(1)}, u32[]{:S(2)}, u32[]{:S(2)}) %collective-permute-start.6) | collective-permute-done | bytes 262176 | tf_op jit(solution)/shard_map/ppermute | solution.py:31
  32.2 6.8 %collective-permute-done.7 = bf16[64,2048]{1,0:T(8,128)(2,1)S(1)} collective-permute-done((bf16[64,2048]{1,0:T(8,128)(2,1)}, bf16[64,2048]{1,0:T(8,128)(2,1)S(1)}, u32[]{:S(2)}, u32[]{:S(2)}) %collective-permute-start.7) | collective-permute-done | bytes 262176 | tf_op jit(solution)/shard_map/ppermute | solution.py:31
  40.3 3.2 %collective-permute-start.11 = (bf16[64,2176]{1,0:T(8,128)(2,1)S(1)}, bf16[64,2176]{1,0:T(8,128)(2,1)S(1)}, u32[]{:S(2)}, u32[]{:S(2)}) collective-permute-start(bf16[64,2176]{1,0:T(8,128)(2,1)S(1)} %concatenate.9.refs_0_), channel_id=1, source_target_pairs={{0,56},{8,0},{16,8},{24,16},{32,24},{40,32},{48,40},{56,48},{1,57}... | collective-permute-start | bytes 835592 | tf_op jit(solution)/shard_map/ppermute | solution.py:31
  43.5 6.2 %collective-permute-done.9.refs_1_ = bf16[64,2176]{1,0:T(8,128)(2,1)S(1)} collective-permute-done((bf16[64,2176]{1,0:T(8,128)(2,1)S(1)}, bf16[64,2176]{1,0:T(8,128)(2,1)S(1)}, u32[]{:S(2)}, u32[]{:S(2)}) %collective-permute-start.9) | collective-permute-done | bytes 278560 | tf_op jit(solution)/shard_map/ppermute | solution.py:31
  49.7 3.2 %collective-permute-start.12 = (bf16[64,2176]{1,0:T(8,128)(2,1)S(1)}, bf16[64,2176]{1,0:T(8,128)(2,1)S(1)}, u32[]{:S(2)}, u32[]{:S(2)}) collective-permute-start(bf16[64,2176]{1,0:T(8,128)(2,1)S(1)} %collective-permute-done.11.refs_4_.refs_0_), channel_id=1, source_target_pairs={{0,56},{8,0},{16,8},{24,16},{32,24},{40,32},{48,40},{56,48},{1,57}... | collective-permute-start | bytes 835592 | tf_op jit(solution)/shard_map/ppermute | solution.py:31
  53.0 5.3 %collective-permute-done.10.refs_2_ = bf16[64,2176]{1,0:T(8,128)(2,1)S(1)} collective-permute-done((bf16[64,2176]{1,0:T(8,128)(2,1)S(1)}, bf16[64,2176]{1,0:T(8,128)(2,1)S(1)}, u32[]{:S(2)}, u32[]{:S(2)}) %collective-permute-start.10) | collective-permute-done | bytes 278560 | tf_op jit(solution)/shard_map/ppermute | solution.py:31
  58.3 3.7 %shard_map.120 = (bf16[384,2048]{1,0:T(8,128)(2,1)}, bf16[384,384]{1,0:T(8,128)(2,1)S(1)}) custom-call(s32[1]{0:T(128)} %bitcast.6.z_ref, bf16[64,2176]{1,0:T(8,128)(2,1)S(1)} %concatenate.9.refs_0_, bf16[64,2176]{1,0:T(8,128)(2,1)S(1)} %collective-permute-done.9.refs_1_, bf16[64,2176]{1,0:T(8,128)(2,1)S(1)} %collective-permute-done.10.refs_2_, ...), custom_call_target="tpu_custom_call" | custom-call | flops 603979776 | bytes 3145728 | tf_op jit(solution)/shard_map/pallas_call | solution.py:264
  62.0 7.1 %all-to-all-start = ((bf16[16,24,2048]{2,1,0:T(8,128)(2,1)}), bf16[16,24,2048]{2,1,0:T(8,128)(2,1)}, u32[]{:S(2)}, u32[]{:S(2)}) async-start(bf16[16,24,2048]{2,1,0:T(8,128)(2,1)} %bitcast.7), calls=%async_computation | async-start | bytes 3145728 | tf_op jit(solution)/shard_map/all_to_all | solution.py:351
  72.1 4.1 %collective-permute-done.14.refs_2_ = bf16[64,2176]{1,0:T(8,128)(2,1)S(1)} collective-permute-done((bf16[64,2176]{1,0:T(8,128)(2,1)S(1)}, bf16[64,2176]{1,0:T(8,128)(2,1)S(1)}, u32[]{:S(2)}, u32[]{:S(2)}) %collective-permute-start.14) | collective-permute-done | bytes 278560 | tf_op jit(solution)/shard_map/ppermute | solution.py:31
  76.2 3.8 %collective-permute-start.16 = (bf16[64,1152]{1,0:T(8,128)(2,1)S(1)}, bf16[64,1152]{1,0:T(8,128)(2,1)S(1)}, u32[]{:S(2)}, u32[]{:S(2)}) collective-permute-start(bf16[64,1152]{1,0:T(8,128)(2,1)S(1)} %slice.96), channel_id=1, source_target_pairs={{0,56},{8,0},{16,8},{24,16},{32,24},{40,32},{48,40},{56,48},{1,57}... | collective-permute-start | bytes 442376 | tf_op jit(solution)/shard_map/ppermute | solution.py:31
  80.0 6.2 %collective-permute-done.15.refs_3_ = bf16[64,1024]{1,0:T(8,128)(2,1)S(1)} collective-permute-done((bf16[64,1024]{1,0:T(8,128)(2,1)S(1)}, bf16[64,1024]{1,0:T(8,128)(2,1)S(1)}, u32[]{:S(2)}, u32[]{:S(2)}) %collective-permute-start.15) | collective-permute-done | bytes 131104 | tf_op jit(solution)/shard_map/ppermute | solution.py:31
  89.1 7.2 %all-to-all-start.1 = ((bf16[16,16,2048]{2,1,0:T(8,128)(2,1)}), bf16[16,16,2048]{2,1,0:T(8,128)(2,1)S(1)}, u32[]{:S(2)}, u32[]{:S(2)}) async-start(bf16[16,16,2048]{2,1,0:T(8,128)(2,1)} %bitcast.9), calls=%async_computation.1 | async-start | bytes 2097152 | tf_op jit(solution)/shard_map/all_to_all | solution.py:351
  96.4 10.0 %shard_map.122 = bf16[384,2048]{1,0:T(8,128)(2,1)} custom-call(bf16[384,2048]{1,0:T(8,128)(2,1)} %bitcast.8.rows_ref, bf16[1,2048,384]{2,1,0:T(8,128)(2,1)} %g0.1, bf16[1,2048,384]{2,1,0:T(8,128)(2,1)} %collective-permute-done.1.g1, bf16[1,2048,384]{2,1,0:T(8,128)(2,1)} %u0.1, bf16[1,2048,384]{2,1,0:T(8,128)(2,1)} %collective-permute-done.2.u1, ...), custom_call_target="tpu_custom_call" | custom-call | flops 3623878656 | bytes 12582912 | tf_op jit(solution)/shard_map/pallas_call | solution.py:328
  108.7 8.7 %shard_map.123 = bf16[256,2048]{1,0:T(8,128)(2,1)} custom-call(bf16[256,2048]{1,0:T(8,128)(2,1)} %bitcast.44, bf16[1,2048,384]{2,1,0:T(8,128)(2,1)} %g0.1, bf16[1,2048,384]{2,1,0:T(8,128)(2,1)} %collective-permute-done.1.g1, bf16[1,2048,384]{2,1,0:T(8,128)(2,1)} %u0.1, bf16[1,2048,384]{2,1,0:T(8,128)(2,1)} %collective-permute-done.2.u1, ...), custom_call_target="tpu_custom_call" | custom-call | flops 2415919104 | bytes 11534336 | tf_op jit(solution)/shard_map/pallas_call | solution.py:328
  117.4 16.5 %all_to_all.20 = bf16[16,16,2048]{2,1,0:T(8,128)(2,1)S(1)} all-to-all(bf16[16,16,2048]{2,1,0:T(8,128)(2,1)} %bitcast.45), channel_id=1, replica_groups=mesh['x'=4,'z'=8,'y'=4,'c'=2] {'x','y'}, dimensions={0} | all-to-all | bytes 2097152 | tf_op jit(solution)/shard_map/all_to_all | solution.py:351
  134.0 5.8 %all-to-all-start.3 = ((bf16[16,24,2048]{2,1,0:T(8,128)(2,1)}), bf16[16,24,2048]{2,1,0:T(8,128)(2,1)S(1)}, u32[]{:S(2)}, u32[]{:S(2)}) async-start(bf16[16,24,2048]{2,1,0:T(8,128)(2,1)} %bitcast.46), calls=%async_computation.3 | async-start | bytes 3145728 | tf_op jit(solution)/shard_map/all_to_all | solution.py:351
  149.4 4.1 %collective-permute-done.17 = bf16[64,1024]{1,0:T(8,128)(2,1)S(1)} collective-permute-done((bf16[64,1024]{1,0:T(8,128)(2,1)S(1)}, bf16[64,1024]{1,0:T(8,128)(2,1)S(1)}, u32[]{:S(2)}, u32[]{:S(2)}) %collective-permute-start.17) | collective-permute-done | bytes 131104 | tf_op jit(solution)/shard_map/ppermute | solution.py:31
  157.0 4.2 %collective-permute-done.18 = bf16[64,1024]{1,0:T(8,128)(2,1)S(1)} collective-permute-done((bf16[64,1024]{1,0:T(8,128)(2,1)S(1)}, bf16[64,1024]{1,0:T(8,128)(2,1)S(1)}, u32[]{:S(2)}, u32[]{:S(2)}) %collective-permute-start.18) | collective-permute-done | bytes 131104 | tf_op jit(solution)/shard_map/ppermute | solution.py:31
  165.3 5.5 %collective-permute-done.23 = bf16[64,2048]{1,0:T(8,128)(2,1)S(1)} collective-permute-done((bf16[64,2048]{1,0:T(8,128)(2,1)S(1)}, bf16[64,2048]{1,0:T(8,128)(2,1)S(1)}, u32[]{:S(2)}, u32[]{:S(2)}) %collective-permute-start.23) | collective-permute-done | bytes 262176 | tf_op jit(solution)/shard_map/ppermute | solution.py:31
  173.4 4.3 %collective-permute-done.26 = bf16[64,2048]{1,0:T(8,128)(2,1)S(1)} collective-permute-done((bf16[64,2048]{1,0:T(8,128)(2,1)S(1)}, bf16[64,2048]{1,0:T(8,128)(2,1)S(1)}, u32[]{:S(2)}, u32[]{:S(2)}) %collective-permute-start.26) | collective-permute-done | bytes 262176 | tf_op jit(solution)/shard_map/ppermute | solution.py:31
  (100 shorter events, 46.0 us)
Async XLA Ops:
  0.0 20.1 %collective-permute-start.5 = (bf16[512,2048]{1,0:T(8,128)(2,1)}, bf16[512,2048]{1,0:T(8,128)(2,1)S(1)}, u32[]{:S(2)}, u32[]{:S(2)}) collective-permute-start(bf16[512,2048]{1,0:T(8,128)(2,1)} %param.17), channel_id=1, source_target_pairs={{0,1},{1,0},{2,3},{3,2},{4,5},{5,4},{6,7},{7,6},{8,9},{9,8},{10,11... | collective-permute-start | bytes 6291464 | tf_op jit(solution)/shard_map/ppermute | solution.py:35
  0.0 18.2 %collective-permute-start.1 = (bf16[1,2048,384]{2,1,0:T(8,128)(2,1)}, bf16[1,2048,384]{2,1,0:T(8,128)(2,1)}, u32[]{:S(2)}, u32[]{:S(2)}) collective-permute-start(bf16[1,2048,384]{2,1,0:T(8,128)(2,1)} %g0.1), channel_id=1, source_target_pairs={{0,1},{1,0},{2,3},{3,2},{4,5},{5,4},{6,7},{7,6},{8,9},{9,8},{10,11... | collective-permute-start | bytes 4718600 | tf_op jit(solution)/shard_map/ppermute | solution.py:35
  0.5 17.7 %collective-permute-start.2 = (bf16[1,2048,384]{2,1,0:T(8,128)(2,1)}, bf16[1,2048,384]{2,1,0:T(8,128)(2,1)}, u32[]{:S(2)}, u32[]{:S(2)}) collective-permute-start(bf16[1,2048,384]{2,1,0:T(8,128)(2,1)} %u0.1), channel_id=1, source_target_pairs={{0,1},{1,0},{2,3},{3,2},{4,5},{5,4},{6,7},{7,6},{8,9},{9,8},{10,11... | collective-permute-start | bytes 4718600 | tf_op jit(solution)/shard_map/ppermute | solution.py:35
  0.5 17.7 %collective-permute-start.3 = (bf16[1,384,2048]{2,1,0:T(8,128)(2,1)}, bf16[1,384,2048]{2,1,0:T(8,128)(2,1)}, u32[]{:S(2)}, u32[]{:S(2)}) collective-permute-start(bf16[1,384,2048]{2,1,0:T(8,128)(2,1)} %d0.1), channel_id=1, source_target_pairs={{0,1},{1,0},{2,3},{3,2},{4,5},{5,4},{6,7},{7,6},{8,9},{9,8},{10,11... | collective-permute-start | bytes 4718600 | tf_op jit(solution)/shard_map/ppermute | solution.py:35
  1.9 11.4 %collective-permute-start = (bf16[2,256,128]{2,1,0:T(8,128)(2,1)S(1)}, bf16[2,256,128]{2,1,0:T(8,128)(2,1)S(1)}, u32[]{:S(2)}, u32[]{:S(2)}) collective-permute-start(bf16[2,256,128]{2,1,0:T(8,128)(2,1)S(1)} %pad_maximum_fusion), channel_id=1, source_target_pairs={{0,8},{8,16},{16,24},{24,32},{32,40},{40,48},{48,56},{56,64},{64,7... | collective-permute-start | bytes 393224 | tf_op jit(solution)/shard_map/ppermute | solution.py:40
  22.1 10.1 %collective-permute-start.6 = (bf16[64,2048]{1,0:T(8,128)(2,1)}, bf16[64,2048]{1,0:T(8,128)(2,1)S(1)}, u32[]{:S(2)}, u32[]{:S(2)}) collective-permute-start(bf16[64,2048]{1,0:T(8,128)(2,1)} %get-tuple-element.59), channel_id=1, source_target_pairs={{0,2},{2,4},{4,6},{6,0},{1,3},{3,5},{5,7},{7,1},{8,10},{10,12},{12... | collective-permute-start | bytes 786440 | tf_op jit(solution)/shard_map/ppermute | solution.py:31
  23.7 15.4 %collective-permute-start.7 = (bf16[64,2048]{1,0:T(8,128)(2,1)}, bf16[64,2048]{1,0:T(8,128)(2,1)S(1)}, u32[]{:S(2)}, u32[]{:S(2)}) collective-permute-start(bf16[64,2048]{1,0:T(8,128)(2,1)} %get-tuple-element.61), channel_id=1, source_target_pairs={{0,4},{2,6},{4,0},{6,2},{1,5},{3,7},{5,1},{7,3},{8,12},{10,14},{12... | collective-permute-start | bytes 786440 | tf_op jit(solution)/shard_map/ppermute | solution.py:31
  26.5 12.5 %collective-permute-start.8 = (bf16[64,2048]{1,0:T(8,128)(2,1)S(1)}, bf16[64,2048]{1,0:T(8,128)(2,1)S(1)}, u32[]{:S(2)}, u32[]{:S(2)}) collective-permute-start(bf16[64,2048]{1,0:T(8,128)(2,1)S(1)} %get-tuple-element.60), channel_id=1, source_target_pairs={{0,6},{2,0},{4,2},{6,4},{1,7},{3,1},{5,3},{7,5},{8,14},{10,8},{12,... | collective-permute-start | bytes 786440 | tf_op jit(solution)/shard_map/ppermute | solution.py:31
  40.2 9.5 %collective-permute-start.9 = (bf16[64,2176]{1,0:T(8,128)(2,1)S(1)}, bf16[64,2176]{1,0:T(8,128)(2,1)S(1)}, u32[]{:S(2)}, u32[]{:S(2)}) collective-permute-start(bf16[64,2176]{1,0:T(8,128)(2,1)S(1)} %concatenate.9.refs_0_), channel_id=1, source_target_pairs={{0,8},{8,16},{16,24},{24,32},{32,40},{40,48},{48,56},{56,0},{1,9},... | collective-permute-start | bytes 835592 | tf_op jit(solution)/shard_map/ppermute | solution.py:31
  40.3 9.4 %collective-permute-start.11 = (bf16[64,2176]{1,0:T(8,128)(2,1)S(1)}, bf16[64,2176]{1,0:T(8,128)(2,1)S(1)}, u32[]{:S(2)}, u32[]{:S(2)}) collective-permute-start(bf16[64,2176]{1,0:T(8,128)(2,1)S(1)} %concatenate.9.refs_0_), channel_id=1, source_target_pairs={{0,56},{8,0},{16,8},{24,16},{32,24},{40,32},{48,40},{56,48},{1,57}... | collective-permute-start | bytes 835592 | tf_op jit(solution)/shard_map/ppermute | solution.py:31
  49.7 8.5 %collective-permute-start.10 = (bf16[64,2176]{1,0:T(8,128)(2,1)S(1)}, bf16[64,2176]{1,0:T(8,128)(2,1)S(1)}, u32[]{:S(2)}, u32[]{:S(2)}) collective-permute-start(bf16[64,2176]{1,0:T(8,128)(2,1)S(1)} %collective-permute-done.9.refs_1_), channel_id=1, source_target_pairs={{0,8},{8,16},{16,24},{24,32},{32,40},{40,48},{48,56},{56,0},{1,9},... | collective-permute-start | bytes 835592 | tf_op jit(solution)/shard_map/ppermute | solution.py:31
  49.7 8.5 %collective-permute-start.12 = (bf16[64,2176]{1,0:T(8,128)(2,1)S(1)}, bf16[64,2176]{1,0:T(8,128)(2,1)S(1)}, u32[]{:S(2)}, u32[]{:S(2)}) collective-permute-start(bf16[64,2176]{1,0:T(8,128)(2,1)S(1)} %collective-permute-done.11.refs_4_.refs_0_), channel_id=1, source_target_pairs={{0,56},{8,0},{16,8},{24,16},{32,24},{40,32},{48,40},{56,48},{1,57}... | collective-permute-start | bytes 835592 | tf_op jit(solution)/shard_map/ppermute | solution.py:31
  62.0 27.2 %all-to-all-start = ((bf16[16,24,2048]{2,1,0:T(8,128)(2,1)}), bf16[16,24,2048]{2,1,0:T(8,128)(2,1)}, u32[]{:S(2)}, u32[]{:S(2)}) async-start(bf16[16,24,2048]{2,1,0:T(8,128)(2,1)} %bitcast.7), calls=%async_computation | async-start | bytes 3145728 | tf_op jit(solution)/shard_map/all_to_all | solution.py:351
  72.1 7.9 %collective-permute-start.13 = (bf16[64,2176]{1,0:T(8,128)(2,1)S(1)}, bf16[64,2176]{1,0:T(8,128)(2,1)S(1)}, u32[]{:S(2)}, u32[]{:S(2)}) collective-permute-start(bf16[64,2176]{1,0:T(8,128)(2,1)S(1)} %collective-permute-done.10.refs_2_), channel_id=1, source_target_pairs={{0,8},{8,16},{16,24},{24,32},{32,40},{40,48},{48,56},{56,0},{1,9},... | collective-permute-start | bytes 835592 | tf_op jit(solution)/shard_map/ppermute | solution.py:31
  76.2 10.0 %collective-permute-start.16 = (bf16[64,1152]{1,0:T(8,128)(2,1)S(1)}, bf16[64,1152]{1,0:T(8,128)(2,1)S(1)}, u32[]{:S(2)}, u32[]{:S(2)}) collective-permute-start(bf16[64,1152]{1,0:T(8,128)(2,1)S(1)} %slice.96), channel_id=1, source_target_pairs={{0,56},{8,0},{16,8},{24,16},{32,24},{40,32},{48,40},{56,48},{1,57}... | collective-permute-start | bytes 442376 | tf_op jit(solution)/shard_map/ppermute | solution.py:31
  89.1 18.6 %all-to-all-start.1 = ((bf16[16,16,2048]{2,1,0:T(8,128)(2,1)}), bf16[16,16,2048]{2,1,0:T(8,128)(2,1)S(1)}, u32[]{:S(2)}, u32[]{:S(2)}) async-start(bf16[16,16,2048]{2,1,0:T(8,128)(2,1)} %bitcast.9), calls=%async_computation.1 | async-start | bytes 2097152 | tf_op jit(solution)/shard_map/all_to_all | solution.py:351
  134.0 22.5 %all-to-all-start.3 = ((bf16[16,24,2048]{2,1,0:T(8,128)(2,1)}), bf16[16,24,2048]{2,1,0:T(8,128)(2,1)S(1)}, u32[]{:S(2)}, u32[]{:S(2)}) async-start(bf16[16,24,2048]{2,1,0:T(8,128)(2,1)} %bitcast.46), calls=%async_computation.3 | async-start | bytes 3145728 | tf_op jit(solution)/shard_map/all_to_all | solution.py:351
  143.8 18.0 %collective-permute-start.20 = (bf16[64,1024]{1,0:T(8,128)(2,1)S(1)}, bf16[64,1024]{1,0:T(8,128)(2,1)S(1)}, u32[]{:S(2)}, u32[]{:S(2)}) collective-permute-start(bf16[64,1024]{1,0:T(8,128)(2,1)S(1)} %slice.99), channel_id=1, source_target_pairs={{0,56},{8,0},{16,8},{24,16},{32,24},{40,32},{48,40},{56,48},{1,57}... | collective-permute-start | bytes 393224 | tf_op jit(solution)/shard_map/ppermute | solution.py:31
  146.0 11.0 %collective-permute-start.19 = (bf16[64,1024]{1,0:T(8,128)(2,1)S(1)}, bf16[64,1024]{1,0:T(8,128)(2,1)S(1)}, u32[]{:S(2)}, u32[]{:S(2)}) collective-permute-start(bf16[64,1024]{1,0:T(8,128)(2,1)S(1)} %slice.98), channel_id=1, source_target_pairs={{0,8},{8,16},{16,24},{24,32},{32,40},{40,48},{48,56},{56,0},{1,9},... | collective-permute-start | bytes 393224 | tf_op jit(solution)/shard_map/ppermute | solution.py:31
  146.8 15.0 %collective-permute-start.22 = (bf16[64,1024]{1,0:T(8,128)(2,1)S(1)}, bf16[64,1024]{1,0:T(8,128)(2,1)S(1)}, u32[]{:S(2)}, u32[]{:S(2)}) collective-permute-start(bf16[64,1024]{1,0:T(8,128)(2,1)S(1)} %add_convert_fusion.3), channel_id=1, source_target_pairs={{0,56},{8,0},{16,8},{24,16},{32,24},{40,32},{48,40},{56,48},{1,57}... | collective-permute-start | bytes 393224 | tf_op jit(solution)/shard_map/ppermute | solution.py:31
  153.6 7.6 %collective-permute-start.18 = (bf16[64,1024]{1,0:T(8,128)(2,1)S(1)}, bf16[64,1024]{1,0:T(8,128)(2,1)S(1)}, u32[]{:S(2)}, u32[]{:S(2)}) collective-permute-start(bf16[64,1024]{1,0:T(8,128)(2,1)S(1)} %add_convert_fusion.4), channel_id=1, source_target_pairs={{0,8},{8,16},{16,24},{24,32},{32,40},{40,48},{48,56},{56,0},{1,9},... | collective-permute-start | bytes 393224 | tf_op jit(solution)/shard_map/ppermute | solution.py:31
  161.3 9.5 %collective-permute-start.23 = (bf16[64,2048]{1,0:T(8,128)(2,1)S(1)}, bf16[64,2048]{1,0:T(8,128)(2,1)S(1)}, u32[]{:S(2)}, u32[]{:S(2)}) collective-permute-start(bf16[64,2048]{1,0:T(8,128)(2,1)S(1)} %fusion.5), channel_id=1, source_target_pairs={{0,8},{8,16},{16,24},{24,32},{32,40},{40,48},{48,56},{56,0},{1,9},... | collective-permute-start | bytes 786440 | tf_op jit(solution)/shard_map/ppermute | solution.py:31
  161.8 9.3 %collective-permute-start.25 = (bf16[64,2048]{1,0:T(8,128)(2,1)S(1)}, bf16[64,2048]{1,0:T(8,128)(2,1)S(1)}, u32[]{:S(2)}, u32[]{:S(2)}) collective-permute-start(bf16[64,2048]{1,0:T(8,128)(2,1)S(1)} %add_convert_fusion.2), channel_id=1, source_target_pairs={{0,56},{8,0},{16,8},{24,16},{32,24},{40,32},{48,40},{56,48},{1,57}... | collective-permute-start | bytes 786440 | tf_op jit(solution)/shard_map/ppermute | solution.py:31
  173.2 7.6 %collective-permute-start.24 = (bf16[64,2048]{1,0:T(8,128)(2,1)S(1)}, bf16[64,2048]{1,0:T(8,128)(2,1)S(1)}, u32[]{:S(2)}, u32[]{:S(2)}) collective-permute-start(bf16[64,2048]{1,0:T(8,128)(2,1)S(1)} %add_convert_fusion.1), channel_id=1, source_target_pairs={{0,8},{8,16},{16,24},{24,32},{32,40},{40,48},{48,56},{56,0},{1,9},... | collective-permute-start | bytes 786440 | tf_op jit(solution)/shard_map/ppermute | solution.py:31
  (16 other events, 111.7 us)

commit v8 on v7

--- a/solution.py
+++ b/solution.py
@@ -174,7 +174,7 @@
     both = mine + jnp.dot(arrived, other_weight, preferred_element_type=F32)
     both = both.reshape(NY, ROWS, out_weight.shape[1])
     sent = both.astype(BF)
-    moved = [shift(sent[k], "y", NY, k) for k in range(1, NY)]
+    moved = [shift(sent[k], "y", NY, k) for k in (2, 1, 3)]
     return both[0] + sum(block.astype(F32) for block in moved)
 
 
@@ -320,7 +320,7 @@
     lax.fori_loop(0, d_all.shape[1] // tile, outer, 0)
 
 
-def expert_rows(rows, gate_pair, up_pair, down_pair):
+def expert_rows(rows, gate_pair, up_pair, down_pair, limit=57):
     count, width = rows.shape
     hid = 2 * gate_pair[0].shape[2]
     whole = pl.BlockSpec(memory_space=pltpu.VMEM)
@@ -337,7 +337,7 @@
             pltpu.VMEM((count, hid), BF),
             pltpu.SemaphoreType.DMA((6,)),
         ],
-        compiler_params=pltpu.CompilerParams(vmem_limit_bytes=57 * 1024 * 1024),
+        compiler_params=pltpu.CompilerParams(vmem_limit_bytes=limit * 1024 * 1024),
         cost_estimate=pl.CostEstimate(
             flops=6 * count * width * hid,
             bytes_accessed=6 * width * hid + 4 * count * width,
@@ -381,6 +381,7 @@
     attn_theirs, attn_mine = attend(queries, key_rows, value_rows, doc_lengths)
     attn_theirs, attn_mine, pairs = lax.optimization_barrier((attn_theirs, attn_mine, pairs))
     mid = residual_in.astype(F32) + project(attn_theirs, attn_mine, out_weight, other_weight)
+    mid = lax.optimization_barrier(mid)
     spread = jnp.mean(mid * mid, axis=1, keepdims=True)
     normed = (mid * lax.rsqrt(spread + 1e-06) * norm_gain[None, :]).astype(BF)
 
@@ -403,7 +404,7 @@
     arrived_far = exchange(out_far)
     pair_near = expert_rows(arrived_near, *pairs)
     arrived_far, pair_near = lax.optimization_barrier((arrived_far, pair_near))
-    pair_far = expert_rows(arrived_far, *pairs)
+    pair_far = expert_rows(arrived_far, *pairs, limit=52)
 
     returned_far = exchange(pair_far)
     returned_far, pair_near = lax.optimization_barrier((returned_far, pair_near))

time: 184 us -> 182 us (0.989)
  transfers between devices with their start and end apart: 30 -> 30, of which waited for: 15 -> 17; matrix products, arithmetic and copies ran while one was open for 4% -> 4% of each run, Pallas kernels for 12% -> 12%
where the time goes in v8:
time: 182 us; the launch traced here: 181 us
  waiting for transfers between devices  59.8 us (33%)
  starting transfers between devices  59.2 us (33%)
  Pallas kernels  32.4 us (18%)
  blocking collectives  16.3 us (9%)
  matrix products  5.39 us (3%)
  local copies, waits for them, and re-layouts  3.69 us (2%)
  other arithmetic  3.47 us (2%)
    ppermute x21, waiting for transfers between devices, shift(): lax.ppermute(value, axis, [(i, (i + by) % size) for i in range(size)])  52.1 us
    ppermute x21, starting transfers between devices, shift(): lax.ppermute(value, axis, [(i, (i + by) % size) for i in range(size)])  33.5 us
    all_to_all x3, starting transfers between devices, exchange(): lax.all_to_all(rows.reshape(PLANE, count // PLANE, width), ('x', 'y'), sp...  20.7 us
    pallas_call x2, Pallas kernels, expert_rows(): pl.pallas_call(expert_body, out_shape=jax.ShapeDtypeStruct((count, width)...  17.6 us
    all_to_all x1, blocking collectives, exchange(): lax.all_to_all(rows.reshape(PLANE, count // PLANE, width), ('x', 'y'), sp...  16.3 us
    pallas_call x2, Pallas kernels, dispatch(): pl.pallas_call(functools.partial(dispatch_body, first_block, first_slot),...  6.65 us
    all_to_all x3, waiting for transfers between devices, exchange(): lax.all_to_all(rows.reshape(PLANE, count // PLANE, width), ('x', 'y'), sp...  4.54 us
    pallas_call x1, Pallas kernels, attend(): pl.pallas_call(early_body, out_shape=(jax.ShapeDtypeStruct((half, width),...  4.2 us
  transfers between devices with their start and end apart: 30, of which 17 were waited for; matrix products, arithmetic and copies ran while one was open for 4% of the time, Pallas kernels for 12%

profile of v8, /device:TPU:2, one launch (start us, length us, event | category | flops | bytes accessed | tf_op | source)
XLA Modules:
  0.0 180.6 jit_solution(14979555483702539242)
XLA Ops:
  1.9 3.8 %collective-permute-start = (bf16[2,256,128]{2,1,0:T(8,128)(2,1)S(1)}, bf16[2,256,128]{2,1,0:T(8,128)(2,1)S(1)}, u32[]{:S(2)}, u32[]{:S(2)}) collective-permute-start(bf16[2,256,128]{2,1,0:T(8,128)(2,1)S(1)} %pad_maximum_fusion), channel_id=1, source_target_pairs={{0,8},{8,16},{16,24},{24,32},{32,40},{40,48},{48,56},{56,64},{64,7... | collective-permute-start | bytes 393224 | tf_op jit(solution)/shard_map/ppermute | solution.py:40
  6.4 3.9 %shard_map.118.late_ref = bf16[256,512]{1,0:T(8,128)(2,1)} custom-call(s32[3]{0:T(128)} %pad_add_fusion.where, bf16[512,512]{1,0:T(8,128)(2,1)} %q_ref.3, bf16[512,512]{1,0:T(8,128)(2,1)} %kb.3, bf16[512,512]{1,0:T(8,128)(2,1)} %kb.3, bf16[512,512]{1,0:T(8,128)(2,1)} %vb.3, bf16[512,512]{1,0:T(8,128)(2,1)} %vb.3, s32[1,128]{1,0:T(1,128)} %bitcast.48), custom_call_target="tpu_custom_call" | custom-call | flops 1073741824 | bytes 786432 | tf_op jit(solution)/shard_map/pallas_call | solution.py:121
  14.0 4.2 %shard_map.119 = (bf16[256,512]{1,0:T(8,128)(2,1)}, bf16[256,512]{1,0:T(8,128)(2,1)}) custom-call(s32[3]{0:T(128)} %pad_add_fusion.where, bf16[512,512]{1,0:T(8,128)(2,1)} %q_ref.3, bf16[2,256,128]{2,1,0:T(8,128)(2,1)} %copy-done.9, bf16[512,512]{1,0:T(8,128)(2,1)} %kb.3, bf16[512,512]{1,0:T(8,128)(2,1)} %vb.3, s32[1,128]{1,0:T(1,128)} %bitcast.49, ...), custom_call_target="tpu_custom_call" | custom-call | flops 1073741824 | bytes 1048576 | tf_op jit(solution)/shard_map/pallas_call | solution.py:142
  21.2 3.3 %collective-permute-start.6 = (bf16[64,2048]{1,0:T(8,128)(2,1)S(1)}, bf16[64,2048]{1,0:T(8,128)(2,1)S(1)}, u32[]{:S(2)}, u32[]{:S(2)}) collective-permute-start(bf16[64,2048]{1,0:T(8,128)(2,1)S(1)} %get-tuple-element.57), channel_id=1, source_target_pairs={{0,4},{2,6},{4,0},{6,2},{1,5},{3,7},{5,1},{7,3},{8,12},{10,14},{12... | collective-permute-start | bytes 786440 | tf_op jit(solution)/shard_map/ppermute | solution.py:31
  28.0 4.0 %collective-permute-done.6 = bf16[64,2048]{1,0:T(8,128)(2,1)S(1)} collective-permute-done((bf16[64,2048]{1,0:T(8,128)(2,1)S(1)}, bf16[64,2048]{1,0:T(8,128)(2,1)S(1)}, u32[]{:S(2)}, u32[]{:S(2)}) %collective-permute-start.6) | collective-permute-done | bytes 262176 | tf_op jit(solution)/shard_map/ppermute | solution.py:31
  32.0 5.2 %collective-permute-done.7 = bf16[64,2048]{1,0:T(8,128)(2,1)} collective-permute-done((bf16[64,2048]{1,0:T(8,128)(2,1)S(1)}, bf16[64,2048]{1,0:T(8,128)(2,1)}, u32[]{:S(2)}, u32[]{:S(2)}) %collective-permute-start.7) | collective-permute-done | bytes 262176 | tf_op jit(solution)/shard_map/ppermute | solution.py:31
  43.0 6.2 %collective-permute-done.9.refs_1_ = bf16[64,2176]{1,0:T(8,128)(2,1)S(1)} collective-permute-done((bf16[64,2176]{1,0:T(8,128)(2,1)S(1)}, bf16[64,2176]{1,0:T(8,128)(2,1)S(1)}, u32[]{:S(2)}, u32[]{:S(2)}) %collective-permute-start.9) | collective-permute-done | bytes 278560 | tf_op jit(solution)/shard_map/ppermute | solution.py:31
  49.2 3.2 %collective-permute-start.12 = (bf16[64,2176]{1,0:T(8,128)(2,1)S(1)}, bf16[64,2176]{1,0:T(8,128)(2,1)S(1)}, u32[]{:S(2)}, u32[]{:S(2)}) collective-permute-start(bf16[64,2176]{1,0:T(8,128)(2,1)S(1)} %collective-permute-done.11.refs_4_.refs_0_), channel_id=1, source_target_pairs={{0,56},{8,0},{16,8},{24,16},{32,24},{40,32},{48,40},{56,48},{1,57}... | collective-permute-start | bytes 835592 | tf_op jit(solution)/shard_map/ppermute | solution.py:31
  52.4 5.3 %collective-permute-done.10.refs_2_ = bf16[64,2176]{1,0:T(8,128)(2,1)S(1)} collective-permute-done((bf16[64,2176]{1,0:T(8,128)(2,1)S(1)}, bf16[64,2176]{1,0:T(8,128)(2,1)S(1)}, u32[]{:S(2)}, u32[]{:S(2)}) %collective-permute-start.10) | collective-permute-done | bytes 278560 | tf_op jit(solution)/shard_map/ppermute | solution.py:31
  57.7 3.7 %shard_map.120 = (bf16[384,2048]{1,0:T(8,128)(2,1)}, bf16[384,384]{1,0:T(8,128)(2,1)S(1)}) custom-call(s32[1]{0:T(128)} %bitcast.6.z_ref, bf16[64,2176]{1,0:T(8,128)(2,1)S(1)} %concatenate.9.refs_0_, bf16[64,2176]{1,0:T(8,128)(2,1)S(1)} %collective-permute-done.9.refs_1_, bf16[64,2176]{1,0:T(8,128)(2,1)S(1)} %collective-permute-done.10.refs_2_, ...), custom_call_target="tpu_custom_call" | custom-call | flops 603979776 | bytes 3145728 | tf_op jit(solution)/shard_map/pallas_call | solution.py:264
  61.5 7.7 %all-to-all-start = ((bf16[16,24,2048]{2,1,0:T(8,128)(2,1)}), bf16[16,24,2048]{2,1,0:T(8,128)(2,1)}, u32[]{:S(2)}, u32[]{:S(2)}) async-start(bf16[16,24,2048]{2,1,0:T(8,128)(2,1)} %bitcast.7), calls=%async_computation | async-start | bytes 3145728 | tf_op jit(solution)/shard_map/all_to_all | solution.py:351
  72.1 4.1 %collective-permute-done.14.refs_2_ = bf16[64,2176]{1,0:T(8,128)(2,1)S(1)} collective-permute-done((bf16[64,2176]{1,0:T(8,128)(2,1)S(1)}, bf16[64,2176]{1,0:T(8,128)(2,1)S(1)}, u32[]{:S(2)}, u32[]{:S(2)}) %collective-permute-start.14) | collective-permute-done | bytes 278560 | tf_op jit(solution)/shard_map/ppermute | solution.py:31
  76.2 3.8 %collective-permute-start.16 = (bf16[64,1152]{1,0:T(8,128)(2,1)S(1)}, bf16[64,1152]{1,0:T(8,128)(2,1)S(1)}, u32[]{:S(2)}, u32[]{:S(2)}) collective-permute-start(bf16[64,1152]{1,0:T(8,128)(2,1)S(1)} %slice.96), channel_id=1, source_target_pairs={{0,56},{8,0},{16,8},{24,16},{32,24},{40,32},{48,40},{56,48},{1,57}... | collective-permute-start | bytes 442376 | tf_op jit(solution)/shard_map/ppermute | solution.py:31
  80.1 6.2 %collective-permute-done.15.refs_3_ = bf16[64,1024]{1,0:T(8,128)(2,1)S(1)} collective-permute-done((bf16[64,1024]{1,0:T(8,128)(2,1)S(1)}, bf16[64,1024]{1,0:T(8,128)(2,1)S(1)}, u32[]{:S(2)}, u32[]{:S(2)}) %collective-permute-start.15) | collective-permute-done | bytes 131104 | tf_op jit(solution)/shard_map/ppermute | solution.py:31
  89.2 7.2 %all-to-all-start.1 = ((bf16[16,16,2048]{2,1,0:T(8,128)(2,1)}), bf16[16,16,2048]{2,1,0:T(8,128)(2,1)S(1)}, u32[]{:S(2)}, u32[]{:S(2)}) async-start(bf16[16,16,2048]{2,1,0:T(8,128)(2,1)} %bitcast.9), calls=%async_computation.1 | async-start | bytes 2097152 | tf_op jit(solution)/shard_map/all_to_all | solution.py:351
  96.4 10.0 %shard_map.122 = bf16[384,2048]{1,0:T(8,128)(2,1)} custom-call(bf16[384,2048]{1,0:T(8,128)(2,1)} %bitcast.8.rows_ref, bf16[1,2048,384]{2,1,0:T(8,128)(2,1)} %g0.1, bf16[1,2048,384]{2,1,0:T(8,128)(2,1)} %collective-permute-done.1.g1, bf16[1,2048,384]{2,1,0:T(8,128)(2,1)} %u0.1, bf16[1,2048,384]{2,1,0:T(8,128)(2,1)} %collective-permute-done.2.u1, ...), custom_call_target="tpu_custom_call" | custom-call | flops 3623878656 | bytes 12582912 | tf_op jit(solution)/shard_map/pallas_call | solution.py:328
  108.8 7.6 %shard_map.123 = bf16[256,2048]{1,0:T(8,128)(2,1)S(1)} custom-call(bf16[256,2048]{1,0:T(8,128)(2,1)} %bitcast.45, bf16[1,2048,384]{2,1,0:T(8,128)(2,1)} %g0.1, bf16[1,2048,384]{2,1,0:T(8,128)(2,1)} %collective-permute-done.1.g1, bf16[1,2048,384]{2,1,0:T(8,128)(2,1)} %u0.1, bf16[1,2048,384]{2,1,0:T(8,128)(2,1)} %collective-permute-done.2.u1, ...), custom_call_target="tpu_custom_call" | custom-call | flops 2415919104 | bytes 11534336 | tf_op jit(solution)/shard_map/pallas_call | solution.py:328
  116.4 16.3 %all_to_all.20 = bf16[16,16,2048]{2,1,0:T(8,128)(2,1)S(1)} all-to-all(bf16[16,16,2048]{2,1,0:T(8,128)(2,1)S(1)} %bitcast.39), channel_id=1, replica_groups=mesh['x'=4,'z'=8,'y'=4,'c'=2] {'x','y'}, dimensions={0} | all-to-all | bytes 2097152 | tf_op jit(solution)/shard_map/all_to_all | solution.py:351
  132.8 5.8 %all-to-all-start.3 = ((bf16[16,24,2048]{2,1,0:T(8,128)(2,1)}), bf16[16,24,2048]{2,1,0:T(8,128)(2,1)S(1)}, u32[]{:S(2)}, u32[]{:S(2)}) async-start(bf16[16,24,2048]{2,1,0:T(8,128)(2,1)} %bitcast.46), calls=%async_computation.3 | async-start | bytes 3145728 | tf_op jit(solution)/shard_map/all_to_all | solution.py:351
  148.1 3.9 %collective-permute-done.17 = bf16[64,1024]{1,0:T(8,128)(2,1)S(1)} collective-permute-done((bf16[64,1024]{1,0:T(8,128)(2,1)S(1)}, bf16[64,1024]{1,0:T(8,128)(2,1)S(1)}, u32[]{:S(2)}, u32[]{:S(2)}) %collective-permute-start.17) | collective-permute-done | bytes 131104 | tf_op jit(solution)/shard_map/ppermute | solution.py:31
  155.8 4.0 %collective-permute-done.18 = bf16[64,1024]{1,0:T(8,128)(2,1)S(1)} collective-permute-done((bf16[64,1024]{1,0:T(8,128)(2,1)S(1)}, bf16[64,1024]{1,0:T(8,128)(2,1)S(1)}, u32[]{:S(2)}, u32[]{:S(2)}) %collective-permute-start.18) | collective-permute-done | bytes 131104 | tf_op jit(solution)/shard_map/ppermute | solution.py:31
  163.8 4.9 %collective-permute-done.23 = bf16[64,2048]{1,0:T(8,128)(2,1)S(1)} collective-permute-done((bf16[64,2048]{1,0:T(8,128)(2,1)S(1)}, bf16[64,2048]{1,0:T(8,128)(2,1)S(1)}, u32[]{:S(2)}, u32[]{:S(2)}) %collective-permute-start.23) | collective-permute-done | bytes 262176 | tf_op jit(solution)/shard_map/ppermute | solution.py:31
  172.2 3.9 %collective-permute-done.26 = bf16[64,2048]{1,0:T(8,128)(2,1)S(1)} collective-permute-done((bf16[64,2048]{1,0:T(8,128)(2,1)S(1)}, bf16[64,2048]{1,0:T(8,128)(2,1)S(1)}, u32[]{:S(2)}, u32[]{:S(2)}) %collective-permute-start.26) | collective-permute-done | bytes 262176 | tf_op jit(solution)/shard_map/ppermute | solution.py:31
  176.1 3.6 %collective-permute-done.24 = bf16[64,2048]{1,0:T(8,128)(2,1)S(1)} collective-permute-done((bf16[64,2048]{1,0:T(8,128)(2,1)S(1)}, bf16[64,2048]{1,0:T(8,128)(2,1)S(1)}, u32[]{:S(2)}, u32[]{:S(2)}) %collective-permute-start.24) | collective-permute-done | bytes 262176 | tf_op jit(solution)/shard_map/ppermute | solution.py:31
  (101 shorter events, 48.3 us)
Async XLA Ops:
  0.0 20.0 %collective-permute-start.5 = (bf16[512,2048]{1,0:T(8,128)(2,1)}, bf16[512,2048]{1,0:T(8,128)(2,1)S(1)}, u32[]{:S(2)}, u32[]{:S(2)}) collective-permute-start(bf16[512,2048]{1,0:T(8,128)(2,1)} %param.17), channel_id=1, source_target_pairs={{0,1},{1,0},{2,3},{3,2},{4,5},{5,4},{6,7},{7,6},{8,9},{9,8},{10,11... | collective-permute-start | bytes 6291464 | tf_op jit(solution)/shard_map/ppermute | solution.py:35
  0.0 18.2 %collective-permute-start.1 = (bf16[1,2048,384]{2,1,0:T(8,128)(2,1)}, bf16[1,2048,384]{2,1,0:T(8,128)(2,1)}, u32[]{:S(2)}, u32[]{:S(2)}) collective-permute-start(bf16[1,2048,384]{2,1,0:T(8,128)(2,1)} %g0.1), channel_id=1, source_target_pairs={{0,1},{1,0},{2,3},{3,2},{4,5},{5,4},{6,7},{7,6},{8,9},{9,8},{10,11... | collective-permute-start | bytes 4718600 | tf_op jit(solution)/shard_map/ppermute | solution.py:35
  0.5 17.7 %collective-permute-start.2 = (bf16[1,2048,384]{2,1,0:T(8,128)(2,1)}, bf16[1,2048,384]{2,1,0:T(8,128)(2,1)}, u32[]{:S(2)}, u32[]{:S(2)}) collective-permute-start(bf16[1,2048,384]{2,1,0:T(8,128)(2,1)} %u0.1), channel_id=1, source_target_pairs={{0,1},{1,0},{2,3},{3,2},{4,5},{5,4},{6,7},{7,6},{8,9},{9,8},{10,11... | collective-permute-start | bytes 4718600 | tf_op jit(solution)/shard_map/ppermute | solution.py:35
  0.5 17.7 %collective-permute-start.3 = (bf16[1,384,2048]{2,1,0:T(8,128)(2,1)}, bf16[1,384,2048]{2,1,0:T(8,128)(2,1)}, u32[]{:S(2)}, u32[]{:S(2)}) collective-permute-start(bf16[1,384,2048]{2,1,0:T(8,128)(2,1)} %d0.1), channel_id=1, source_target_pairs={{0,1},{1,0},{2,3},{3,2},{4,5},{5,4},{6,7},{7,6},{8,9},{9,8},{10,11... | collective-permute-start | bytes 4718600 | tf_op jit(solution)/shard_map/ppermute | solution.py:35
  1.9 11.4 %collective-permute-start = (bf16[2,256,128]{2,1,0:T(8,128)(2,1)S(1)}, bf16[2,256,128]{2,1,0:T(8,128)(2,1)S(1)}, u32[]{:S(2)}, u32[]{:S(2)}) collective-permute-start(bf16[2,256,128]{2,1,0:T(8,128)(2,1)S(1)} %pad_maximum_fusion), channel_id=1, source_target_pairs={{0,8},{8,16},{16,24},{24,32},{32,40},{40,48},{48,56},{56,64},{64,7... | collective-permute-start | bytes 393224 | tf_op jit(solution)/shard_map/ppermute | solution.py:40
  21.2 10.7 %collective-permute-start.6 = (bf16[64,2048]{1,0:T(8,128)(2,1)S(1)}, bf16[64,2048]{1,0:T(8,128)(2,1)S(1)}, u32[]{:S(2)}, u32[]{:S(2)}) collective-permute-start(bf16[64,2048]{1,0:T(8,128)(2,1)S(1)} %get-tuple-element.57), channel_id=1, source_target_pairs={{0,4},{2,6},{4,0},{6,2},{1,5},{3,7},{5,1},{7,3},{8,12},{10,14},{12... | collective-permute-start | bytes 786440 | tf_op jit(solution)/shard_map/ppermute | solution.py:31
  24.5 12.7 %collective-permute-start.7 = (bf16[64,2048]{1,0:T(8,128)(2,1)S(1)}, bf16[64,2048]{1,0:T(8,128)(2,1)}, u32[]{:S(2)}, u32[]{:S(2)}) collective-permute-start(bf16[64,2048]{1,0:T(8,128)(2,1)S(1)} %get-tuple-element.59), channel_id=1, source_target_pairs={{0,2},{2,4},{4,6},{6,0},{1,3},{3,5},{5,7},{7,1},{8,10},{10,12},{12... | collective-permute-start | bytes 786440 | tf_op jit(solution)/shard_map/ppermute | solution.py:31
  25.2 12.4 %collective-permute-start.8 = (bf16[64,2048]{1,0:T(8,128)(2,1)S(1)}, bf16[64,2048]{1,0:T(8,128)(2,1)}, u32[]{:S(2)}, u32[]{:S(2)}) collective-permute-start(bf16[64,2048]{1,0:T(8,128)(2,1)S(1)} %get-tuple-element.58), channel_id=1, source_target_pairs={{0,6},{2,0},{4,2},{6,4},{1,7},{3,1},{5,3},{7,5},{8,14},{10,8},{12,... | collective-permute-start | bytes 786440 | tf_op jit(solution)/shard_map/ppermute | solution.py:31
  39.7 9.5 %collective-permute-start.9 = (bf16[64,2176]{1,0:T(8,128)(2,1)S(1)}, bf16[64,2176]{1,0:T(8,128)(2,1)S(1)}, u32[]{:S(2)}, u32[]{:S(2)}) collective-permute-start(bf16[64,2176]{1,0:T(8,128)(2,1)S(1)} %concatenate.9.refs_0_), channel_id=1, source_target_pairs={{0,8},{8,16},{16,24},{24,32},{32,40},{40,48},{48,56},{56,0},{1,9},... | collective-permute-start | bytes 835592 | tf_op jit(solution)/shard_map/ppermute | solution.py:31
  39.8 9.4 %collective-permute-start.11 = (bf16[64,2176]{1,0:T(8,128)(2,1)S(1)}, bf16[64,2176]{1,0:T(8,128)(2,1)S(1)}, u32[]{:S(2)}, u32[]{:S(2)}) collective-permute-start(bf16[64,2176]{1,0:T(8,128)(2,1)S(1)} %concatenate.9.refs_0_), channel_id=1, source_target_pairs={{0,56},{8,0},{16,8},{24,16},{32,24},{40,32},{48,40},{56,48},{1,57}... | collective-permute-start | bytes 835592 | tf_op jit(solution)/shard_map/ppermute | solution.py:31
  49.2 8.5 %collective-permute-start.10 = (bf16[64,2176]{1,0:T(8,128)(2,1)S(1)}, bf16[64,2176]{1,0:T(8,128)(2,1)S(1)}, u32[]{:S(2)}, u32[]{:S(2)}) collective-permute-start(bf16[64,2176]{1,0:T(8,128)(2,1)S(1)} %collective-permute-done.9.refs_1_), channel_id=1, source_target_pairs={{0,8},{8,16},{16,24},{24,32},{32,40},{40,48},{48,56},{56,0},{1,9},... | collective-permute-start | bytes 835592 | tf_op jit(solution)/shard_map/ppermute | solution.py:31
  49.2 8.5 %collective-permute-start.12 = (bf16[64,2176]{1,0:T(8,128)(2,1)S(1)}, bf16[64,2176]{1,0:T(8,128)(2,1)S(1)}, u32[]{:S(2)}, u32[]{:S(2)}) collective-permute-start(bf16[64,2176]{1,0:T(8,128)(2,1)S(1)} %collective-permute-done.11.refs_4_.refs_0_), channel_id=1, source_target_pairs={{0,56},{8,0},{16,8},{24,16},{32,24},{40,32},{48,40},{56,48},{1,57}... | collective-permute-start | bytes 835592 | tf_op jit(solution)/shard_map/ppermute | solution.py:31
  61.5 27.7 %all-to-all-start = ((bf16[16,24,2048]{2,1,0:T(8,128)(2,1)}), bf16[16,24,2048]{2,1,0:T(8,128)(2,1)}, u32[]{:S(2)}, u32[]{:S(2)}) async-start(bf16[16,24,2048]{2,1,0:T(8,128)(2,1)} %bitcast.7), calls=%async_computation | async-start | bytes 3145728 | tf_op jit(solution)/shard_map/all_to_all | solution.py:351
  72.1 7.9 %collective-permute-start.13 = (bf16[64,2176]{1,0:T(8,128)(2,1)S(1)}, bf16[64,2176]{1,0:T(8,128)(2,1)S(1)}, u32[]{:S(2)}, u32[]{:S(2)}) collective-permute-start(bf16[64,2176]{1,0:T(8,128)(2,1)S(1)} %collective-permute-done.10.refs_2_), channel_id=1, source_target_pairs={{0,8},{8,16},{16,24},{24,32},{32,40},{40,48},{48,56},{56,0},{1,9},... | collective-permute-start | bytes 835592 | tf_op jit(solution)/shard_map/ppermute | solution.py:31
  76.2 10.0 %collective-permute-start.16 = (bf16[64,1152]{1,0:T(8,128)(2,1)S(1)}, bf16[64,1152]{1,0:T(8,128)(2,1)S(1)}, u32[]{:S(2)}, u32[]{:S(2)}) collective-permute-start(bf16[64,1152]{1,0:T(8,128)(2,1)S(1)} %slice.96), channel_id=1, source_target_pairs={{0,56},{8,0},{16,8},{24,16},{32,24},{40,32},{48,40},{56,48},{1,57}... | collective-permute-start | bytes 442376 | tf_op jit(solution)/shard_map/ppermute | solution.py:31
  89.2 18.6 %all-to-all-start.1 = ((bf16[16,16,2048]{2,1,0:T(8,128)(2,1)}), bf16[16,16,2048]{2,1,0:T(8,128)(2,1)S(1)}, u32[]{:S(2)}, u32[]{:S(2)}) async-start(bf16[16,16,2048]{2,1,0:T(8,128)(2,1)} %bitcast.9), calls=%async_computation.1 | async-start | bytes 2097152 | tf_op jit(solution)/shard_map/all_to_all | solution.py:351
  132.8 22.5 %all-to-all-start.3 = ((bf16[16,24,2048]{2,1,0:T(8,128)(2,1)}), bf16[16,24,2048]{2,1,0:T(8,128)(2,1)S(1)}, u32[]{:S(2)}, u32[]{:S(2)}) async-start(bf16[16,24,2048]{2,1,0:T(8,128)(2,1)} %bitcast.46), calls=%async_computation.3 | async-start | bytes 3145728 | tf_op jit(solution)/shard_map/all_to_all | solution.py:351
  142.6 17.8 %collective-permute-start.20 = (bf16[64,1024]{1,0:T(8,128)(2,1)S(1)}, bf16[64,1024]{1,0:T(8,128)(2,1)S(1)}, u32[]{:S(2)}, u32[]{:S(2)}) collective-permute-start(bf16[64,1024]{1,0:T(8,128)(2,1)S(1)} %slice.99), channel_id=1, source_target_pairs={{0,56},{8,0},{16,8},{24,16},{32,24},{40,32},{48,40},{56,48},{1,57}... | collective-permute-start | bytes 393224 | tf_op jit(solution)/shard_map/ppermute | solution.py:31
  144.8 11.0 %collective-permute-start.19 = (bf16[64,1024]{1,0:T(8,128)(2,1)S(1)}, bf16[64,1024]{1,0:T(8,128)(2,1)S(1)}, u32[]{:S(2)}, u32[]{:S(2)}) collective-permute-start(bf16[64,1024]{1,0:T(8,128)(2,1)S(1)} %slice.98), channel_id=1, source_target_pairs={{0,8},{8,16},{16,24},{24,32},{32,40},{40,48},{48,56},{56,0},{1,9},... | collective-permute-start | bytes 393224 | tf_op jit(solution)/shard_map/ppermute | solution.py:31
  145.7 14.8 %collective-permute-start.22 = (bf16[64,1024]{1,0:T(8,128)(2,1)S(1)}, bf16[64,1024]{1,0:T(8,128)(2,1)S(1)}, u32[]{:S(2)}, u32[]{:S(2)}) collective-permute-start(bf16[64,1024]{1,0:T(8,128)(2,1)S(1)} %add_convert_fusion.3), channel_id=1, source_target_pairs={{0,56},{8,0},{16,8},{24,16},{32,24},{40,32},{48,40},{56,48},{1,57}... | collective-permute-start | bytes 393224 | tf_op jit(solution)/shard_map/ppermute | solution.py:31
  152.1 7.7 %collective-permute-start.18 = (bf16[64,1024]{1,0:T(8,128)(2,1)S(1)}, bf16[64,1024]{1,0:T(8,128)(2,1)S(1)}, u32[]{:S(2)}, u32[]{:S(2)}) collective-permute-start(bf16[64,1024]{1,0:T(8,128)(2,1)S(1)} %add_convert_fusion.4), channel_id=1, source_target_pairs={{0,8},{8,16},{16,24},{24,32},{32,40},{40,48},{48,56},{56,0},{1,9},... | collective-permute-start | bytes 393224 | tf_op jit(solution)/shard_map/ppermute | solution.py:31
  159.8 8.9 %collective-permute-start.23 = (bf16[64,2048]{1,0:T(8,128)(2,1)S(1)}, bf16[64,2048]{1,0:T(8,128)(2,1)S(1)}, u32[]{:S(2)}, u32[]{:S(2)}) collective-permute-start(bf16[64,2048]{1,0:T(8,128)(2,1)S(1)} %fusion.5), channel_id=1, source_target_pairs={{0,8},{8,16},{16,24},{24,32},{32,40},{40,48},{48,56},{56,0},{1,9},... | collective-permute-start | bytes 786440 | tf_op jit(solution)/shard_map/ppermute | solution.py:31
  160.5 9.1 %collective-permute-start.25 = (bf16[64,2048]{1,0:T(8,128)(2,1)S(1)}, bf16[64,2048]{1,0:T(8,128)(2,1)S(1)}, u32[]{:S(2)}, u32[]{:S(2)}) collective-permute-start(bf16[64,2048]{1,0:T(8,128)(2,1)S(1)} %add_convert_fusion.2), channel_id=1, source_target_pairs={{0,56},{8,0},{16,8},{24,16},{32,24},{40,32},{48,40},{56,48},{1,57}... | collective-permute-start | bytes 786440 | tf_op jit(solution)/shard_map/ppermute | solution.py:31
  172.2 7.6 %collective-permute-start.24 = (bf16[64,2048]{1,0:T(8,128)(2,1)S(1)}, bf16[64,2048]{1,0:T(8,128)(2,1)S(1)}, u32[]{:S(2)}, u32[]{:S(2)}) collective-permute-start(bf16[64,2048]{1,0:T(8,128)(2,1)S(1)} %add_convert_fusion.1), channel_id=1, source_target_pairs={{0,8},{8,16},{16,24},{24,32},{32,40},{40,48},{48,56},{56,0},{1,9},... | collective-permute-start | bytes 786440 | tf_op jit(solution)/shard_map/ppermute | solution.py:31
  (16 other events, 109.8 us)
